TPU v7x, 32 devices: a whole 2x2x4 slice. The times are simulated.
32 devices in a mesh: prompt: 4 (over z), slot: 8 (over y, x, core).
Axes of the slice: x: 2, y: 2, z: 4, core: 2. Of those that a mesh axis runs over, the one named last changes fastest.
Arguments:
- patch_kv: bfloat16 [4, 64, 128, 2048], P('prompt', 'slot'), may hold values from -6 to 6
- routes: int32 [4, 64], P('prompt', 'slot'), may hold values from -1 to 7, as said below
- prefix_kv: bfloat16 [4, 512, 2048], P('prompt', None, 'slot'), may hold values from -4 to 4
- prefix_len: int32 [4], P('prompt'), may hold values from 1 to 512, 1536 in all
- queries: bfloat16 [4, 8, 256, 8192], P('prompt', 'slot'), may hold values from -160 to 160
- suffix_kv: bfloat16 [4, 8, 256, 2048], P('prompt', 'slot'), may hold values from -6 to 6
- score_head: float32 [8192], replicated, may hold values from -0.0625 to 0.0625
Outputs:
- context: bfloat16 [4, 8, 256, 8192], P('prompt', 'slot')
- advantage: float32 [4, 8], P('prompt', 'slot')
Inputs may be any that keep to these rules, and one draw needn't show every extreme that they name: `routes`: in the list of one generating device each judge index appears at most once, and in one prompt's lists each judge index appears exactly 4 times; -1 marks an empty slot.
All inputs are finite; a program needn't handle non-finite values. No bound on the sum of `prefix_len` on one device may be relied on, other than what follows from the above.
Results may differ from a plain program's by a relative error of at most 0.005.
Values may be sent and summed in bfloat16 or wider, within the bound.
No kernel may reach another device: no remote copies, remote signals or barrier semaphores. Data moves between devices by JAX's collectives and lax.ppermute only.
A program may use at most 128 MiB of HBM per device.

v0:
```python
import math

import jax
import jax.numpy as jnp
from jax import lax
from jax.sharding import PartitionSpec as P

HEADS = 64
KVH = 8
HD = 128


def per_device(patch_kv, routes, prefix_kv, prefix_len, queries, suffix_kv, score_head):
    slot_count = lax.axis_size("slot")
    prompt_count = lax.axis_size("prompt")
    tile_rows = patch_kv.shape[2]
    width_kv = patch_kv.shape[3]
    suffix_rows = queries.shape[2]
    prefix_rows = prefix_kv.shape[1]
    groups = HEADS // KVH
    factor = 1.0 / math.sqrt(HD)
    judges = jnp.arange(slot_count, dtype=jnp.int32)
    matches = routes[0][None, :] == judges[:, None]
    outgoing = jnp.einsum(
        "dk,krc->drc", matches.astype(jnp.bfloat16), patch_kv[0], preferred_element_type=jnp.float32
    ).astype(jnp.bfloat16)
    carried = jnp.any(matches, axis=1).astype(jnp.bfloat16)
    incoming, arrived = (
        lax.all_to_all(outgoing, "slot", split_axis=0, concat_axis=0, tiled=True),
        lax.all_to_all(carried, "slot", split_axis=0, concat_axis=0, tiled=True),
    )
    live = arrived > 0
    tiles_kept = slot_count // 2
    kept_index = jnp.nonzero(live, size=tiles_kept)[0].astype(jnp.int32)
    image_rows = incoming[kept_index].reshape(tiles_kept * tile_rows, width_kv)
    prefix_whole = lax.all_gather(prefix_kv[0], "slot", axis=1, tiled=True)
    rows_all = jnp.concatenate([prefix_whole, image_rows, suffix_kv[0, 0]], axis=0)
    image_count = image_rows.shape[0]
    columns = jnp.arange(prefix_rows + image_count + suffix_rows, dtype=jnp.int32)[None, :]
    positions = jnp.arange(suffix_rows, dtype=jnp.int32)[:, None]
    allowed = jnp.where(
        columns < prefix_rows,
        columns < prefix_len[0],
        jnp.where(
            columns < prefix_rows + image_count,
            True,
            columns - prefix_rows - image_count <= positions,
        ),
    )
    grouped_queries = jnp.transpose(
        queries[0, 0].reshape(suffix_rows, KVH, groups, HD), (1, 2, 0, 3)
    )

    def one_group(group):
        query_rows = lax.dynamic_index_in_dim(grouped_queries, group, 0, keepdims=False)
        key_rows = lax.dynamic_slice_in_dim(rows_all, group * HD, HD, 1)
        value_rows = lax.dynamic_slice_in_dim(rows_all, (KVH + group) * HD, HD, 1)
        scores = (
            jnp.einsum("gsd,kd->gsk", query_rows, key_rows, preferred_element_type=jnp.float32)
            * factor
        )
        scores = jnp.where(allowed[None, :, :], scores, -1e30)
        peak = jnp.max(scores, axis=-1, keepdims=True)
        weights = jnp.exp(scores - peak)
        totals = jnp.sum(weights, axis=-1, keepdims=True)
        rounded = weights.astype(jnp.bfloat16)
        mixed = jnp.einsum("gsk,kd->gsd", rounded, value_rows, preferred_element_type=jnp.float32)
        return mixed / totals

    blocks = lax.map(one_group, jnp.arange(KVH, dtype=jnp.int32))
    context = (
        jnp.transpose(blocks, (2, 0, 1, 3)).reshape(suffix_rows, HEADS * HD).astype(jnp.bfloat16)
    )
    score = jnp.dot(
        context[suffix_rows - 1].astype(jnp.float32),
        score_head,
        precision=lax.Precision.HIGHEST,
        preferred_element_type=jnp.float32,
    )
    centre = lax.psum(score, "slot") / slot_count
    deviation = score - centre
    spread = lax.psum(deviation * deviation, ("prompt", "slot")) / (prompt_count * slot_count)
    advantage = deviation / jnp.sqrt(spread + 1e-06)
    return (context[None, None], advantage.reshape(1, 1))


def solution(mesh):
    placed = (
        P("prompt", "slot", None, None),
        P("prompt", "slot"),
        P("prompt", None, "slot"),
        P("prompt"),
        P("prompt", "slot", None, None),
        P("prompt", "slot", None, None),
        P(),
    )
    return jax.shard_map(
        per_device,
        mesh=mesh,
        in_specs=placed,
        out_specs=(P("prompt", "slot", None, None), P("prompt", "slot")),
        check_vma=False,
    )
```

profile of v0, /device:TPU:0, one launch (start us, length us, event | category | flops | bytes accessed | tf_op | source)
XLA Modules:
  0.0 337.2 jit_solution(14619025608659021119)
XLA Ops:
  8.6 5.2 %all-to-all-start.1 = ((bf16[8,1,1]{2,1,0:T(2,128)(2,1)}), bf16[8,1,1]{2,1,0:T(2,128)(2,1)S(1)}, u32[]{:S(2)}, u32[]{:S(2)}) async-start(bf16[8,1,1]{2,1,0:T(2,128)(2,1)} %copy.25), calls=%async_computation.1 | async-start | bytes 8192 | tf_op jit(solution)/shard_map/all_to_all | solution.py:30
  13.8 5.1 %fusion.25 = bf16[8,128,2048]{2,0,1:T(8,128)(2,1)S(1)} fusion(bf16[8,128,2048]{2,1,0:T(8,128)(2,1)} %bitcast.60, s32[8]{0:T(128)} %bitcast.64), kind=kOutput, calls=%fused_computation.30 | convolution fusion | flops 35651648 | bytes 8388640 | tf_op jit(solution)/shard_map/dk,krc->drc/dot_general | solution.py:24
  18.9 4.3 %copy.24 = bf16[8,128,2048]{2,1,0:T(8,128)(2,1)} copy(bf16[8,128,2048]{2,0,1:T(8,128)(2,1)S(1)} %fusion.25) | data formatting | bytes 8388608 | tf_op jit(solution)/shard_map/convert_element_type | solution.py:26
  23.2 4.5 %all-to-all-start = ((bf16[8,128,2048]{2,1,0:T(8,128)(2,1)}), bf16[8,128,2048]{2,1,0:T(8,128)(2,1)}, u32[]{:S(2)}, u32[]{:S(2)}) async-start(bf16[8,128,2048]{2,1,0:T(8,128)(2,1)} %copy.24), calls=%async_computation | async-start | bytes 8388608 | tf_op jit(solution)/shard_map/all_to_all | solution.py:29
  29.1 6.5 %copy.22 = bf16[1,1,256,8192]{2,3,1,0:T(8,128)(2,1)} copy(bf16[1,1,256,8192]{3,2,1,0:T(8,128)(2,1)} %param.13) | data formatting | bytes 8388608 | tf_op args[4]
  38.3 46.9 %all-to-all-done = bf16[8,128,2048]{2,1,0:T(8,128)(2,1)} async-done(((bf16[8,128,2048]{2,1,0:T(8,128)(2,1)}), bf16[8,128,2048]{2,1,0:T(8,128)(2,1)}, u32[]{:S(2)}, u32[]{:S(2)}) %all-to-all-start) | async-done | bytes 4194336 | tf_op jit(solution)/shard_map/all_to_all | solution.py:29
  88.2 4.6 %pad_maximum_fusion = bf16[1280,2048]{1,0:T(8,128)(2,1)} fusion(bf16[256,2048]{1,0:T(8,128)(2,1)S(1)} %bitcast.62, bf16[512,2048]{1,0:T(8,128)(2,1)S(1)} %bitcast.59, bf16[512,2048]{1,0:T(8,128)(2,1)} %bitcast.61), kind=kLoop, calls=%fused_computation.26 | loop fusion | flops 15728640 | bytes 10485760 | tf_op jit(solution)/shard_map/concatenate | solution.py:37
  92.8 173.9 %while.11 = (s32[]{:T(128)}, bf16[8,8,256,128]{3,1,0,2:T(8,128)(2,1)}, s32[8]{0:T(128)S(1)}, bf16[8,8,256,128]{2,3,1,0:T(8,128)(2,1)}, bf16[1280,2048]{1,0:T(8,1...) while((s32[]{:T(128)}, ...), condition=%wide.region_8.9_spmd.clone, body=%wide.region_5.8_spmd.clone.sunk | while | flops 1372516352 | bytes 77514296 | solution.py:70
  99.9 4.0 %copy-done = f32[8,256,1280]{2,1,0:T(8,128)} copy-done((f32[8,256,1280]{2,1,0:T(8,128)}, f32[8,256,1280]{2,1,0:T(8,128)S(1)}, u32[]{:S(2)}) %copy-start) | copy-done | bytes 10485784 | tf_op jit(solution)/shard_map/while
  106.7 6.6 %divide_bitcast_fusion.2 = bf16[1,8,256,128]{3,2,1,0:T(8,128)(2,1)S(1)} fusion(f32[8,256,1280]{2,1,0:T(8,128)} %copy-done, f32[8,256]{1,0:T(8,128)S(1)} %get-tuple-element.168, pred[256,1280]{1,0:T(8,128)(4,1)S(1)} %fusion.47, f32[8,256]{1,0:T(8,128)S(1)} %fusion.49, bf16[1280,2048]{1,0:T(8,128)(2,1)} %get-tuple-element.201, s32[]{:T(128)S(6)} %select_n.139), kind=kOutput, calls=%fused_computation.14.clone.1 | convolution fusion | flops 682098688 | bytes 11681796 | tf_op jit(solution)/shard_map/while/body/eval_jaxpr/gsk,kd->gsd/dot_general | solution.py:67
  121.7 4.0 %copy-done = f32[8,256,1280]{2,1,0:T(8,128)} copy-done((f32[8,256,1280]{2,1,0:T(8,128)}, f32[8,256,1280]{2,1,0:T(8,128)S(1)}, u32[]{:S(2)}) %copy-start) | copy-done | bytes 10485784 | tf_op jit(solution)/shard_map/while
  128.4 6.6 %divide_bitcast_fusion.2 = bf16[1,8,256,128]{3,2,1,0:T(8,128)(2,1)S(1)} fusion(f32[8,256,1280]{2,1,0:T(8,128)} %copy-done, f32[8,256]{1,0:T(8,128)S(1)} %get-tuple-element.168, pred[256,1280]{1,0:T(8,128)(4,1)S(1)} %fusion.47, f32[8,256]{1,0:T(8,128)S(1)} %fusion.49, bf16[1280,2048]{1,0:T(8,128)(2,1)} %get-tuple-element.201, s32[]{:T(128)S(6)} %select_n.139), kind=kOutput, calls=%fused_computation.14.clone.1 | convolution fusion | flops 682098688 | bytes 11681796 | tf_op jit(solution)/shard_map/while/body/eval_jaxpr/gsk,kd->gsd/dot_general | solution.py:67
  143.4 4.0 %copy-done = f32[8,256,1280]{2,1,0:T(8,128)} copy-done((f32[8,256,1280]{2,1,0:T(8,128)}, f32[8,256,1280]{2,1,0:T(8,128)S(1)}, u32[]{:S(2)}) %copy-start) | copy-done | bytes 10485784 | tf_op jit(solution)/shard_map/while
  150.1 6.6 %divide_bitcast_fusion.2 = bf16[1,8,256,128]{3,2,1,0:T(8,128)(2,1)S(1)} fusion(f32[8,256,1280]{2,1,0:T(8,128)} %copy-done, f32[8,256]{1,0:T(8,128)S(1)} %get-tuple-element.168, pred[256,1280]{1,0:T(8,128)(4,1)S(1)} %fusion.47, f32[8,256]{1,0:T(8,128)S(1)} %fusion.49, bf16[1280,2048]{1,0:T(8,128)(2,1)} %get-tuple-element.201, s32[]{:T(128)S(6)} %select_n.139), kind=kOutput, calls=%fused_computation.14.clone.1 | convolution fusion | flops 682098688 | bytes 11681796 | tf_op jit(solution)/shard_map/while/body/eval_jaxpr/gsk,kd->gsd/dot_general | solution.py:67
  171.9 6.6 %divide_bitcast_fusion.2 = bf16[1,8,256,128]{3,2,1,0:T(8,128)(2,1)S(1)} fusion(f32[8,256,1280]{2,1,0:T(8,128)} %copy-done, f32[8,256]{1,0:T(8,128)S(1)} %get-tuple-element.168, pred[256,1280]{1,0:T(8,128)(4,1)S(1)} %fusion.47, f32[8,256]{1,0:T(8,128)S(1)} %fusion.49, bf16[1280,2048]{1,0:T(8,128)(2,1)} %get-tuple-element.201, s32[]{:T(128)S(6)} %select_n.139), kind=kOutput, calls=%fused_computation.14.clone.1 | convolution fusion | flops 682098688 | bytes 11681796 | tf_op jit(solution)/shard_map/while/body/eval_jaxpr/gsk,kd->gsd/dot_general | solution.py:67
  186.8 4.0 %copy-done = f32[8,256,1280]{2,1,0:T(8,128)} copy-done((f32[8,256,1280]{2,1,0:T(8,128)}, f32[8,256,1280]{2,1,0:T(8,128)S(1)}, u32[]{:S(2)}) %copy-start) | copy-done | bytes 10485784 | tf_op jit(solution)/shard_map/while
  193.6 6.6 %divide_bitcast_fusion.2 = bf16[1,8,256,128]{3,2,1,0:T(8,128)(2,1)S(1)} fusion(f32[8,256,1280]{2,1,0:T(8,128)} %copy-done, f32[8,256]{1,0:T(8,128)S(1)} %get-tuple-element.168, pred[256,1280]{1,0:T(8,128)(4,1)S(1)} %fusion.47, f32[8,256]{1,0:T(8,128)S(1)} %fusion.49, bf16[1280,2048]{1,0:T(8,128)(2,1)} %get-tuple-element.201, s32[]{:T(128)S(6)} %select_n.139), kind=kOutput, calls=%fused_computation.14.clone.1 | convolution fusion | flops 682098688 | bytes 11681796 | tf_op jit(solution)/shard_map/while/body/eval_jaxpr/gsk,kd->gsd/dot_general | solution.py:67
  208.5 4.0 %copy-done = f32[8,256,1280]{2,1,0:T(8,128)} copy-done((f32[8,256,1280]{2,1,0:T(8,128)}, f32[8,256,1280]{2,1,0:T(8,128)S(1)}, u32[]{:S(2)}) %copy-start) | copy-done | bytes 10485784 | tf_op jit(solution)/shard_map/while
  215.3 6.7 %divide_bitcast_fusion.2 = bf16[1,8,256,128]{3,2,1,0:T(8,128)(2,1)S(1)} fusion(f32[8,256,1280]{2,1,0:T(8,128)} %copy-done, f32[8,256]{1,0:T(8,128)S(1)} %get-tuple-element.168, pred[256,1280]{1,0:T(8,128)(4,1)S(1)} %fusion.47, f32[8,256]{1,0:T(8,128)S(1)} %fusion.49, bf16[1280,2048]{1,0:T(8,128)(2,1)} %get-tuple-element.201, s32[]{:T(128)S(6)} %select_n.139), kind=kOutput, calls=%fused_computation.14.clone.1 | convolution fusion | flops 682098688 | bytes 11681796 | tf_op jit(solution)/shard_map/while/body/eval_jaxpr/gsk,kd->gsd/dot_general | solution.py:67
  237.1 6.6 %divide_bitcast_fusion.2 = bf16[1,8,256,128]{3,2,1,0:T(8,128)(2,1)S(1)} fusion(f32[8,256,1280]{2,1,0:T(8,128)} %copy-done, f32[8,256]{1,0:T(8,128)S(1)} %get-tuple-element.168, pred[256,1280]{1,0:T(8,128)(4,1)S(1)} %fusion.47, f32[8,256]{1,0:T(8,128)S(1)} %fusion.49, bf16[1280,2048]{1,0:T(8,128)(2,1)} %get-tuple-element.201, s32[]{:T(128)S(6)} %select_n.139), kind=kOutput, calls=%fused_computation.14.clone.1 | convolution fusion | flops 682098688 | bytes 11681796 | tf_op jit(solution)/shard_map/while/body/eval_jaxpr/gsk,kd->gsd/dot_general | solution.py:67
  258.8 6.6 %divide_bitcast_fusion.2 = bf16[1,8,256,128]{3,2,1,0:T(8,128)(2,1)S(1)} fusion(f32[8,256,1280]{2,1,0:T(8,128)} %copy-done, f32[8,256]{1,0:T(8,128)S(1)} %get-tuple-element.168, pred[256,1280]{1,0:T(8,128)(4,1)S(1)} %fusion.47, f32[8,256]{1,0:T(8,128)S(1)} %fusion.49, bf16[1280,2048]{1,0:T(8,128)(2,1)} %get-tuple-element.201, s32[]{:T(128)S(6)} %select_n.139), kind=kOutput, calls=%fused_computation.14.clone.1 | convolution fusion | flops 682098688 | bytes 11681796 | tf_op jit(solution)/shard_map/while/body/eval_jaxpr/gsk,kd->gsd/dot_general | solution.py:67
  268.0 12.4 %psum.14 = f32[]{:T(128)} all-reduce(f32[]{:T(128)} %fusion.28), channel_id=1, replica_groups=mesh['prompt'=4,'slot'=8] {'slot'}, use_global_device_ids=true, to_apply=%region_9.10 | all-reduce | flops 1 | bytes 8 | tf_op jit(solution)/shard_map/psum | solution.py:80
  281.7 7.3 %convert_element_type.65 = bf16[1,1,256,8192]{3,2,1,0:T(8,128)(2,1)} reshape(bf16[256,8,8,128]{3,2,1,0:T(8,128)(2,1)} %bitcast.42) | data formatting | bytes 8388608 | tf_op jit(solution)/shard_map/convert_element_type | solution.py:72
  289.0 39.5 %psum.15 = f32[]{:T(128)} all-reduce(f32[]{:T(128)S(6)} %mul.12), channel_id=1, replica_groups=mesh['prompt'=4,'slot'=8] {'prompt','slot'}, use_global_device_ids=true, to_apply=%region_10.11 | all-reduce | flops 1 | bytes 8 | tf_op jit(solution)/shard_map/psum | solution.py:82
  (77 shorter events, 87.5 us)
Async XLA Ops:
  8.6 14.5 %all-to-all-start.1 = ((bf16[8,1,1]{2,1,0:T(2,128)(2,1)}), bf16[8,1,1]{2,1,0:T(2,128)(2,1)S(1)}, u32[]{:S(2)}, u32[]{:S(2)}) async-start(bf16[8,1,1]{2,1,0:T(2,128)(2,1)} %copy.25), calls=%async_computation.1 | async-start | bytes 8192 | tf_op jit(solution)/shard_map/all_to_all | solution.py:30
  23.2 62.1 %all-to-all-start = ((bf16[8,128,2048]{2,1,0:T(8,128)(2,1)}), bf16[8,128,2048]{2,1,0:T(8,128)(2,1)}, u32[]{:S(2)}, u32[]{:S(2)}) async-start(bf16[8,128,2048]{2,1,0:T(8,128)(2,1)} %copy.24), calls=%async_computation | async-start | bytes 8388608 | tf_op jit(solution)/shard_map/all_to_all | solution.py:29
  27.7 60.4 %all-gather.3.cloned.1.call-start = ((), (), s32[]{:S(2)}) async-start(), calls=%async_computation.2 | async-start | bytes 2359296 | tf_op jit(solution)/shard_map/all_gather | solution.py:36
  29.1 59.0 %copy-start.1 = (bf16[1,1,256,2048]{3,2,1,0:T(8,128)(2,1)S(1)}, bf16[1,1,256,2048]{3,2,1,0:T(8,128)(2,1)}, u32[]{:S(2)}) copy-start(bf16[1,1,256,2048]{3,2,1,0:T(8,128)(2,1)} %param.14) | copy-start | bytes 3145732
  92.8 173.9 %copy-start.2 = (f32[8192]{0:T(1024)S(1)}, f32[8192]{0:T(1024)}, u32[]{:S(2)}) copy-start(f32[8192]{0:T(1024)} %param.15) | copy-start | bytes 98308
  99.9 4.0 %copy-start = (f32[8,256,1280]{2,1,0:T(8,128)}, f32[8,256,1280]{2,1,0:T(8,128)S(1)}, u32[]{:S(2)}) copy-start(f32[8,256,1280]{2,1,0:T(8,128)S(1)} %get-tuple-element.167) | copy-start | bytes 31457284 | tf_op jit(solution)/shard_map/while
  121.6 4.0 %copy-start = (f32[8,256,1280]{2,1,0:T(8,128)}, f32[8,256,1280]{2,1,0:T(8,128)S(1)}, u32[]{:S(2)}) copy-start(f32[8,256,1280]{2,1,0:T(8,128)S(1)} %get-tuple-element.167) | copy-start | bytes 31457284 | tf_op jit(solution)/shard_map/while
  143.3 4.0 %copy-start = (f32[8,256,1280]{2,1,0:T(8,128)}, f32[8,256,1280]{2,1,0:T(8,128)S(1)}, u32[]{:S(2)}) copy-start(f32[8,256,1280]{2,1,0:T(8,128)S(1)} %get-tuple-element.167) | copy-start | bytes 31457284 | tf_op jit(solution)/shard_map/while
  165.1 4.0 %copy-start = (f32[8,256,1280]{2,1,0:T(8,128)}, f32[8,256,1280]{2,1,0:T(8,128)S(1)}, u32[]{:S(2)}) copy-start(f32[8,256,1280]{2,1,0:T(8,128)S(1)} %get-tuple-element.167) | copy-start | bytes 31457284 | tf_op jit(solution)/shard_map/while
  186.8 4.0 %copy-start = (f32[8,256,1280]{2,1,0:T(8,128)}, f32[8,256,1280]{2,1,0:T(8,128)S(1)}, u32[]{:S(2)}) copy-start(f32[8,256,1280]{2,1,0:T(8,128)S(1)} %get-tuple-element.167) | copy-start | bytes 31457284 | tf_op jit(solution)/shard_map/while
  208.5 4.0 %copy-start = (f32[8,256,1280]{2,1,0:T(8,128)}, f32[8,256,1280]{2,1,0:T(8,128)S(1)}, u32[]{:S(2)}) copy-start(f32[8,256,1280]{2,1,0:T(8,128)S(1)} %get-tuple-element.167) | copy-start | bytes 31457284 | tf_op jit(solution)/shard_map/while
  230.3 4.0 %copy-start = (f32[8,256,1280]{2,1,0:T(8,128)}, f32[8,256,1280]{2,1,0:T(8,128)S(1)}, u32[]{:S(2)}) copy-start(f32[8,256,1280]{2,1,0:T(8,128)S(1)} %get-tuple-element.167) | copy-start | bytes 31457284 | tf_op jit(solution)/shard_map/while
  252.0 4.0 %copy-start = (f32[8,256,1280]{2,1,0:T(8,128)}, f32[8,256,1280]{2,1,0:T(8,128)S(1)}, u32[]{:S(2)}) copy-start(f32[8,256,1280]{2,1,0:T(8,128)S(1)} %get-tuple-element.167) | copy-start | bytes 31457284 | tf_op jit(solution)/shard_map/while
Sparse Core Ops, SparseCore 0:
  30.4 48.5 all-gather.2
where the time goes:
time: 338 us; the launch traced here: 337 us
  matrix products  85.3 us (25%)
  local copies, waits for them, and re-layouts  68.3 us (20%)
  blocking collectives  51.9 us (15%)
  waiting for transfers between devices  47.6 us (14%)
  other arithmetic  33.8 us (10%)
  loops' own time  22.4 us (7%)
  between operations  17.9 us (5%)
  starting transfers between devices  9.76 us (3%)
    dot_general x8, matrix products, one_group(): jnp.einsum('gsk,kd->gsd', rounded, value_rows, preferred_element_type=jnp...  53.2 us
    all_to_all x1, waiting for transfers between devices, per_device(): lax.all_to_all(outgoing, 'slot', split_axis=0, concat_axis=0, tiled=True)  46.9 us
    psum x1, blocking collectives, per_device(): lax.psum(deviation * deviation, ('prompt', 'slot'))  39.5 us
    while x16, local copies, waits for them, and re-layouts  31.9 us
    dot_general x8, matrix products, one_group(): jnp.einsum('gsd,kd->gsk', query_rows, key_rows, preferred_element_type=jn...  27.1 us
    another operation x1, loops' own time, per_device(): blocks = lax.map(one_group, jnp.arange(KVH, dtype=jnp.int32))  22.4 us
    reduce_sum x8, other arithmetic, one_group(): totals = jnp.sum(weights, axis=-1, keepdims=True)  22.2 us
    psum x1, blocking collectives, per_device(): centre = lax.psum(score, 'slot') / slot_count  12.4 us
  transfers between devices with their start and end apart: 3, of which 1 were waited for; matrix products, arithmetic and copies ran while one was open for 6% of the time, Pallas kernels for 0%

commit v1 on v0

v1 whole, which is shorter than its diff:
```python
import functools
import math

import jax
import jax.numpy as jnp
from jax import lax
from jax.experimental import pallas as pl
from jax.experimental.pallas import tpu as pltpu
from jax.sharding import PartitionSpec as P

HEADS = 64
KVH = 8
HD = 128
GROUPS = HEADS // KVH
SCALE = math.log2(math.e) / math.sqrt(HD)
LOW = -1e30
EXTRA = 16
NT = (((1,), (1,)), ((), ()))
VMEM_LIMIT = 56 * 2**20


def pack_kernel(head_from, heads, chips, routes_ref, patch_ref, *rest):
    outs, sem = rest[:chips], rest[chips]
    slots = patch_ref.shape[0]
    me = lax.axis_index("slot")
    chip, core = me // 2, me % 2
    width = heads * HD
    copies = []
    for offset in range(chips):
        for other in range(2):
            judge = 2 * (chip ^ offset) + (core ^ other)
            tile = jnp.int32(0)
            for s in range(slots):
                tile = jnp.where(routes_ref[s] == judge, s, tile)
            for half in range(2):
                copies.append(
                    pltpu.make_async_copy(
                        patch_ref.at[tile, :, pl.ds((half * KVH + head_from) * HD, width)],
                        outs[offset].at[other, :, pl.ds(half * width, width)],
                        sem.at[len(copies)],
                    )
                )
    for copy in copies:
        copy.start()
    for copy in copies:
        copy.wait()


def pack(head_from, heads, chips, routes, patch):
    rows = patch.shape[1]
    shape = jax.ShapeDtypeStruct((2, rows, 2 * heads * HD), patch.dtype)
    return pl.pallas_call(
        functools.partial(pack_kernel, head_from, heads, chips),
        out_shape=[shape] * chips,
        in_specs=[pl.BlockSpec(memory_space=pltpu.SMEM), pl.BlockSpec(memory_space=pl.ANY)],
        out_specs=[pl.BlockSpec(memory_space=pl.ANY)] * chips,
        scratch_shapes=[pltpu.SemaphoreType.DMA((4 * chips,))],
        cost_estimate=pl.CostEstimate(
            flops=0, bytes_accessed=chips * 8 * rows * heads * HD * 2, transcendentals=0
        ),
        name="pack_tiles",
    )(routes, patch)


def prefix_kernel(chips, *rest):
    near, far, out, sem = rest[:chips], rest[chips], rest[chips + 1], rest[chips + 2]
    rows, columns = out.shape[0], near[0].shape[1]
    me = lax.axis_index("slot")
    chip, core = me // 2, me % 2
    copies = []
    for offset in range(chips):
        for other in range(2):
            owner = 2 * (chip ^ offset) + (core ^ other)
            source = near[offset] if other == 0 else far.at[offset]
            copies.append(
                pltpu.make_async_copy(
                    source.at[pl.ds(0, rows), :],
                    out.at[:, pl.ds(pl.multiple_of(owner * columns, 128), columns)],
                    sem.at[len(copies)],
                )
            )
    for copy in copies:
        copy.start()
    for copy in copies:
        copy.wait()


def join_prefix(chips, rows, near, far):
    width = 2 * chips * near[0].shape[1]
    return pl.pallas_call(
        functools.partial(prefix_kernel, chips),
        out_shape=jax.ShapeDtypeStruct((rows, width), near[0].dtype),
        in_specs=[pl.BlockSpec(memory_space=pl.ANY)] * (chips + 1),
        out_specs=pl.BlockSpec(memory_space=pl.ANY),
        scratch_shapes=[pltpu.SemaphoreType.DMA((2 * chips,))],
        cost_estimate=pl.CostEstimate(flops=0, bytes_accessed=rows * width * 4, transcendentals=0),
        name="join_prefix",
    )(*near, far)


def attention_kernel(chips, kept, aliased, meta_ref, head_ref, q_ref, pk_ref, pv_ref, sk_ref, sv_ref, *rest):
    tiles = rest[: 4 * chips]
    rest = rest[4 * chips + (1 if aliased else 0) :]
    o_ref, score_ref, kbuf, vbuf = rest
    slots = 2 * chips
    prefix_rows, suffix_rows = pk_ref.shape[0], sk_ref.shape[0]
    tile_rows = tiles[0].shape[1]
    start = prefix_rows + kept * tile_rows
    total = start + suffix_rows
    length = meta_ref[2 * slots]

    @pl.when(pl.program_id(0) == 0)
    def _():
        score_ref[...] = jnp.zeros_like(score_ref)

    live = lax.broadcasted_iota(jnp.int32, (prefix_rows, HD), 0) < length
    kbuf[:prefix_rows] = jnp.where(live, pk_ref[...], pk_ref[0:1, :])
    vbuf[:prefix_rows, :HD] = jnp.where(live, pv_ref[...], jnp.zeros_like(pv_ref[...]))
    vbuf[:prefix_rows, HD:] = live.astype(vbuf.dtype)
    vbuf[prefix_rows:, HD:] = jnp.ones((total - prefix_rows, HD), vbuf.dtype)
    kbuf[start:] = sk_ref[...]
    vbuf[start:, :HD] = sv_ref[...]
    for n in range(slots):
        @pl.when(meta_ref[n] > 0)
        def _(n=n):
            row = pl.multiple_of(prefix_rows + meta_ref[slots + n] * tile_rows, tile_rows)
            kbuf[pl.ds(row, tile_rows), :] = tiles[2 * n][0]
            vbuf[pl.ds(row, tile_rows), :HD] = tiles[2 * n + 1][0]

    causal = lax.broadcasted_iota(jnp.int32, (suffix_rows, suffix_rows), 1) <= lax.broadcasted_iota(
        jnp.int32, (suffix_rows, suffix_rows), 0
    )

    def scores(h):
        s = lax.dot_general(
            q_ref[:, h * HD : (h + 1) * HD], kbuf[...], NT, preferred_element_type=jnp.float32
        )
        return jnp.concatenate([s[:, :start], jnp.where(causal, s[:, start:], LOW)], axis=1)

    def finish(s, h):
        peak = jnp.max(s, axis=1, keepdims=True)
        weights = jnp.exp2((s - peak) * SCALE).astype(jnp.bfloat16)
        mixed = jnp.dot(weights, vbuf[...], preferred_element_type=jnp.float32)
        out = (mixed[:, :HD] / mixed[:, HD:]).astype(o_ref.dtype)
        o_ref[:, h * HD : (h + 1) * HD] = out
        last = out[suffix_rows - 8 :, :].astype(jnp.float32)
        score_ref[...] += last * head_ref[0:1, h * HD : (h + 1) * HD]

    held = scores(0)
    for h in range(1, GROUPS):
        following = scores(h)
        finish(held, h - 1)
        held = following
    finish(held, GROUPS - 1)


def attend(chips, kept, head_from, heads, meta, head, queries, prefix, suffix, near, far, context):
    rows = queries.shape[0]
    prefix_rows, suffix_rows = prefix.shape[0], suffix.shape[0]
    tile_rows = near[0].shape[1]
    total = prefix_rows + kept * tile_rows + suffix_rows
    wide = GROUPS * HD
    column = lambda shift: (lambda g: (0, head_from + shift + g))
    specs = [
        pl.BlockSpec(memory_space=pltpu.SMEM),
        pl.BlockSpec((1, wide), column(0)),
        pl.BlockSpec((rows, wide), column(0)),
        pl.BlockSpec((prefix_rows, HD), column(0)),
        pl.BlockSpec((prefix_rows, HD), column(KVH)),
        pl.BlockSpec((suffix_rows, HD), column(0)),
        pl.BlockSpec((suffix_rows, HD), column(KVH)),
    ]
    operands = [meta, head, queries, prefix, prefix, suffix, suffix]
    for offset in range(chips):
        for other in range(2):
            array, place = (near[offset], 0) if other == 0 else (far, offset)
            for half in range(2):
                specs.append(
                    pl.BlockSpec(
                        (1, tile_rows, HD), lambda g, p=place, s=half * heads: (p, 0, s + g)
                    )
                )
                operands.append(array)
    aliases = {}
    if context is not None:
        aliases = {len(operands): 0}
        specs.append(pl.BlockSpec(memory_space=pl.ANY))
        operands.append(context)
    return pl.pallas_call(
        functools.partial(attention_kernel, chips, kept, context is not None),
        grid=(heads,),
        out_shape=[
            jax.ShapeDtypeStruct(queries.shape, queries.dtype),
            jax.ShapeDtypeStruct((8, HD), jnp.float32),
        ],
        in_specs=specs,
        out_specs=[
            pl.BlockSpec((rows, wide), column(0)),
            pl.BlockSpec((8, HD), lambda g: (0, 0)),
        ],
        scratch_shapes=[
            pltpu.VMEM((total, HD), queries.dtype),
            pltpu.VMEM((total, 2 * HD), queries.dtype),
        ],
        input_output_aliases=aliases,
        compiler_params=pltpu.CompilerParams(vmem_limit_bytes=VMEM_LIMIT),
        cost_estimate=pl.CostEstimate(
            flops=heads * GROUPS * rows * total * HD * 8,
            bytes_accessed=heads * (rows * wide * 4 + total * HD * 4),
            transcendentals=heads * GROUPS * rows * total,
        ),
        name="attend",
    )(*operands)


def per_device(patch_kv, routes, prefix_kv, prefix_len, queries, suffix_kv, score_head):
    slot_count = lax.axis_size("slot")
    prompt_count = lax.axis_size("prompt")
    chips = slot_count // 2
    kept = slot_count // 2
    slots = routes.shape[1]
    prefix_rows, prefix_columns = prefix_kv.shape[1:]
    me = lax.axis_index("slot")
    chip, core = me // 2, me % 2

    def swap(x, k):
        return lax.ppermute(x, "slot", [(i, i ^ k) for i in range(slot_count)])

    listed = jnp.pad(routes.astype(jnp.bfloat16), ((0, EXTRA - 1), (0, prefix_columns - slots)))
    block = jnp.concatenate([prefix_kv[0], listed], axis=0)
    near = [block] + [swap(block, 2 * offset) for offset in range(1, chips)]
    far = swap(jnp.stack(near), 1)
    lists = [part for offset in range(chips) for part in (near[offset], far[offset])]
    lists = jnp.stack([part[prefix_rows, :slots] for part in lists]).astype(jnp.int32)
    present = jnp.any(lists == me, axis=1).astype(jnp.int32)
    meta = jnp.concatenate([present, jnp.cumsum(present) - present, prefix_len]).astype(jnp.int32)
    prefix = join_prefix(chips, prefix_rows, near, far)

    parts = ((0, 3), (3, 2), (5, 2), (7, 1))
    arrived = []
    for n, (head_from, heads) in enumerate(parts):
        buffers = pack(head_from, heads, chips, routes[0], patch_kv[0])
        if n >= 2:
            buffers = list(lax.optimization_barrier((tuple(buffers), arrived[n - 2][0]))[0])
        got = [buffers[0]] + [swap(buffers[offset], 2 * offset) for offset in range(1, chips)]
        passed = swap(jnp.stack([part[1] for part in got]), 1)
        arrived.append((got, passed))

    head = score_head.reshape(1, -1)
    context, shares = None, []
    for (head_from, heads), (got, passed) in zip(parts, arrived):
        context, share = attend(
            chips, kept, head_from, heads, meta, head, queries[0, 0], prefix, suffix_kv[0, 0],
            got, passed, context,
        )
        shares.append(share[7])
    score = jnp.sum(sum(shares)).reshape(1)

    pair = jnp.concatenate([score, swap(score, 1)])
    every = jnp.concatenate([pair] + [swap(pair, 2 * offset) for offset in range(1, chips)])
    centre = jnp.sum(every) / slot_count
    own = jnp.sum((every - centre) ** 2).reshape(1)
    squares = own
    for k in range(1, prompt_count):
        squares = squares + lax.ppermute(own, "prompt", [(i, i ^ k) for i in range(prompt_count)])
    spread = squares / (prompt_count * slot_count)
    advantage = (score - centre) / jnp.sqrt(spread + 1e-06)
    return (context[None, None], advantage.reshape(1, 1))


def solution(mesh):
    placed = (
        P("prompt", "slot", None, None),
        P("prompt", "slot"),
        P("prompt", None, "slot"),
        P("prompt"),
        P("prompt", "slot", None, None),
        P("prompt", "slot", None, None),
        P(),
    )
    return jax.shard_map(
        per_device,
        mesh=mesh,
        in_specs=placed,
        out_specs=(P("prompt", "slot", None, None), P("prompt", "slot")),
        check_vma=False,
    )
```

time: 338 us -> 308 us (0.911)
  Pallas kernels: 0 us -> 238 us
  matrix products: 85.3 us -> 0 us
  local copies, waits for them, and re-layouts: 68.3 us -> 8.54 us
  blocking collectives: 51.9 us -> 0 us
  waiting for transfers between devices: 47.6 us -> 11.4 us
  loops' own time: 22.4 us -> 0 us
  other arithmetic: 33.8 us -> 11.7 us
  starting transfers between devices: 9.76 us -> 27.8 us
  between operations: 17.9 us -> 9.29 us
    pallas_call x0 -> x9, Pallas kernels: none -> 238 us  [the longest x4 135 us: pack(): pl.pallas_call(functools.partial(pack_kernel, head_from, heads, chips), o...]
    dot_general x17 -> x0, matrix products: 85.3 us -> none  [the longest x8 53.2 us: one_group(): jnp.einsum('gsk,kd->gsd', rounded, value_rows, preferred_element_type=jnp...]
    psum x2 -> x0, blocking collectives: 51.9 us -> none  [the longest x1 39.5 us: per_device(): lax.psum(deviation * deviation, ('prompt', 'slot'))]
    all_to_all x2 -> x0, waiting for transfers between devices: 46.9 us -> none  [the longest x1 46.9 us: per_device(): lax.all_to_all(outgoing, 'slot', split_axis=0, concat_axis=0, tiled=True)]
    while x16 -> x0, local copies, waits for them, and re-layouts: 31.9 us -> none
    ppermute x0 -> x27, starting transfers between devices: none -> 27.8 us  [the longest x24 23.4 us: swap(): return lax.ppermute(x, 'slot', [(i, i ^ k) for i in range(slot_count)])]
    another operation x1 -> x0, loops' own time: 22.4 us -> none  [per_device(): blocks = lax.map(one_group, jnp.arange(KVH, dtype=jnp.int32))]
    reduce_sum x9 -> x5, other arithmetic: 23.1 us -> 3.76 us  [the longest x3 1.83 us: per_device(): centre = jnp.sum(every) / slot_count]
  transfers between devices with their start and end apart: 3 -> 27, of which waited for: 1 -> 5; matrix products, arithmetic and copies ran while one was open for 6% -> 3% of each run, Pallas kernels for 0% -> 76%
where the time goes in v1:
time: 308 us; the launch traced here: 307 us
  Pallas kernels  238 us (77%)
  starting transfers between devices  27.8 us (9%)
  other arithmetic  11.7 us (4%)
  waiting for transfers between devices  11.4 us (4%)
  between operations  9.29 us (3%)
  local copies, waits for them, and re-layouts  8.54 us (3%)
    pallas_call x4, Pallas kernels, pack(): pl.pallas_call(functools.partial(pack_kernel, head_from, heads, chips), o...  135 us
    pallas_call x1, Pallas kernels, join_prefix(): pl.pallas_call(functools.partial(prefix_kernel, chips), out_shape=jax.Sha...  64.7 us
    pallas_call x4, Pallas kernels, attend(): pl.pallas_call(functools.partial(attention_kernel, chips, kept, context i...  38.4 us
    ppermute x24, starting transfers between devices, swap(): return lax.ppermute(x, 'slot', [(i, i ^ k) for i in range(slot_count)])  23.4 us
    ppermute x24, waiting for transfers between devices, swap(): return lax.ppermute(x, 'slot', [(i, i ^ k) for i in range(slot_count)])  8.68 us
  transfers between devices with their start and end apart: 27, of which 5 were waited for; matrix products, arithmetic and copies ran while one was open for 3% of the time, Pallas kernels for 76%

profile of v1, /device:TPU:0, one launch (start us, length us, event | category | flops | bytes accessed | tf_op | source)
XLA Modules:
  0.0 307.0 jit_solution(2064490129129183301)
XLA Ops:
  2.3 3.0 collective-permute-start
  5.3 1.5 collective-permute-start.1
  6.8 33.7 %pack_tiles.5 = (bf16[2,128,512]{2,1,0:T(8,128)(2,1)}, bf16[2,128,512]{2,1,0:T(8,128)(2,1)}, bf16[2,128,512]{2,1,0:T(8,128)(2,1)}, bf16[2,128,512]{2,1,0:T(8,128)(2,1)}) custom-call(s32[8]{0:T(128)} %bitcast.54, bf16[8,128,2048]{2,1,0:T(8,128)(2,1)} %bitcast.29), custom_call_target="tpu_custom_call" | custom-call | bytes 2097152 | tf_op jit(solution)/shard_map/pack_tiles/pallas_call | solution.py:52
  40.5 2.0 collective-permute-start.4
  42.6 1.5 collective-permute-start.5
  45.3 49.7 %pack_tiles.7 = (bf16[2,128,768]{2,1,0:T(8,128)(2,1)}, bf16[2,128,768]{2,1,0:T(8,128)(2,1)}, bf16[2,128,768]{2,1,0:T(8,128)(2,1)}, bf16[2,128,768]{2,1,0:T(8,128)(2,1)}) custom-call(s32[8]{0:T(128)} %bitcast.55, bf16[8,128,2048]{2,1,0:T(8,128)(2,1)} %bitcast.30), custom_call_target="tpu_custom_call" | custom-call | bytes 3145728 | tf_op jit(solution)/shard_map/pack_tiles/pallas_call | solution.py:52
  95.7 2.9 collective-permute-start.13
  98.7 17.9 %pack_tiles.4 = (bf16[2,128,256]{2,1,0:T(8,128)(2,1)}, bf16[2,128,256]{2,1,0:T(8,128)(2,1)}, bf16[2,128,256]{2,1,0:T(8,128)(2,1)}, bf16[2,128,256]{2,1,0:T(8,128)(2,1)}) custom-call(s32[8]{0:T(128)} %bitcast.56, bf16[8,128,2048]{2,1,0:T(8,128)(2,1)} %bitcast.31), custom_call_target="tpu_custom_call" | custom-call | bytes 1048576 | tf_op jit(solution)/shard_map/pack_tiles/pallas_call | solution.py:52
  116.7 4.1 %collective-permute-done.6.rest_12_.rest_13_ = bf16[2,128,512]{2,1,0:T(8,128)(2,1)S(1)} collective-permute-done((bf16[2,128,512]{2,1,0:T(8,128)(2,1)S(1)}, bf16[2,128,512]{2,1,0:T(8,128)(2,1)S(1)}, u32[]{:S(2)}, u32[]{:S(2)}) %collective-permute-start.6) | collective-permute-done | bytes 262176 | tf_op jit(solution)/shard_map/ppermute | solution.py:227
  121.1 1.8 collective-permute-start.8
  124.3 33.8 %pack_tiles.6 = (bf16[2,128,512]{2,1,0:T(8,128)(2,1)}, bf16[2,128,512]{2,1,0:T(8,128)(2,1)}, bf16[2,128,512]{2,1,0:T(8,128)(2,1)}, bf16[2,128,512]{2,1,0:T(8,128)(2,1)}) custom-call(s32[8]{0:T(128)} %bitcast.57, bf16[8,128,2048]{2,1,0:T(8,128)(2,1)} %bitcast.32), custom_call_target="tpu_custom_call" | custom-call | bytes 2097152 | tf_op jit(solution)/shard_map/pack_tiles/pallas_call | solution.py:52
  159.4 1.8 collective-permute-start.15
  161.3 1.5 collective-permute-start.16
  169.1 1.9 collective-permute-done.15.rest_8_.rest_9_
  171.0 1.5 collective-permute-done.16.rest_12_.rest_13_
  174.8 64.7 %join_prefix.1.pk_ref.pv_ref = bf16[512,2048]{1,0:T(8,128)(2,1)} custom-call(bf16[528,256]{1,0:T(8,128)(2,1)} %copy-done.15, bf16[528,256]{1,0:T(8,128)(2,1)} %copy-done.12, bf16[528,256]{1,0:T(8,128)(2,1)} %copy-done.13, bf16[528,256]{1,0:T(8,128)(2,1)} %copy-done.14, bf16[4,528,256]{2,1,0:T(8,128)(2,1)} %copy-done.3), custom_call_target="tpu_custom_call" | custom-call | bytes 4194304 | tf_op jit(solution)/shard_map/join_prefix/pallas_call | solution.py:90
  240.1 13.5 %attend.4 = (bf16[256,8192]{1,0:T(8,128)(2,1)}, f32[8,128]{1,0:T(8,128)}) custom-call(s32[17]{0:T(128)} %pad_add_fusion.meta_ref, f32[1,8192]{1,0:T(1,128)} %bitcast.49, bf16[256,8192]{1,0:T(8,128)(2,1)} %bitcast.41, bf16[512,2048]{1,0:T(8,128)(2,1)} %join_prefix.1.pk_ref.pv_ref, bf16[512,2048]{1,0:T(8,128)(2,1)} %join_prefix.1.pk_ref.pv_ref, ...), custom_call_target="tpu_custom_call" | custom-call | flops 8053063680 | bytes 5111808 | tf_op jit(solution)/shard_map/attend/pallas_call | solution.py:189
  254.4 9.5 %attend.5 = (bf16[256,8192]{1,0:T(8,128)(2,1)}, f32[8,128]{1,0:T(8,128)}) custom-call(s32[17]{0:T(128)} %pad_add_fusion.meta_ref, f32[1,8192]{1,0:T(1,128)} %bitcast.50, bf16[256,8192]{1,0:T(8,128)(2,1)} %bitcast.42, bf16[512,2048]{1,0:T(8,128)(2,1)} %join_prefix.1.pk_ref.pv_ref, ...), custom_call_target="tpu_custom_call", output_to_operand_aliasing={{0}: (23, {})} | custom-call | flops 5368709120 | bytes 3407872 | tf_op jit(solution)/shard_map/attend/pallas_call | solution.py:189
  264.7 9.5 %attend.6 = (bf16[256,8192]{1,0:T(8,128)(2,1)}, f32[8,128]{1,0:T(8,128)}) custom-call(s32[17]{0:T(128)} %pad_add_fusion.meta_ref, f32[1,8192]{1,0:T(1,128)} %bitcast.51, bf16[256,8192]{1,0:T(8,128)(2,1)} %bitcast.43, bf16[512,2048]{1,0:T(8,128)(2,1)} %join_prefix.1.pk_ref.pv_ref, ...), custom_call_target="tpu_custom_call", output_to_operand_aliasing={{0}: (23, {})} | custom-call | flops 5368709120 | bytes 3407872 | tf_op jit(solution)/shard_map/attend/pallas_call | solution.py:189
  275.0 5.9 %attend.7 = (bf16[256,8192]{1,0:T(8,128)(2,1)}, f32[8,128]{1,0:T(8,128)}) custom-call(s32[17]{0:T(128)} %pad_add_fusion.meta_ref, f32[1,8192]{1,0:T(1,128)} %bitcast.52, bf16[256,8192]{1,0:T(8,128)(2,1)} %bitcast.44, bf16[512,2048]{1,0:T(8,128)(2,1)} %join_prefix.1.pk_ref.pv_ref, ...), custom_call_target="tpu_custom_call", output_to_operand_aliasing={{0}: (23, {})} | custom-call | flops 2684354560 | bytes 1703936 | tf_op jit(solution)/shard_map/attend/pallas_call | solution.py:189
  286.4 1.5 collective-permute-start.22
  295.5 1.6 collective-permute-start.24
  297.1 2.6 collective-permute-start.25
  302.5 2.7 collective-permute-done.26
  (131 shorter events, 27.5 us)
Async XLA Ops:
  2.3 41.8 %collective-permute-start = (bf16[528,256]{1,0:T(8,128)(2,1)S(1)}, bf16[528,256]{1,0:T(8,128)(2,1)S(1)}, u32[]{:S(2)}, u32[]{:S(2)}) collective-permute-start(bf16[528,256]{1,0:T(8,128)(2,1)S(1)} %get-tuple-element.71.rest_0_), channel_id=1, source_target_pairs={{0,2},{1,3},{2,0},{3,1},{4,6},{5,7},{6,4},{7,5},{8,10},{9,11},{10,... | collective-permute-start | bytes 811016 | tf_op jit(solution)/shard_map/ppermute | solution.py:227
  5.3 38.8 %collective-permute-start.1 = (bf16[528,256]{1,0:T(8,128)(2,1)S(1)}, bf16[528,256]{1,0:T(8,128)(2,1)S(1)}, u32[]{:S(2)}, u32[]{:S(2)}) collective-permute-start(bf16[528,256]{1,0:T(8,128)(2,1)S(1)} %get-tuple-element.71.rest_0_), channel_id=1, source_target_pairs={{0,4},{1,5},{2,6},{3,7},{4,0},{5,1},{6,2},{7,3},{8,12},{9,13},{10,... | collective-permute-start | bytes 811016 | tf_op jit(solution)/shard_map/ppermute | solution.py:227
  6.8 37.3 %collective-permute-start.2 = (bf16[528,256]{1,0:T(8,128)(2,1)S(1)}, bf16[528,256]{1,0:T(8,128)(2,1)S(1)}, u32[]{:S(2)}, u32[]{:S(2)}) collective-permute-start(bf16[528,256]{1,0:T(8,128)(2,1)S(1)} %get-tuple-element.71.rest_0_), channel_id=1, source_target_pairs={{0,6},{1,7},{2,4},{3,5},{4,2},{5,3},{6,0},{7,1},{8,14},{9,15},{10,... | collective-permute-start | bytes 811016 | tf_op jit(solution)/shard_map/ppermute | solution.py:227
  40.5 55.2 %collective-permute-start.4 = (bf16[2,128,512]{2,1,0:T(8,128)(2,1)}, bf16[2,128,512]{2,1,0:T(8,128)(2,1)S(1)}, u32[]{:S(2)}, u32[]{:S(2)}) collective-permute-start(bf16[2,128,512]{2,1,0:T(8,128)(2,1)} %get-tuple-element.39), channel_id=1, source_target_pairs={{0,2},{1,3},{2,0},{3,1},{4,6},{5,7},{6,4},{7,5},{8,10},{9,11},{10,... | collective-permute-start | bytes 786440 | tf_op jit(solution)/shard_map/ppermute | solution.py:227
  42.6 56.1 %collective-permute-start.5 = (bf16[2,128,512]{2,1,0:T(8,128)(2,1)}, bf16[2,128,512]{2,1,0:T(8,128)(2,1)S(1)}, u32[]{:S(2)}, u32[]{:S(2)}) collective-permute-start(bf16[2,128,512]{2,1,0:T(8,128)(2,1)} %get-tuple-element.40), channel_id=1, source_target_pairs={{0,4},{1,5},{2,6},{3,7},{4,0},{5,1},{6,2},{7,3},{8,12},{9,13},{10,... | collective-permute-start | bytes 786440 | tf_op jit(solution)/shard_map/ppermute | solution.py:227
  45.3 128.1 %collective-permute-start.3 = (bf16[4,528,256]{2,1,0:T(8,128)(2,1)}, bf16[4,528,256]{2,1,0:T(8,128)(2,1)S(1)}, u32[]{:S(2)}, u32[]{:S(2)}) collective-permute-start(bf16[4,528,256]{2,1,0:T(8,128)(2,1)} %pad_maximum_fusion), channel_id=1, source_target_pairs={{0,1},{1,0},{2,3},{3,2},{4,5},{5,4},{6,7},{7,6},{8,9},{9,8},{10,11... | collective-permute-start | bytes 3244040 | tf_op jit(solution)/shard_map/ppermute | solution.py:227
  95.0 26.1 %collective-permute-start.11 = (bf16[2,128,768]{2,1,0:T(8,128)(2,1)}, bf16[2,128,768]{2,1,0:T(8,128)(2,1)}, u32[]{:S(2)}, u32[]{:S(2)}) collective-permute-start(bf16[2,128,768]{2,1,0:T(8,128)(2,1)} %get-tuple-element.51), channel_id=1, source_target_pairs={{0,2},{1,3},{2,0},{3,1},{4,6},{5,7},{6,4},{7,5},{8,10},{9,11},{10,... | collective-permute-start | bytes 1179656 | tf_op jit(solution)/shard_map/ppermute | solution.py:227
  95.7 27.2 %collective-permute-start.12 = (bf16[2,128,768]{2,1,0:T(8,128)(2,1)}, bf16[2,128,768]{2,1,0:T(8,128)(2,1)}, u32[]{:S(2)}, u32[]{:S(2)}) collective-permute-start(bf16[2,128,768]{2,1,0:T(8,128)(2,1)} %get-tuple-element.52), channel_id=1, source_target_pairs={{0,4},{1,5},{2,6},{3,7},{4,0},{5,1},{6,2},{7,3},{8,12},{9,13},{10,... | collective-permute-start | bytes 1179656 | tf_op jit(solution)/shard_map/ppermute | solution.py:227
  95.7 63.3 %collective-permute-start.13 = (bf16[2,128,768]{2,1,0:T(8,128)(2,1)}, bf16[2,128,768]{2,1,0:T(8,128)(2,1)}, u32[]{:S(2)}, u32[]{:S(2)}) collective-permute-start(bf16[2,128,768]{2,1,0:T(8,128)(2,1)} %get-tuple-element.53), channel_id=1, source_target_pairs={{0,6},{1,7},{2,4},{3,5},{4,2},{5,3},{6,0},{7,1},{8,14},{9,15},{10,... | collective-permute-start | bytes 1179656 | tf_op jit(solution)/shard_map/ppermute | solution.py:227
  98.6 22.2 %collective-permute-start.6 = (bf16[2,128,512]{2,1,0:T(8,128)(2,1)S(1)}, bf16[2,128,512]{2,1,0:T(8,128)(2,1)S(1)}, u32[]{:S(2)}, u32[]{:S(2)}) collective-permute-start(bf16[2,128,512]{2,1,0:T(8,128)(2,1)S(1)} %copy-done.23), channel_id=1, source_target_pairs={{0,6},{1,7},{2,4},{3,5},{4,2},{5,3},{6,0},{7,1},{8,14},{9,15},{10,... | collective-permute-start | bytes 786440 | tf_op jit(solution)/shard_map/ppermute | solution.py:227
  120.8 38.6 %collective-permute-start.7 = (bf16[2,128,256]{2,1,0:T(8,128)(2,1)}, bf16[2,128,256]{2,1,0:T(8,128)(2,1)S(1)}, u32[]{:S(2)}, u32[]{:S(2)}) collective-permute-start(bf16[2,128,256]{2,1,0:T(8,128)(2,1)} %get-tuple-element.43), channel_id=1, source_target_pairs={{0,2},{1,3},{2,0},{3,1},{4,6},{5,7},{6,4},{7,5},{8,10},{9,11},{10,... | collective-permute-start | bytes 393224 | tf_op jit(solution)/shard_map/ppermute | solution.py:227
  121.1 40.2 %collective-permute-start.8 = (bf16[2,128,256]{2,1,0:T(8,128)(2,1)}, bf16[2,128,256]{2,1,0:T(8,128)(2,1)S(1)}, u32[]{:S(2)}, u32[]{:S(2)}) collective-permute-start(bf16[2,128,256]{2,1,0:T(8,128)(2,1)} %get-tuple-element.44), channel_id=1, source_target_pairs={{0,4},{1,5},{2,6},{3,7},{4,0},{5,1},{6,2},{7,3},{8,12},{9,13},{10,... | collective-permute-start | bytes 393224 | tf_op jit(solution)/shard_map/ppermute | solution.py:227
  122.9 40.9 %collective-permute-start.9 = (bf16[2,128,256]{2,1,0:T(8,128)(2,1)}, bf16[2,128,256]{2,1,0:T(8,128)(2,1)}, u32[]{:S(2)}, u32[]{:S(2)}) collective-permute-start(bf16[2,128,256]{2,1,0:T(8,128)(2,1)} %get-tuple-element.45), channel_id=1, source_target_pairs={{0,6},{1,7},{2,4},{3,5},{4,2},{5,3},{6,0},{7,1},{8,14},{9,15},{10,... | collective-permute-start | bytes 393224 | tf_op jit(solution)/shard_map/ppermute | solution.py:227
  159.1 9.5 %collective-permute-start.14 = (bf16[2,128,512]{2,1,0:T(8,128)(2,1)S(1)}, bf16[2,128,512]{2,1,0:T(8,128)(2,1)S(1)}, u32[]{:S(2)}, u32[]{:S(2)}) collective-permute-start(bf16[2,128,512]{2,1,0:T(8,128)(2,1)S(1)} %copy-done.22), channel_id=1, source_target_pairs={{0,2},{1,3},{2,0},{3,1},{4,6},{5,7},{6,4},{7,5},{8,10},{9,11},{10,... | collective-permute-start | bytes 786440 | tf_op jit(solution)/shard_map/ppermute | solution.py:227
  159.4 11.6 %collective-permute-start.15 = (bf16[2,128,512]{2,1,0:T(8,128)(2,1)S(1)}, bf16[2,128,512]{2,1,0:T(8,128)(2,1)S(1)}, u32[]{:S(2)}, u32[]{:S(2)}) collective-permute-start(bf16[2,128,512]{2,1,0:T(8,128)(2,1)S(1)} %copy-done.21), channel_id=1, source_target_pairs={{0,4},{1,5},{2,6},{3,7},{4,0},{5,1},{6,2},{7,3},{8,12},{9,13},{10,... | collective-permute-start | bytes 786440 | tf_op jit(solution)/shard_map/ppermute | solution.py:227
  161.3 11.3 %collective-permute-start.16 = (bf16[2,128,512]{2,1,0:T(8,128)(2,1)S(1)}, bf16[2,128,512]{2,1,0:T(8,128)(2,1)S(1)}, u32[]{:S(2)}, u32[]{:S(2)}) collective-permute-start(bf16[2,128,512]{2,1,0:T(8,128)(2,1)S(1)} %copy-done.20), channel_id=1, source_target_pairs={{0,6},{1,7},{2,4},{3,5},{4,2},{5,3},{6,0},{7,1},{8,14},{9,15},{10,... | collective-permute-start | bytes 786440 | tf_op jit(solution)/shard_map/ppermute | solution.py:227
  163.7 89.8 %collective-permute-start.18 = (bf16[4,128,512]{2,1,0:T(8,128)(2,1)}, bf16[4,128,512]{2,1,0:T(8,128)(2,1)S(1)}, u32[]{:S(2)}, u32[]{:S(2)}) collective-permute-start(bf16[4,128,512]{2,1,0:T(8,128)(2,1)} %pad_maximum_fusion.3), channel_id=1, source_target_pairs={{0,1},{1,0},{2,3},{3,2},{4,5},{5,4},{6,7},{7,6},{8,9},{9,8},{10,11... | collective-permute-start | bytes 1572872 | tf_op jit(solution)/shard_map/ppermute | solution.py:227
  168.6 105.7 %collective-permute-start.10 = (bf16[4,128,256]{2,1,0:T(8,128)(2,1)S(1)}, bf16[4,128,256]{2,1,0:T(8,128)(2,1)S(1)}, u32[]{:S(2)}, u32[]{:S(2)}) collective-permute-start(bf16[4,128,256]{2,1,0:T(8,128)(2,1)S(1)} %pad_maximum_fusion.4), channel_id=1, source_target_pairs={{0,1},{1,0},{2,3},{3,2},{4,5},{5,4},{6,7},{7,6},{8,9},{9,8},{10,11... | collective-permute-start | bytes 786440 | tf_op jit(solution)/shard_map/ppermute | solution.py:227
  171.0 69.1 %collective-permute-start.19 = (bf16[4,128,768]{2,1,0:T(8,128)(2,1)}, bf16[4,128,768]{2,1,0:T(8,128)(2,1)}, u32[]{:S(2)}, u32[]{:S(2)}) collective-permute-start(bf16[4,128,768]{2,1,0:T(8,128)(2,1)} %pad_maximum_fusion.1), channel_id=1, source_target_pairs={{0,1},{1,0},{2,3},{3,2},{4,5},{5,4},{6,7},{7,6},{8,9},{9,8},{10,11... | collective-permute-start | bytes 2359304 | tf_op jit(solution)/shard_map/ppermute | solution.py:227
  173.4 90.5 %collective-permute-start.17 = (bf16[4,128,512]{2,1,0:T(8,128)(2,1)}, bf16[4,128,512]{2,1,0:T(8,128)(2,1)S(1)}, u32[]{:S(2)}, u32[]{:S(2)}) collective-permute-start(bf16[4,128,512]{2,1,0:T(8,128)(2,1)} %pad_maximum_fusion.2), channel_id=1, source_target_pairs={{0,1},{1,0},{2,3},{3,2},{4,5},{5,4},{6,7},{7,6},{8,9},{9,8},{10,11... | collective-permute-start | bytes 1572872 | tf_op jit(solution)/shard_map/ppermute | solution.py:227
  285.1 4.8 %collective-permute-start.21 = (f32[2]{0:T(128)S(1)}, f32[2]{0:T(128)S(1)}, u32[]{:S(2)}, u32[]{:S(2)}) collective-permute-start(f32[2]{0:T(128)S(1)} %pad_maximum_fusion.5), channel_id=1, source_target_pairs={{0,2},{1,3},{2,0},{3,1},{4,6},{5,7},{6,4},{7,5},{8,10},{9,11},{10,... | collective-permute-start | bytes 32 | tf_op jit(solution)/shard_map/ppermute | solution.py:227
  286.4 4.7 %collective-permute-start.22 = (f32[2]{0:T(128)S(1)}, f32[2]{0:T(128)S(1)}, u32[]{:S(2)}, u32[]{:S(2)}) collective-permute-start(f32[2]{0:T(128)S(1)} %pad_maximum_fusion.5), channel_id=1, source_target_pairs={{0,4},{1,5},{2,6},{3,7},{4,0},{5,1},{6,2},{7,3},{8,12},{9,13},{10,... | collective-permute-start | bytes 32 | tf_op jit(solution)/shard_map/ppermute | solution.py:227
  295.5 5.0 %collective-permute-start.24 = (f32[1]{0:T(128)}, f32[1]{0:T(128)}, u32[]{:S(2)}, u32[]{:S(2)}) collective-permute-start(f32[1]{0:T(128)} %bitcast.20), channel_id=1, source_target_pairs={{0,8},{8,0},{16,24},{24,16},{1,9},{9,1},{17,25},{25,17},{2,10},{10... | collective-permute-start | bytes 20 | tf_op jit(solution)/shard_map/ppermute | solution.py:265
  299.7 5.5 %collective-permute-start.26 = (f32[1]{0:T(128)}, f32[1]{0:T(128)}, u32[]{:S(2)}, u32[]{:S(2)}) collective-permute-start(f32[1]{0:T(128)} %bitcast.20), channel_id=1, source_target_pairs={{0,24},{8,16},{16,8},{24,0},{1,25},{9,17},{17,9},{25,1},{2,26},{10... | collective-permute-start | bytes 20 | tf_op jit(solution)/shard_map/ppermute | solution.py:265
  (27 other events, 719.3 us)

commit v2 on v0

v2 whole, which is shorter than its diff:
```python
import functools
import math

import jax
import jax.numpy as jnp
from jax import lax
from jax.experimental import pallas as pl
from jax.experimental.pallas import tpu as pltpu
from jax.sharding import PartitionSpec as P

HEADS = 64
KVH = 8
HD = 128
GROUPS = HEADS // KVH
SCALE = math.log2(math.e) / math.sqrt(HD)
LOW = -1e30
ROOM = 100.0
PARTS = ((0, 6, True), (6, 2, False))
LAST = 16
EMPTY = 1024.0
NT = (((1,), (1,)), ((), ()))
VMEM_LIMIT = 56 * 2**20


def lasting(microseconds):
    return pl.CostEstimate(flops=0, bytes_accessed=int(microseconds * 3.5e6), transcendentals=0)


PARAMS = pltpu.CompilerParams(vmem_limit_bytes=VMEM_LIMIT)


def slot_of(judge, routes):
    tile, found = jnp.int32(0), jnp.bool_(False)
    for s in range(routes.shape[0]):
        here = routes[s] == judge
        tile, found = jnp.where(here, s, tile), found | here
    return tile, found


def pack_kernel(chips, parts, me, routes, mate_routes, *rest):
    tiles, outs = rest[: 2 * chips], list(rest[2 * chips :])
    chip, core = me[0] // 2, me[0] % 2
    top = (lax.broadcasted_iota(jnp.int32, (16, HD), 0) == 0) & (pl.program_id(0) == 0)
    for head_from, heads, together in parts:
        width = heads * HD
        for offset in range(chips):
            out = outs[0].at[chip ^ offset] if together else outs.pop(0)
            for n, held in enumerate((routes, mate_routes)):
                tile = tiles[2 * offset + n]
                found = slot_of(2 * (chip ^ offset) + core, held)[1]
                for half in range(2):
                    first = (half * KVH + head_from) * HD
                    out[n, :, half * width : (half + 1) * width] = tile[0, :, first : first + width]
                mark = top & jnp.logical_not(found)
                kept = tile[0, :16, head_from * HD : (head_from + 1) * HD]
                out[n, :16, :HD] = jnp.where(mark, jnp.full_like(kept, EMPTY), kept)
        if together:
            outs.pop(0)


def pack(parts, chips, me, routes, mate_routes, patch, mate_patch):
    tile_rows, width = patch.shape[1:]
    rows = tile_rows // 4
    shapes, specs, sources = [], [], []
    for _, heads, together in parts:
        shape = (2, tile_rows, 2 * heads * HD)
        block = (2, rows, 2 * heads * HD)
        if together:
            shapes.append((chips,) + shape)
            specs.append(pl.BlockSpec((chips,) + block, lambda r, *_: (0, 0, r, 0)))
        else:
            shapes += [shape] * chips
            specs += [pl.BlockSpec(block, lambda r, *_: (0, r, 0))] * chips
    for offset in range(chips):
        for n in range(2):

            def source(r, me, *held, offset=offset, n=n):
                judge = 2 * ((me[0] // 2) ^ offset) + me[0] % 2
                return slot_of(judge, held[n])[0], r, 0

            sources.append(pl.BlockSpec((1, rows, width), source))
    return pl.pallas_call(
        functools.partial(pack_kernel, chips, parts),
        out_shape=[jax.ShapeDtypeStruct(shape, patch.dtype) for shape in shapes],
        grid_spec=pltpu.PrefetchScalarGridSpec(
            num_scalar_prefetch=3,
            grid=(tile_rows // rows,),
            in_specs=sources,
            out_specs=specs,
        ),
        compiler_params=PARAMS,
        cost_estimate=lasting(5),
        name="pack_tiles",
    )(me, routes, mate_routes, *([patch, mate_patch] * chips))


def pipelined(scores, finish):
    held = scores(0)
    for h in range(1, GROUPS):
        following = scores(h)
        finish(held, h - 1)
        held = following
    finish(held, GROUPS - 1)


def text_kernel(
    per_slot, me, length, q_ref, kn_ref, kf_ref, vn_ref, vf_ref, sk_ref, sv_ref, o_ref, stat_ref,
    kbuf, vbuf,
):
    prefix_rows, suffix_rows = kn_ref.shape[1], sk_ref.shape[0]
    g = pl.program_id(0)
    live = lax.broadcasted_iota(jnp.int32, (prefix_rows, HD), 0) < length[0]

    @pl.when(g == 0)
    def _():
        vbuf[:prefix_rows, HD:] = live.astype(vbuf.dtype)
        vbuf[prefix_rows:, HD:] = jnp.ones((suffix_rows, HD), vbuf.dtype)

    def held_by(head, near, far):
        return jnp.where((head // per_slot) % 2 == me[0] % 2, near[0], far[0])

    keys = held_by(g, kn_ref, kf_ref)
    values = held_by(KVH + g, vn_ref, vf_ref)
    kbuf[:prefix_rows] = jnp.where(live, keys, keys[0:1, :])
    vbuf[:prefix_rows, :HD] = jnp.where(live, values, jnp.zeros_like(values))
    kbuf[prefix_rows:] = sk_ref[...]
    vbuf[prefix_rows:, :HD] = sv_ref[...]
    causal = lax.broadcasted_iota(jnp.int32, (suffix_rows, suffix_rows), 1) <= lax.broadcasted_iota(
        jnp.int32, (suffix_rows, suffix_rows), 0
    )
    def scores(h):
        s = lax.dot_general(
            q_ref[:, h * HD : (h + 1) * HD], kbuf[...], NT, preferred_element_type=jnp.float32
        )
        return jnp.concatenate(
            [s[:, :prefix_rows], jnp.where(causal, s[:, prefix_rows:], LOW)], axis=1
        )

    def finish(s, h):
        peak = jnp.max(s, axis=1, keepdims=True) * SCALE
        weights = jnp.exp2(s * SCALE - peak).astype(jnp.bfloat16)
        mixed = jnp.dot(weights, vbuf[...], preferred_element_type=jnp.float32)
        o_ref[:, h * HD : (h + 1) * HD] = mixed[:, :HD]
        stat_ref[:, h : h + 1] = peak
        stat_ref[:, GROUPS + h : GROUPS + h + 1] = mixed[:, HD : HD + 1]

    pipelined(scores, finish)


def attend_text(me, length, queries, near, far, suffix):
    rows = queries.shape[0]
    prefix_rows, suffix_rows = near.shape[1], suffix.shape[0]
    per_slot = near.shape[2] // HD
    total, wide = prefix_rows + suffix_rows, GROUPS * HD

    def block(shift):
        def index(g, me, length):
            head = shift + g
            return (head // per_slot // 2) ^ (me[0] // 2), 0, head % per_slot

        return pl.BlockSpec((1, prefix_rows, HD), index)

    return pl.pallas_call(
        functools.partial(text_kernel, per_slot),
        out_shape=[
            jax.ShapeDtypeStruct(queries.shape, jnp.float32),
            jax.ShapeDtypeStruct((rows, KVH * HD), jnp.float32),
        ],
        grid_spec=pltpu.PrefetchScalarGridSpec(
            num_scalar_prefetch=2,
            grid=(KVH,),
            in_specs=[
                pl.BlockSpec((rows, wide), lambda g, me, length: (0, g)),
                block(0),
                block(0),
                block(KVH),
                block(KVH),
                pl.BlockSpec((suffix_rows, HD), lambda g, me, length: (0, g)),
                pl.BlockSpec((suffix_rows, HD), lambda g, me, length: (0, KVH + g)),
            ],
            out_specs=[
                pl.BlockSpec((rows, wide), lambda g, me, length: (0, g)),
                pl.BlockSpec((rows, HD), lambda g, me, length: (0, g)),
            ],
            scratch_shapes=[
                pltpu.VMEM((total, HD), queries.dtype),
                pltpu.VMEM((total, 2 * HD), queries.dtype),
            ],
        ),
        compiler_params=PARAMS,
        cost_estimate=lasting(21),
        name="attend_text",
    )(me, length, queries, near, far, near, far, suffix, suffix)


def image_kernel(
    chips, kept, together, chained, stored, scored, head_ref, q_ref, acc_ref, stat_ref, *rest
):
    rest = list(rest)
    tiles = [rest.pop(0) for _ in range(1 if together else chips)]
    before = rest.pop(0) if chained and scored else None
    if chained and stored:
        rest.pop(0)
    o_ref = rest.pop(0) if stored else None
    score_ref = rest.pop(0) if scored else None
    kbuf, vbuf, gain_ref, place_ref = rest
    slots = 2 * chips
    rows = q_ref.shape[0]
    tile_rows, width = tiles[0].shape[-2], tiles[0].shape[-1] // 2
    total = kept * tile_rows
    g = pl.program_id(0)

    @pl.when(g == 0)
    def _():
        gain_ref[...] = before[...] if before is not None else jnp.zeros_like(gain_ref)
        vbuf[:, HD:] = jnp.ones((total + tile_rows, HD), vbuf.dtype)
        count = jnp.int32(0)
        for n in range(slots):
            tile = tiles[0].at[n // 2, n % 2] if together else tiles[n // 2].at[n % 2]
            found = jnp.max(tile[0:1, :HD].astype(jnp.float32)) < EMPTY
            place_ref[n] = jnp.where(found, count, kept)
            count = count + jnp.where(found, 1, 0)

    for n in range(slots):
        row = pl.multiple_of(place_ref[n] * tile_rows, tile_rows)
        tile = tiles[0].at[n // 2, n % 2] if together else tiles[n // 2].at[n % 2]
        column = pl.ds(pl.multiple_of(g * HD, HD), HD)
        kbuf[pl.ds(row, tile_rows), :] = tile[:, column]
        column = pl.ds(pl.multiple_of(width + g * HD, HD), HD)
        vbuf[pl.ds(row, tile_rows), :HD] = tile[:, column]

    def scores(column):
        return lax.dot_general(
            q_ref[:, column], kbuf[:total], NT, preferred_element_type=jnp.float32
        )

    def close(summed, totals, column):
        out = (summed / totals).astype(jnp.bfloat16)
        if stored:
            o_ref[:, column] = out
        last = out[rows - 8 :, :].astype(jnp.float32)
        return last * head_ref[0:1, column] if scored else 0.0

    gains = [jnp.zeros((8, HD), jnp.float32), jnp.full((8, HD), LOW, jnp.float32)]

    def finish(s, h):
        column = slice(h * HD, (h + 1) * HD)
        held = stat_ref[:, h : h + 1]
        powers = []
        for k in range(total // HD):
            power = s[:, k * HD : (k + 1) * HD] * SCALE - held
            gains[1] = jnp.maximum(gains[1], jnp.max(power.reshape(rows // 8, 8, HD), axis=0))
            powers.append(jnp.exp2(power).astype(jnp.bfloat16))
        weights = jnp.concatenate(powers, axis=1)
        mixed = jnp.dot(weights, vbuf[:total], preferred_element_type=jnp.float32)
        totals = mixed[:, HD:] + stat_ref[:, GROUPS + h : GROUPS + h + 1]
        gains[0] = gains[0] + close(mixed[:, :HD] + acc_ref[:, column], totals, column)

    pipelined(lambda h: scores(slice(h * HD, (h + 1) * HD)), finish)
    fits = jnp.max(gains[1]) < ROOM

    if scored:
        @pl.when(fits)
        def _():
            gain_ref[...] += gains[0]

    @pl.when(jnp.logical_not(fits))
    def _():
        def one(h, gain):
            column = pl.ds(pl.multiple_of(h * HD, HD), HD)
            s = scores(column) * SCALE
            lane = lax.broadcasted_iota(jnp.int32, (rows, HD), 1)
            held = jnp.sum(jnp.where(lane == h, stat_ref[...], 0.0), axis=1, keepdims=True)
            sums = jnp.where(lane == GROUPS + h, stat_ref[...], 0.0)
            sums = jnp.sum(sums, axis=1, keepdims=True)
            peak = jnp.maximum(held, jnp.max(s, axis=1, keepdims=True))
            weights = jnp.exp2(s - peak).astype(jnp.bfloat16)
            mixed = jnp.dot(weights, vbuf[:total], preferred_element_type=jnp.float32)
            fade = jnp.exp2(held - peak)
            summed = acc_ref[:, column] * fade + mixed[:, :HD]
            totals = sums * fade + mixed[:, HD:]
            return gain + close(summed, totals, column)

        gain = lax.fori_loop(0, GROUPS, one, jnp.zeros((8, HD), jnp.float32))
        if scored:
            gain_ref[...] += gain

    if scored:
        @pl.when(g == pl.num_programs(0) - 1)
        def _():
            if stored:
                score_ref[...] = gain_ref[...]
            else:
                score_ref[...] = jnp.broadcast_to(gain_ref[7:8, :], score_ref.shape)


def attend_image(
    chips, kept, part, head, queries, text, tiles, context=None, share=None, devices=0
):
    head_from, heads, together = part
    stored, scored = devices == 0, devices > 0 or context is None
    chained = context is not None or share is not None
    all_rows = queries.shape[0]
    rows = all_rows if stored else LAST
    tile_rows = tiles[0].shape[-2]
    total, wide = kept * tile_rows, GROUPS * HD
    column = lambda g: (all_rows // rows - 1, head_from + g)
    fixed = lambda g: (0, 0)
    specs = [
        pl.BlockSpec((1, wide), lambda g: (0, head_from + g)),
        pl.BlockSpec((rows, wide), column),
        pl.BlockSpec((rows, wide), column),
        pl.BlockSpec((rows, HD), column),
    ] + [pl.BlockSpec(memory_space=pltpu.VMEM) for tile in tiles]
    operands = [head, queries, *text, *tiles]
    aliases, shapes, outs = {}, [], []
    if chained and scored:
        specs.append(pl.BlockSpec((8, HD), fixed))
        operands.append(share)
    if chained and stored:
        aliases = {len(operands): 0}
        specs.append(pl.BlockSpec(memory_space=pl.ANY))
        operands.append(context)
    if stored:
        shapes.append(jax.ShapeDtypeStruct(queries.shape, queries.dtype))
        outs.append(pl.BlockSpec((rows, wide), column))
    if scored:
        shape = (8 if stored else devices, HD)
        shapes.append(jax.ShapeDtypeStruct(shape, jnp.float32))
        outs.append(pl.BlockSpec(shape, fixed))
    return pl.pallas_call(
        functools.partial(image_kernel, chips, kept, together, chained, stored, scored),
        out_shape=shapes,
        grid=(heads,),
        in_specs=specs,
        out_specs=outs,
        scratch_shapes=[
            pltpu.VMEM((total + tile_rows, HD), queries.dtype),
            pltpu.VMEM((total + tile_rows, 2 * HD), queries.dtype),
            pltpu.VMEM((8, HD), jnp.float32),
            pltpu.SMEM((2 * chips,), jnp.int32),
        ],
        input_output_aliases=aliases,
        compiler_params=PARAMS,
        cost_estimate=lasting(2 * heads),
        name="attend_image" if stored else "last_rows",
    )(*operands)


def normalize_kernel(prompts, slots, every_ref, out_ref):
    own = lax.axis_index("prompt") * slots + lax.axis_index("slot")
    score = jnp.sum(every_ref[...], axis=1, keepdims=True)
    score = jnp.broadcast_to(score, every_ref.shape).reshape(prompts, slots, HD)
    deviation = score - jnp.sum(score, axis=1, keepdims=True) / slots
    spread = jnp.sum(jnp.sum(deviation * deviation, axis=0), axis=0, keepdims=True)
    advantage = deviation / jnp.sqrt(spread / (prompts * slots) + 1e-06)
    advantage = advantage.reshape(prompts * slots, HD)
    row = lax.broadcasted_iota(jnp.int32, advantage.shape, 0)
    out_ref[...] = jnp.sum(jnp.where(row == own, advantage, 0.0), axis=0, keepdims=True)[:, :1]


def per_device(patch_kv, routes, prefix_kv, prefix_len, queries, suffix_kv, score_head):
    slot_count = lax.axis_size("slot")
    prompt_count = lax.axis_size("prompt")
    chips = slot_count // 2
    kept = slot_count // 2
    me = lax.axis_index("slot").astype(jnp.int32).reshape(1)

    def swap(x, k):
        return lax.ppermute(x, "slot", [(i, i ^ k) for i in range(slot_count)])

    mate_patch, mate_routes = swap(patch_kv[0], 1), swap(routes[0], 1)
    near = [prefix_kv] + [swap(prefix_kv, 2 * offset) for offset in range(1, chips)]
    buffers = pack(PARTS, chips, me, routes[0], mate_routes, patch_kv[0], mate_patch)
    buffers = lax.optimization_barrier((list(buffers), near))[0]
    near = jnp.concatenate(near, axis=0)
    far = swap(near, 1)
    text = attend_text(me, prefix_len, queries[0, 0], near, far, suffix_kv[0, 0])

    head = score_head.reshape(1, -1)
    groups = [[2 * a + b for a in range(chips)] for b in range(2)]
    arrived, first = [], 0
    for n, (_, _, together) in enumerate(PARTS):
        sent = buffers[first : first + (1 if together else chips)]
        first += len(sent)
        if together:
            arrived.append(
                [lax.all_to_all(sent[0], "slot", 0, 0, tiled=True, axis_index_groups=groups)]
            )
        else:
            arrived.append(
                [sent[0]] + [swap(sent[offset], 2 * offset) for offset in range(1, chips)]
            )
    devices = prompt_count * slot_count
    image = functools.partial(attend_image, chips, kept)
    context, share = image(PARTS[0], head, queries[0, 0], text, arrived[0])
    (shares,) = image(
        PARTS[1], head, queries[0, 0], text, arrived[1], share=share, devices=devices
    )
    every = lax.all_to_all(shares, ("prompt", "slot"), 0, 0, tiled=True)
    (context,) = image(
        PARTS[1], head, queries[0, 0], text, arrived[1], context=context
    )
    advantage = pl.pallas_call(
        functools.partial(normalize_kernel, prompt_count, slot_count),
        out_shape=jax.ShapeDtypeStruct((1, 1), jnp.float32),
        in_specs=[pl.BlockSpec(memory_space=pltpu.VMEM)],
        out_specs=pl.BlockSpec(memory_space=pltpu.VMEM),
        cost_estimate=lasting(1),
        name="normalize",
    )(every)
    return (context[None, None], advantage)


def solution(mesh):
    placed = (
        P("prompt", "slot", None, None),
        P("prompt", "slot"),
        P("prompt", None, "slot"),
        P("prompt"),
        P("prompt", "slot", None, None),
        P("prompt", "slot", None, None),
        P(),
    )
    return jax.shard_map(
        per_device,
        mesh=mesh,
        in_specs=placed,
        out_specs=(P("prompt", "slot", None, None), P("prompt", "slot")),
        check_vma=False,
    )
```

time: 338 us -> 93.5 us (0.28)
  matrix products: 85.3 us -> 0 us
  local copies, waits for them, and re-layouts: 68.3 us -> 7.97 us
  Pallas kernels: 0 us -> 53.4 us
  blocking collectives: 51.9 us -> 0 us
  waiting for transfers between devices: 47.6 us -> 13.1 us
  other arithmetic: 33.8 us -> 0 us
  loops' own time: 22.4 us -> 0 us
  between operations: 17.9 us -> 1.42 us
  starting transfers between devices: 9.76 us -> 16.9 us
    dot_general x17 -> x0, matrix products: 85.3 us -> none  [the longest x8 53.2 us: one_group(): jnp.einsum('gsk,kd->gsd', rounded, value_rows, preferred_element_type=jnp...]
    pallas_call x0 -> x6, Pallas kernels: none -> 53.4 us  [the longest x1 23.9 us: attend_text(): pl.pallas_call(functools.partial(text_kernel, per_slot), out_shape=[jax.S...]
    psum x2 -> x0, blocking collectives: 51.9 us -> none  [the longest x1 39.5 us: per_device(): lax.psum(deviation * deviation, ('prompt', 'slot'))]
    all_to_all x2, waiting for transfers between devices: 46.9 us -> 6.63 us  [the longest x1 5.32 us: per_device(): lax.all_to_all(sent[0], 'slot', 0, 0, tiled=True, axis_index_groups=groups)]
    while x16 -> x0, local copies, waits for them, and re-layouts: 31.9 us -> none
    reduce_sum x9 -> x0, other arithmetic: 23.1 us -> none  [the longest x8 22.2 us: one_group(): totals = jnp.sum(weights, axis=-1, keepdims=True)]
    another operation x1 -> x0, loops' own time: 22.4 us -> none  [per_device(): blocks = lax.map(one_group, jnp.arange(KVH, dtype=jnp.int32))]
    convert_element_type x3 -> x0, local copies, waits for them, and re-layouts: 12.2 us -> none  [the longest x1 7.28 us: per_device(): jnp.transpose(blocks, (2, 0, 1, 3)).reshape(suffix_rows, HEADS * HD)]
  transfers between devices with their start and end apart: 3 -> 11, of which waited for: 1 -> 5; matrix products, arithmetic and copies ran while one was open for 6% -> 3% of each run, Pallas kernels for 0% -> 52%
where the time goes in v2:
time: 93.5 us; the launch traced here: 92.8 us
  Pallas kernels  53.4 us (57%)
  starting transfers between devices  16.9 us (18%)
  waiting for transfers between devices  13.1 us (14%)
  local copies, waits for them, and re-layouts  7.97 us (9%)
  between operations  1.42 us (2%)
    pallas_call x1, Pallas kernels, attend_text(): pl.pallas_call(functools.partial(text_kernel, per_slot), out_shape=[jax.S...  23.9 us
    pallas_call x3, Pallas kernels, attend_image(): pl.pallas_call(functools.partial(image_kernel, chips, kept, together, cha...  22.3 us
    ppermute x9, starting transfers between devices, swap(): return lax.ppermute(x, 'slot', [(i, i ^ k) for i in range(slot_count)])  8.29 us
    unnamed x23, local copies, waits for them, and re-layouts  7 us
    ppermute x9, waiting for transfers between devices, swap(): return lax.ppermute(x, 'slot', [(i, i ^ k) for i in range(slot_count)])  6.49 us
    pallas_call x1, Pallas kernels, pack(): pl.pallas_call(functools.partial(pack_kernel, chips, parts), out_shape=[j...  5.83 us
    all_to_all x1, waiting for transfers between devices, per_device(): lax.all_to_all(sent[0], 'slot', 0, 0, tiled=True, axis_index_groups=groups)  5.32 us
    all_to_all x1, starting transfers between devices, per_device(): every = lax.all_to_all(shares, ('prompt', 'slot'), 0, 0, tiled=True)  4.92 us
  transfers between devices with their start and end apart: 11, of which 5 were waited for; matrix products, arithmetic and copies ran while one was open for 3% of the time, Pallas kernels for 52%

profile of v2, /device:TPU:0, one launch (start us, length us, event | category | flops | bytes accessed | tf_op | source)
XLA Modules:
  0.0 92.8 jit_solution(16857498720977585290)
XLA Ops:
  1.1 2.6 %collective-permute-start = (bf16[1,512,256]{2,1,0:T(8,128)(2,1)}, bf16[1,512,256]{2,1,0:T(8,128)(2,1)S(1)}, u32[]{:S(2)}, u32[]{:S(2)}) collective-permute-start(bf16[1,512,256]{2,1,0:T(8,128)(2,1)} %param.9), channel_id=1, source_target_pairs={{0,2},{1,3},{2,0},{3,1},{4,6},{5,7},{6,4},{7,5},{8,10},{9,11},{10,... | collective-permute-start | bytes 786440 | tf_op jit(solution)/shard_map/ppermute | solution.py:370
  3.7 1.5 %collective-permute-start.1 = (bf16[1,512,256]{2,1,0:T(8,128)(2,1)}, bf16[1,512,256]{2,1,0:T(8,128)(2,1)S(1)}, u32[]{:S(2)}, u32[]{:S(2)}) collective-permute-start(bf16[1,512,256]{2,1,0:T(8,128)(2,1)} %param.9), channel_id=1, source_target_pairs={{0,4},{1,5},{2,6},{3,7},{4,0},{5,1},{6,2},{7,3},{8,12},{9,13},{10,... | collective-permute-start | bytes 786440 | tf_op jit(solution)/shard_map/ppermute | solution.py:370
  5.3 2.8 %collective-permute-done.4.mate_routes = s32[8]{0:T(128)S(1)} collective-permute-done((s32[8]{0:T(128)}, s32[8]{0:T(128)S(1)}, u32[]{:S(2)}, u32[]{:S(2)}) %collective-permute-start.4) | collective-permute-done | bytes 64 | tf_op jit(solution)/shard_map/ppermute | solution.py:370
  8.6 5.8 %pack_tiles.1 = (bf16[4,2,128,1536]{3,2,1,0:T(8,128)(2,1)}, bf16[2,128,512]{2,1,0:T(8,128)(2,1)}, bf16[2,128,512]{2,1,0:T(8,128)(2,1)}, bf16[2,128,512]{2,1,0:T(8,128)(2,1)}, bf16[2,128,512]{2,1,0:T(8,128)(2,1)}) custom-call(s32[1]{0:T(128)} %bitcast.2.me, s32[8]{0:T(128)} %bitcast.29, s32[8]{0:T(128)} %copy-done.9, bf16[8,128,2048]{2,1,0:T(8,128)(2,1)} %bitcast.16, ...), custom_call_target="tpu_custom_call" | custom-call | bytes 17500000 | tf_op jit(solution)/shard_map/pack_tiles/pallas_call | solution.py:82
  14.5 3.5 %collective-permute-done.1 = bf16[1,512,256]{2,1,0:T(8,128)(2,1)S(1)} collective-permute-done((bf16[1,512,256]{2,1,0:T(8,128)(2,1)}, bf16[1,512,256]{2,1,0:T(8,128)(2,1)S(1)}, u32[]{:S(2)}, u32[]{:S(2)}) %collective-permute-start.1) | collective-permute-done | bytes 262176 | tf_op jit(solution)/shard_map/ppermute | solution.py:370
  17.9 0.7 copy-done.6
  18.7 3.7 %all-to-all-start = ((bf16[4,2,128,1536]{3,2,1,0:T(8,128)(2,1)}), bf16[4,2,128,1536]{3,2,1,0:T(8,128)(2,1)S(1)}, u32[]{:S(2)}, u32[]{:S(2)}) async-start(bf16[4,2,128,1536]{3,2,1,0:T(8,128)(2,1)} %get-tuple-element.27), calls=%async_computation | async-start | bytes 6291456 | tf_op jit(solution)/shard_map/all_to_all | solution.py:388
  22.4 1.0 %constant_dynamic-update-slice_fusion.2 = bf16[4,512,256]{2,1,0:T(8,128)(2,1)S(1)} fusion(bf16[4,512,256]{2,1,0:T(8,128)(2,1)S(1)} %constant_dynamic-update-slice_fusion.3, bf16[1,512,256]{2,1,0:T(8,128)(2,1)} %copy-done.5), kind=kLoop, calls=%fused_computation.2 | loop fusion | bytes 524288
  23.4 1.0 %constant_dynamic-update-slice_fusion.1 = bf16[4,512,256]{2,1,0:T(8,128)(2,1)S(1)} fusion(bf16[4,512,256]{2,1,0:T(8,128)(2,1)S(1)} %constant_dynamic-update-slice_fusion.2, bf16[1,512,256]{2,1,0:T(8,128)(2,1)} %copy-done.6), kind=kLoop, calls=%fused_computation.1 | loop fusion | bytes 524288
  24.4 1.0 %constant_dynamic-update-slice_fusion.kn_ref.vn_ref = bf16[4,512,256]{2,1,0:T(8,128)(2,1)S(1)} fusion(bf16[4,512,256]{2,1,0:T(8,128)(2,1)S(1)} %constant_dynamic-update-slice_fusion.1, bf16[1,512,256]{2,1,0:T(8,128)(2,1)} %copy-done.7), kind=kLoop, calls=%fused_computation | loop fusion | bytes 524288 | tf_op jit(solution)/shard_map/concatenate | solution.py:376
  25.4 2.0 %collective-permute-start.6 = (bf16[2,128,512]{2,1,0:T(8,128)(2,1)}, bf16[2,128,512]{2,1,0:T(8,128)(2,1)S(1)}, u32[]{:S(2)}, u32[]{:S(2)}) collective-permute-start(bf16[2,128,512]{2,1,0:T(8,128)(2,1)} %get-tuple-element.24), channel_id=1, source_target_pairs={{0,2},{1,3},{2,0},{3,1},{4,6},{5,7},{6,4},{7,5},{8,10},{9,11},{10,... | collective-permute-start | bytes 786440 | tf_op jit(solution)/shard_map/ppermute | solution.py:370
  27.5 1.5 %collective-permute-start.7 = (bf16[2,128,512]{2,1,0:T(8,128)(2,1)}, bf16[2,128,512]{2,1,0:T(8,128)(2,1)}, u32[]{:S(2)}, u32[]{:S(2)}) collective-permute-start(bf16[2,128,512]{2,1,0:T(8,128)(2,1)} %get-tuple-element.25), channel_id=1, source_target_pairs={{0,4},{1,5},{2,6},{3,7},{4,0},{5,1},{6,2},{7,3},{8,12},{9,13},{10,... | collective-permute-start | bytes 786440 | tf_op jit(solution)/shard_map/ppermute | solution.py:370
  29.7 1.0 %copy-done.2 = bf16[4,512,256]{2,1,0:T(8,128)(2,1)} copy-done((bf16[4,512,256]{2,1,0:T(8,128)(2,1)}, bf16[4,512,256]{2,1,0:T(8,128)(2,1)S(1)}, u32[]{:S(2)}) %copy-start.2) | copy-done | bytes 1048600
  30.7 23.9 %attend_text.1 = (f32[256,8192]{1,0:T(8,128)}, f32[256,1024]{1,0:T(8,128)}) custom-call(s32[1]{0:T(128)} %bitcast.2.me, s32[1]{0:T(128)S(6)} %copy.15.length, bf16[256,8192]{1,0:T(8,128)(2,1)} %bitcast.11, bf16[4,512,256]{2,1,0:T(8,128)(2,1)} %copy-done.1, bf16[4,512,256]{2,1,0:T(8,128)(2,1)} %copy-done.2, bf16[4,512,256]{2,1,0:T(8,128)(2,1)} %copy-done.1, ...), custom_call_target="tpu_custom_call" | custom-call | bytes 73500000 | tf_op jit(solution)/shard_map/attend_text/pallas_call | solution.py:163
  54.6 5.3 %all-to-all-done.rest_0_ = bf16[4,2,128,1536]{3,2,1,0:T(8,128)(2,1)S(1)} async-done(((bf16[4,2,128,1536]{3,2,1,0:T(8,128)(2,1)}), bf16[4,2,128,1536]{3,2,1,0:T(8,128)(2,1)S(1)}, u32[]{:S(2)}, u32[]{:S(2)}) %all-to-all-start) | async-done | bytes 3145760 | tf_op jit(solution)/shard_map/all_to_all | solution.py:388
  59.9 1.7 %copy-done = bf16[4,2,128,1536]{3,2,1,0:T(8,128)(2,1)} copy-done((bf16[4,2,128,1536]{3,2,1,0:T(8,128)(2,1)}, bf16[4,2,128,1536]{3,2,1,0:T(8,128)(2,1)S(1)}, u32[]{:S(2)}) %copy-start) | copy-done | bytes 3145752
  61.6 12.8 %attend_image.2 = (bf16[256,8192]{1,0:T(8,128)(2,1)}, f32[8,128]{1,0:T(8,128)}) custom-call(f32[1,8192]{1,0:T(1,128)} %bitcast.23, bf16[256,8192]{1,0:T(8,128)(2,1)} %bitcast.12, f32[256,8192]{1,0:T(8,128)} %get-tuple-element.16.acc_ref, f32[256,1024]{1,0:T(8,128)} %get-tuple-element.17.stat_ref, bf16[4,2,128,1536]{3,2,1,0:T(8,128)(2,1)} %copy-done), custom_call_target="tpu_custom_call" | custom-call | bytes 42000000 | tf_op jit(solution)/shard_map/attend_image/pallas_call | solution.py:331
  74.4 0.7 copy-done.3
  75.1 3.7 %last_rows.1 = f32[32,128]{1,0:T(8,128)} custom-call(f32[1,8192]{1,0:T(1,128)} %bitcast.24, bf16[256,8192]{1,0:T(8,128)(2,1)} %bitcast.13, f32[256,8192]{1,0:T(8,128)} %get-tuple-element.16.acc_ref, f32[256,1024]{1,0:T(8,128)} %get-tuple-element.17.stat_ref, bf16[2,128,512]{2,1,0:T(8,128)(2,1)} %get-tuple-element.23.rest_0_, bf16[2,128,512]{2,1,0:T(8,128)(2,1)} %copy-done.3, ...), custom_call_target="tpu_custom_call" | custom-call | bytes 14000000 | tf_op jit(solution)/shard_map/last_rows/pallas_call | solution.py:331
  78.8 4.9 %all-to-all-start.1 = ((f32[32,1,128]{2,1,0:T(1,128)}), f32[32,1,128]{2,1,0:T(1,128)S(1)}, u32[]{:S(2)}, u32[]{:S(2)}) async-start(f32[32,1,128]{2,1,0:T(1,128)} %bitcast.26), calls=%async_computation.1 | async-start | bytes 32768 | tf_op jit(solution)/shard_map/all_to_all | solution.py:400
  83.7 5.8 %attend_image.3 = bf16[256,8192]{1,0:T(8,128)(2,1)} custom-call(f32[1,8192]{1,0:T(1,128)} %bitcast.25, bf16[256,8192]{1,0:T(8,128)(2,1)} %bitcast.14, f32[256,8192]{1,0:T(8,128)} %get-tuple-element.16.acc_ref, f32[256,1024]{1,0:T(8,128)} %get-tuple-element.17.stat_ref, ...), custom_call_target="tpu_custom_call", output_to_operand_aliasing={{}: (8, {})} | custom-call | bytes 14000000 | tf_op jit(solution)/shard_map/attend_image/pallas_call | solution.py:331
  89.5 1.3 %all-to-all-done.1 = f32[32,1,128]{2,1,0:T(1,128)S(1)} async-done(((f32[32,1,128]{2,1,0:T(1,128)}), f32[32,1,128]{2,1,0:T(1,128)S(1)}, u32[]{:S(2)}, u32[]{:S(2)}) %all-to-all-start.1) | async-done | bytes 16416 | tf_op jit(solution)/shard_map/all_to_all | solution.py:400
  90.9 0.6 copy-done.8
  91.5 1.4 %normalize.1 = f32[1,1]{1,0:T(1,128)} custom-call(f32[32,128]{1,0:T(8,128)} %bitcast.27), custom_call_target="tpu_custom_call" | custom-call | bytes 3500000 | tf_op jit(solution)/shard_map/normalize/pallas_call | solution.py:404
  (28 shorter events, 1.4 us)
Async XLA Ops:
  0.6 7.6 %collective-permute-start.5 = (bf16[8,128,2048]{2,1,0:T(8,128)(2,1)}, bf16[8,128,2048]{2,1,0:T(8,128)(2,1)}, u32[]{:S(2)}, u32[]{:S(2)}) collective-permute-start(bf16[8,128,2048]{2,1,0:T(8,128)(2,1)} %bitcast.15), channel_id=1, source_target_pairs={{0,1},{1,0},{2,3},{3,2},{4,5},{5,4},{6,7},{7,6},{8,9},{9,8},{10,11... | collective-permute-start | bytes 12582920 | tf_op jit(solution)/shard_map/ppermute | solution.py:370
  1.1 13.3 %collective-permute-start = (bf16[1,512,256]{2,1,0:T(8,128)(2,1)}, bf16[1,512,256]{2,1,0:T(8,128)(2,1)S(1)}, u32[]{:S(2)}, u32[]{:S(2)}) collective-permute-start(bf16[1,512,256]{2,1,0:T(8,128)(2,1)} %param.9), channel_id=1, source_target_pairs={{0,2},{1,3},{2,0},{3,1},{4,6},{5,7},{6,4},{7,5},{8,10},{9,11},{10,... | collective-permute-start | bytes 786440 | tf_op jit(solution)/shard_map/ppermute | solution.py:370
  3.7 14.2 %collective-permute-start.1 = (bf16[1,512,256]{2,1,0:T(8,128)(2,1)}, bf16[1,512,256]{2,1,0:T(8,128)(2,1)S(1)}, u32[]{:S(2)}, u32[]{:S(2)}) collective-permute-start(bf16[1,512,256]{2,1,0:T(8,128)(2,1)} %param.9), channel_id=1, source_target_pairs={{0,4},{1,5},{2,6},{3,7},{4,0},{5,1},{6,2},{7,3},{8,12},{9,13},{10,... | collective-permute-start | bytes 786440 | tf_op jit(solution)/shard_map/ppermute | solution.py:370
  5.2 12.7 %collective-permute-start.2 = (bf16[1,512,256]{2,1,0:T(8,128)(2,1)}, bf16[1,512,256]{2,1,0:T(8,128)(2,1)S(1)}, u32[]{:S(2)}, u32[]{:S(2)}) collective-permute-start(bf16[1,512,256]{2,1,0:T(8,128)(2,1)} %param.9), channel_id=1, source_target_pairs={{0,6},{1,7},{2,4},{3,5},{4,2},{5,3},{6,0},{7,1},{8,14},{9,15},{10,... | collective-permute-start | bytes 786440 | tf_op jit(solution)/shard_map/ppermute | solution.py:370
  5.3 2.8 %collective-permute-start.4 = (s32[8]{0:T(128)}, s32[8]{0:T(128)S(1)}, u32[]{:S(2)}, u32[]{:S(2)}) collective-permute-start(s32[8]{0:T(128)} %bitcast.28), channel_id=1, source_target_pairs={{0,1},{1,0},{2,3},{3,2},{4,5},{5,4},{6,7},{7,6},{8,9},{9,8},{10,11... | collective-permute-start | bytes 104 | tf_op jit(solution)/shard_map/ppermute | solution.py:370
  8.1 0.5 copy-start.9
  14.4 8.0 %copy-start.4 = (bf16[1,512,256]{2,1,0:T(8,128)(2,1)S(1)}, bf16[1,512,256]{2,1,0:T(8,128)(2,1)}, u32[]{:S(2)}) copy-start(bf16[1,512,256]{2,1,0:T(8,128)(2,1)} %param.9) | copy-start | bytes 786436
  14.4 3.5 %copy-start.5 = (bf16[1,512,256]{2,1,0:T(8,128)(2,1)}, bf16[1,512,256]{2,1,0:T(8,128)(2,1)S(1)}, u32[]{:S(2)}) copy-start(bf16[1,512,256]{2,1,0:T(8,128)(2,1)S(1)} %collective-permute-done) | copy-start | bytes 786436
  17.9 0.7 copy-start.6
  17.9 0.8 copy-start.7
  18.7 41.2 %all-to-all-start = ((bf16[4,2,128,1536]{3,2,1,0:T(8,128)(2,1)}), bf16[4,2,128,1536]{3,2,1,0:T(8,128)(2,1)S(1)}, u32[]{:S(2)}, u32[]{:S(2)}) async-start(bf16[4,2,128,1536]{3,2,1,0:T(8,128)(2,1)} %get-tuple-element.27), calls=%async_computation | async-start | bytes 6291456 | tf_op jit(solution)/shard_map/all_to_all | solution.py:388
  25.4 4.4 %copy-start.1 = (bf16[4,512,256]{2,1,0:T(8,128)(2,1)}, bf16[4,512,256]{2,1,0:T(8,128)(2,1)S(1)}, u32[]{:S(2)}) copy-start(bf16[4,512,256]{2,1,0:T(8,128)(2,1)S(1)} %constant_dynamic-update-slice_fusion.kn_ref.vn_ref) | copy-start | bytes 3145732
  25.4 4.3 %collective-permute-start.3 = (bf16[4,512,256]{2,1,0:T(8,128)(2,1)S(1)}, bf16[4,512,256]{2,1,0:T(8,128)(2,1)S(1)}, u32[]{:S(2)}, u32[]{:S(2)}) collective-permute-start(bf16[4,512,256]{2,1,0:T(8,128)(2,1)S(1)} %constant_dynamic-update-slice_fusion.kn_ref.vn_ref), channel_id=1, source_target_pairs={{0,1},{1,0},{2,3},{3,2},{4,5},{5,4},{6,7},{7,6},{8,9},{9,8},{10,11... | collective-permute-start | bytes 3145736 | tf_op jit(solution)/shard_map/ppermute | solution.py:370
  25.4 48.9 %collective-permute-start.6 = (bf16[2,128,512]{2,1,0:T(8,128)(2,1)}, bf16[2,128,512]{2,1,0:T(8,128)(2,1)S(1)}, u32[]{:S(2)}, u32[]{:S(2)}) collective-permute-start(bf16[2,128,512]{2,1,0:T(8,128)(2,1)} %get-tuple-element.24), channel_id=1, source_target_pairs={{0,2},{1,3},{2,0},{3,1},{4,6},{5,7},{6,4},{7,5},{8,10},{9,11},{10,... | collective-permute-start | bytes 786440 | tf_op jit(solution)/shard_map/ppermute | solution.py:370
  27.5 46.9 %collective-permute-start.7 = (bf16[2,128,512]{2,1,0:T(8,128)(2,1)}, bf16[2,128,512]{2,1,0:T(8,128)(2,1)}, u32[]{:S(2)}, u32[]{:S(2)}) collective-permute-start(bf16[2,128,512]{2,1,0:T(8,128)(2,1)} %get-tuple-element.25), channel_id=1, source_target_pairs={{0,4},{1,5},{2,6},{3,7},{4,0},{5,1},{6,2},{7,3},{8,12},{9,13},{10,... | collective-permute-start | bytes 786440 | tf_op jit(solution)/shard_map/ppermute | solution.py:370
  29.0 45.4 %collective-permute-start.8 = (bf16[2,128,512]{2,1,0:T(8,128)(2,1)}, bf16[2,128,512]{2,1,0:T(8,128)(2,1)}, u32[]{:S(2)}, u32[]{:S(2)}) collective-permute-start(bf16[2,128,512]{2,1,0:T(8,128)(2,1)} %get-tuple-element.26), channel_id=1, source_target_pairs={{0,6},{1,7},{2,4},{3,5},{4,2},{5,3},{6,0},{7,1},{8,14},{9,15},{10,... | collective-permute-start | bytes 786440 | tf_op jit(solution)/shard_map/ppermute | solution.py:370
  29.7 1.0 %copy-start.2 = (bf16[4,512,256]{2,1,0:T(8,128)(2,1)}, bf16[4,512,256]{2,1,0:T(8,128)(2,1)S(1)}, u32[]{:S(2)}) copy-start(bf16[4,512,256]{2,1,0:T(8,128)(2,1)S(1)} %collective-permute-done.3.kf_ref.vf_ref) | copy-start | bytes 3145732
  59.9 1.7 %copy-start = (bf16[4,2,128,1536]{3,2,1,0:T(8,128)(2,1)}, bf16[4,2,128,1536]{3,2,1,0:T(8,128)(2,1)S(1)}, u32[]{:S(2)}) copy-start(bf16[4,2,128,1536]{3,2,1,0:T(8,128)(2,1)S(1)} %all-to-all-done.rest_0_) | copy-start | bytes 9437188
  74.4 0.7 copy-start.3
  78.8 12.1 %all-to-all-start.1 = ((f32[32,1,128]{2,1,0:T(1,128)}), f32[32,1,128]{2,1,0:T(1,128)S(1)}, u32[]{:S(2)}, u32[]{:S(2)}) async-start(f32[32,1,128]{2,1,0:T(1,128)} %bitcast.26), calls=%async_computation.1 | async-start | bytes 32768 | tf_op jit(solution)/shard_map/all_to_all | solution.py:400
  90.9 0.6 copy-start.8

commit v3 on v2

v3 whole, which is shorter than its diff:
```python
import functools
import math

import jax
import jax.numpy as jnp
from jax import lax
from jax.experimental import pallas as pl
from jax.experimental.pallas import tpu as pltpu
from jax.sharding import PartitionSpec as P

HEADS = 64
KVH = 8
HD = 128
GROUPS = HEADS // KVH
SCALE = math.log2(math.e) / math.sqrt(HD)
LOW = -1e30
ROOM = 100.0
PARTS = ((0, 5, False), (5, 3, False))
LAST = 16
EMPTY = 1024.0
NT = (((1,), (1,)), ((), ()))


def lasting(microseconds):
    return pl.CostEstimate(flops=0, bytes_accessed=int(microseconds * 3.5e6), transcendentals=0)


PARAMS = pltpu.CompilerParams(vmem_limit_bytes=62 * 2**20)


def slot_of(judge, routes):
    tile, found = jnp.int32(0), jnp.bool_(False)
    for s in range(routes.shape[0]):
        here = routes[s] == judge
        tile, found = jnp.where(here, s, tile), found | here
    return tile, found


def pack_kernel(chips, parts, me, routes, mate_routes, *rest):
    tiles, outs = rest[: 2 * chips], list(rest[2 * chips :])
    chip, core = me[0] // 2, me[0] % 2
    top = (lax.broadcasted_iota(jnp.int32, (16, HD), 0) == 0) & (pl.program_id(0) == 0)
    for head_from, heads, together in parts:
        width = heads * HD
        for offset in range(chips):
            out = outs[0].at[chip ^ offset] if together else outs.pop(0)
            for n, held in enumerate((routes, mate_routes)):
                tile = tiles[2 * offset + n]
                found = slot_of(2 * (chip ^ offset) + core, held)[1]
                for half in range(2):
                    first = (half * KVH + head_from) * HD
                    out[n, :, half * width : (half + 1) * width] = tile[0, :, first : first + width]
                mark = top & jnp.logical_not(found)
                kept = tile[0, :16, head_from * HD : (head_from + 1) * HD]
                out[n, :16, :HD] = jnp.where(mark, jnp.full_like(kept, EMPTY), kept)
        if together:
            outs.pop(0)


def pack(parts, chips, me, routes, mate_routes, patch, mate_patch):
    tile_rows, width = patch.shape[1:]
    rows = tile_rows // 4
    shapes, specs, sources = [], [], []
    for _, heads, together in parts:
        shape = (2, tile_rows, 2 * heads * HD)
        block = (2, rows, 2 * heads * HD)
        if together:
            shapes.append((chips,) + shape)
            specs.append(pl.BlockSpec((chips,) + block, lambda r, *_: (0, 0, r, 0)))
        else:
            shapes += [shape] * chips
            specs += [pl.BlockSpec(block, lambda r, *_: (0, r, 0))] * chips
    for offset in range(chips):
        for n in range(2):

            def source(r, me, *held, offset=offset, n=n):
                judge = 2 * ((me[0] // 2) ^ offset) + me[0] % 2
                return slot_of(judge, held[n])[0], r, 0

            sources.append(pl.BlockSpec((1, rows, width), source))
    return pl.pallas_call(
        functools.partial(pack_kernel, chips, parts),
        out_shape=[jax.ShapeDtypeStruct(shape, patch.dtype) for shape in shapes],
        grid_spec=pltpu.PrefetchScalarGridSpec(
            num_scalar_prefetch=3,
            grid=(tile_rows // rows,),
            in_specs=sources,
            out_specs=specs,
        ),
        compiler_params=PARAMS,
        cost_estimate=lasting(5),
        name="pack_tiles",
    )(me, routes, mate_routes, *([patch, mate_patch] * chips))


def pipelined(scores, finish):
    held = scores(0)
    for h in range(1, GROUPS):
        following = scores(h)
        finish(held, h - 1)
        held = following
    finish(held, GROUPS - 1)


def fill_text(me, length, head, blocks, sk_ref, sv_ref, kbuf, vbuf):
    prefix_rows, columns = blocks[0].shape
    chip, core = me[0] // 2, me[0] % 2
    live = lax.broadcasted_iota(jnp.int32, (prefix_rows, HD), 0) < length[0]
    for buf, column, ref in ((kbuf, head, sk_ref), (vbuf, KVH + head, sv_ref)):
        owner, within = column // (columns // HD), column % (columns // HD)
        wanted = 2 * ((owner // 2) ^ chip) + ((owner % 2) ^ core)
        span = pl.ds(pl.multiple_of(within * HD, HD), HD)
        for n, block in enumerate(blocks):

            @pl.when(wanted == n)
            def _(buf=buf, block=block, span=span):
                rows = block[:, span]
                other = rows[0:1, :] if buf is kbuf else jnp.zeros_like(rows)
                buf[:prefix_rows, :HD] = jnp.where(live, rows, other)

        buf[prefix_rows:, :HD] = ref[...]

    @pl.when(pl.program_id(0) == 0)
    def _():
        vbuf[:prefix_rows, HD:] = live.astype(vbuf.dtype)
        vbuf[prefix_rows:, HD:] = jnp.ones((sk_ref.shape[0], HD), vbuf.dtype)


def text_kernel(slots, me, length, q_ref, *rest):
    blocks, (sk_ref, sv_ref, o_ref, stat_ref, kv_ref, kbuf, vbuf) = rest[:slots], rest[slots:]
    suffix_rows = sk_ref.shape[0]
    prefix_rows = kbuf.shape[0] - suffix_rows
    fill_text(me, length, pl.program_id(0), blocks, sk_ref, sv_ref, kbuf, vbuf)
    kv_ref[0, :, :HD] = kbuf[...]
    kv_ref[0, :, HD:] = vbuf[:, :HD]
    causal = lax.broadcasted_iota(jnp.int32, (suffix_rows, suffix_rows), 1) <= lax.broadcasted_iota(
        jnp.int32, (suffix_rows, suffix_rows), 0
    )

    def scores(h):
        s = lax.dot_general(
            q_ref[:, h * HD : (h + 1) * HD], kbuf[...], NT, preferred_element_type=jnp.float32
        )
        return jnp.concatenate(
            [s[:, :prefix_rows], jnp.where(causal, s[:, prefix_rows:], LOW)], axis=1
        )

    def finish(s, h):
        peak = jnp.max(s, axis=1, keepdims=True)
        weights = jnp.exp2((s - peak) * SCALE).astype(jnp.bfloat16)
        mixed = jnp.dot(weights, vbuf[...], preferred_element_type=jnp.float32)
        o_ref[:, h * HD : (h + 1) * HD] = mixed[:, :HD]
        stat_ref[:, h : h + 1] = peak
        stat_ref[:, GROUPS + h : GROUPS + h + 1] = mixed[:, HD : HD + 1]

    pipelined(scores, finish)


def attend_text(me, length, queries, prefix, suffix):
    rows = queries.shape[0]
    total, wide = prefix[0].shape[0] + suffix.shape[0], GROUPS * HD
    column = lambda g, *_: (0, g)
    return pl.pallas_call(
        functools.partial(text_kernel, len(prefix)),
        out_shape=[
            jax.ShapeDtypeStruct(queries.shape, jnp.float32),
            jax.ShapeDtypeStruct((rows, KVH * HD), jnp.float32),
            jax.ShapeDtypeStruct((KVH, total, 2 * HD), queries.dtype),
        ],
        grid_spec=pltpu.PrefetchScalarGridSpec(
            num_scalar_prefetch=2,
            grid=(KVH,),
            in_specs=[pl.BlockSpec((rows, wide), column)]
            + [pl.BlockSpec(block.shape, lambda g, *_: (0, 0)) for block in prefix]
            + [
                pl.BlockSpec((suffix.shape[0], HD), column),
                pl.BlockSpec((suffix.shape[0], HD), lambda g, *_: (0, KVH + g)),
            ],
            out_specs=[
                pl.BlockSpec((rows, wide), column),
                pl.BlockSpec((rows, HD), column),
                pl.BlockSpec((1, total, 2 * HD), lambda g, *_: (g, 0, 0)),
            ],
            scratch_shapes=[
                pltpu.VMEM((total, HD), queries.dtype),
                pltpu.VMEM((total, 2 * HD), queries.dtype),
            ],
        ),
        compiler_params=PARAMS,
        cost_estimate=lasting(21),
        name="attend_text",
    )(me, length, queries, *prefix, suffix, suffix)


def tile_at(tiles, n):
    return tiles[0].at[n // 2, n % 2] if len(tiles) == 1 else tiles[n // 2].at[n % 2]


def place_tiles(slots, kept, tiles, place_ref):
    count = jnp.int32(0)
    for n in range(slots):
        found = jnp.max(tile_at(tiles, n)[0:1, :HD].astype(jnp.float32)) < EMPTY
        place_ref[n] = jnp.where(found, count, kept)
        count = count + jnp.where(found, 1, 0)


def fill_image(slots, head, tiles, place_ref, kbuf, vbuf):
    tile_rows, width = tiles[0].shape[-2], tiles[0].shape[-1] // 2
    for n in range(slots):
        row = pl.ds(pl.multiple_of(place_ref[n] * tile_rows, tile_rows), tile_rows)
        tile = tile_at(tiles, n)
        for buf, first in ((kbuf, 0), (vbuf, width)):
            column = first + head * HD
            column = column if isinstance(head, int) else pl.multiple_of(column, HD)
            buf[row, :HD] = tile[:, pl.ds(column, HD)]


def image_kernel(slots, kept, count, last, q_ref, acc_ref, stat_ref, *rest):
    tiles, rest = rest[:count], rest[count:]
    if last:
        length, last_ref, head_ref, text_ref, o_ref, score_ref, kbuf, vbuf, place_ref = rest[:9]
        last_kbuf, last_vbuf, kv_ref, sem = rest[9:]
        head_from, heads, prefix_rows = last
        copy = pltpu.make_async_copy(text_ref.at[pl.ds(head_from, heads)], kv_ref, sem)
    else:
        o_ref, kbuf, vbuf, place_ref = rest[-4:]
    tile_rows = tiles[0].shape[-2]
    total, rows = kept * tile_rows, q_ref.shape[0]
    g = pl.program_id(0)

    @pl.when(g == 0)
    def _():
        vbuf[:, HD:] = jnp.ones((total + tile_rows, HD), vbuf.dtype)
        place_tiles(slots, kept, tiles, place_ref)
        if last:
            copy.start()

    fill_image(slots, g, tiles, place_ref, kbuf, vbuf)

    def scores(column):
        return lax.dot_general(
            q_ref[:, column], kbuf[:total], NT, preferred_element_type=jnp.float32
        )

    def close(summed, totals, column):
        o_ref[:, column] = (summed / totals).astype(o_ref.dtype)

    largest = [jnp.full((8, HD), LOW, jnp.float32)]

    def finish(s, h):
        column = slice(h * HD, (h + 1) * HD)
        held = stat_ref[:, h : h + 1]
        powers = []
        for k in range(total // HD):
            power = (s[:, k * HD : (k + 1) * HD] - held) * SCALE
            largest[0] = jnp.maximum(largest[0], jnp.max(power.reshape(rows // 8, 8, HD), axis=0))
            powers.append(jnp.exp2(power).astype(jnp.bfloat16))
        weights = jnp.concatenate(powers, axis=1)
        mixed = jnp.dot(weights, vbuf[:total], preferred_element_type=jnp.float32)
        totals = mixed[:, HD:] + stat_ref[:, GROUPS + h : GROUPS + h + 1]
        close(mixed[:, :HD] + acc_ref[:, column], totals, column)

    pipelined(lambda h: scores(slice(h * HD, (h + 1) * HD)), finish)

    @pl.when(jnp.logical_not(jnp.max(largest[0]) < ROOM))
    def _():
        @pl.loop(0, GROUPS)
        def _(h):
            column = pl.ds(pl.multiple_of(h * HD, HD), HD)
            s = scores(column)
            lane = lax.broadcasted_iota(jnp.int32, (rows, HD), 1)
            held = jnp.sum(jnp.where(lane == h, stat_ref[...], 0.0), axis=1, keepdims=True)
            sums = jnp.where(lane == GROUPS + h, stat_ref[...], 0.0)
            sums = jnp.sum(sums, axis=1, keepdims=True)
            peak = jnp.maximum(held, jnp.max(s, axis=1, keepdims=True))
            weights = jnp.exp2((s - peak) * SCALE).astype(jnp.bfloat16)
            mixed = jnp.dot(weights, vbuf[:total], preferred_element_type=jnp.float32)
            fade = jnp.exp2((held - peak) * SCALE)
            summed = acc_ref[:, column] * fade + mixed[:, :HD]
            close(summed, sums * fade + mixed[:, HD:], column)

    if last:
        @pl.when(g == heads - 1)
        def _():
            copy.wait()
            score_ref[...] = last_row_gain(
                slots, head_from, heads, prefix_rows, total, length, last_ref, head_ref, kv_ref, tiles,
                place_ref, last_kbuf, last_vbuf,
            )


def attend_image(chips, kept, part, tiles, queries, summed, stats, context=None, last=None):
    head_from, heads, _ = part
    tile_rows = tiles[0].shape[-2]
    total, wide, rows = kept * tile_rows, GROUPS * HD, queries.shape[0]
    column = lambda g: (0, head_from + g)
    specs = [pl.BlockSpec((rows, wide), column)] * 2 + [pl.BlockSpec((rows, HD), column)]
    specs += [pl.BlockSpec(tile.shape, lambda g, d=tile.ndim: (0,) * d) for tile in tiles]
    operands = [queries, summed, stats, *tiles]
    shapes = [jax.ShapeDtypeStruct(queries.shape, queries.dtype)]
    outs = [pl.BlockSpec((rows, wide), column)]
    scratch = [
        pltpu.VMEM((total + tile_rows, HD), queries.dtype),
        pltpu.VMEM((total + tile_rows, 2 * HD), queries.dtype),
        pltpu.SMEM((2 * chips,), jnp.int32),
    ]
    aliases, static = {}, None
    if last is not None:
        length, prefix_rows, head, text_rows = last
        static = (head_from, heads, prefix_rows)
        end = rows // LAST - 1
        operands += [length, queries, head, text_rows]
        specs += [
            pl.BlockSpec(memory_space=pltpu.SMEM),
            pl.BlockSpec((LAST, queries.shape[1]), lambda g: (end, 0)),
            pl.BlockSpec(head.shape, lambda g: (0, 0)),
            pl.BlockSpec(memory_space=pl.ANY),
        ]
        shapes.append(jax.ShapeDtypeStruct((GROUPS, HD), jnp.float32))
        outs.append(pl.BlockSpec((GROUPS, HD), lambda g: (0, 0)))
        scratch += last_scratch(heads, total + tile_rows, queries.dtype) + [
            pltpu.VMEM((heads,) + text_rows.shape[1:], queries.dtype),
            pltpu.SemaphoreType.DMA,
        ]
    if context is not None:
        aliases = {len(operands): 0}
        operands.append(context)
        specs.append(pl.BlockSpec(memory_space=pl.ANY))
    return pl.pallas_call(
        functools.partial(image_kernel, 2 * chips, kept, len(tiles), static),
        out_shape=shapes,
        grid=(heads,),
        in_specs=specs,
        out_specs=outs,
        scratch_shapes=scratch,
        input_output_aliases=aliases,
        compiler_params=PARAMS,
        cost_estimate=lasting(2 * heads),
        name="attend_image",
    )(*operands)


def last_row_gain(slots, head_from, heads, prefix_rows, total, length, q_ref, head_ref, kv_ref, tiles, place_ref, kbuf, vbuf):
    gain = jnp.zeros((GROUPS, HD), jnp.float32)
    column = lax.broadcasted_iota(jnp.int32, (GROUPS, kv_ref.shape[1]), 1)
    live = (column < length[0]) | (column >= prefix_rows)
    for i in range(heads):
        fill_image(slots, i, tiles, place_ref, kbuf.at[i], vbuf.at[i])
    for i in range(heads):
        first = (head_from + i) * GROUPS
        q = [q_ref[:, (first + h) * HD : (first + h + 1) * HD] for h in range(GROUPS)]
        q = jnp.concatenate([part.astype(jnp.float32)[-1:] for part in q], axis=0)
        q = q.astype(jnp.bfloat16)
        s = [
            lax.dot_general(q, keys, NT, preferred_element_type=jnp.float32)
            for keys in (kv_ref[i, :, :HD], kbuf[i, :total])
        ]
        s[0] = jnp.where(live, s[0], LOW)
        peak = jnp.maximum(*[jnp.max(part, axis=1, keepdims=True) for part in s])
        weights = [jnp.exp2((part - peak) * SCALE) for part in s]
        mixed = sum(
            jnp.dot(part.astype(jnp.bfloat16), values, preferred_element_type=jnp.float32)
            for part, values in zip(weights, (kv_ref[i, :, HD:], vbuf[i, :total]))
        )
        totals = sum(jnp.sum(part, axis=1, keepdims=True) for part in weights)
        out = (mixed / totals).astype(jnp.bfloat16).astype(jnp.float32)
        gain = gain + out * head_ref[first : first + GROUPS, :]
    return gain


def last_kernel(slots, kept, count, head_from, heads, prefix_rows, length, q_ref, head_ref, kv_ref, *rest):
    tiles, (before, score_ref, kbuf, vbuf, place_ref) = rest[:count], rest[count:]
    total = kept * tiles[0].shape[-2]
    place_tiles(slots, kept, tiles, place_ref)
    gain = before[...] + last_row_gain(
        slots, head_from, heads, prefix_rows, total, length, q_ref, head_ref, kv_ref, tiles, place_ref,
        kbuf, vbuf,
    )
    score_ref[...] = jnp.broadcast_to(jnp.sum(gain, axis=0, keepdims=True), score_ref.shape)


def last_scratch(heads, rows, dtype):
    return [pltpu.VMEM((heads, rows, HD), dtype)] * 2


def last_rows(chips, kept, part, tiles, queries, length, prefix_rows, head, text_rows, share, devices):
    head_from, heads, _ = part
    tile_rows, text = tiles[0].shape[-2], text_rows.shape[1]
    whole = lambda x: pl.BlockSpec(x.shape, lambda g, d=x.ndim: (0,) * d)
    end = queries.shape[0] // LAST - 1
    specs = [
        pl.BlockSpec(memory_space=pltpu.SMEM),
        pl.BlockSpec((LAST, queries.shape[1]), lambda g: (end, 0)),
        whole(head),
        pl.BlockSpec(
            (pl.Element(heads), pl.Element(text), pl.Element(2 * HD)), lambda g: (head_from, 0, 0)
        ),
    ]
    shape = (devices, HD)
    return pl.pallas_call(
        functools.partial(
            last_kernel, 2 * chips, kept, len(tiles), head_from, heads, prefix_rows
        ),
        out_shape=jax.ShapeDtypeStruct(shape, jnp.float32),
        grid=(1,),
        in_specs=specs + [whole(tile) for tile in tiles] + [whole(share)],
        out_specs=pl.BlockSpec(shape, lambda g: (0, 0)),
        scratch_shapes=last_scratch(heads, (kept + 1) * tile_rows, queries.dtype)
        + [pltpu.SMEM((2 * chips,), jnp.int32)],
        compiler_params=PARAMS,
        cost_estimate=lasting(heads),
        name="last_rows",
    )(length, queries, head, text_rows, *tiles, share)


def normalize_kernel(prompts, slots, every_ref, out_ref):
    own = lax.axis_index("prompt") * slots + lax.axis_index("slot")
    score = jnp.sum(every_ref[...], axis=1, keepdims=True)
    score = jnp.broadcast_to(score, every_ref.shape).reshape(prompts, slots, HD)
    deviation = score - jnp.sum(score, axis=1, keepdims=True) / slots
    spread = jnp.sum(jnp.sum(deviation * deviation, axis=0), axis=0, keepdims=True)
    advantage = deviation / jnp.sqrt(spread / (prompts * slots) + 1e-06)
    advantage = advantage.reshape(prompts * slots, HD)
    row = lax.broadcasted_iota(jnp.int32, advantage.shape, 0)
    out_ref[...] = jnp.sum(jnp.where(row == own, advantage, 0.0), axis=0, keepdims=True)[:, :1]


def per_device(patch_kv, routes, prefix_kv, prefix_len, queries, suffix_kv, score_head):
    slot_count = lax.axis_size("slot")
    prompt_count = lax.axis_size("prompt")
    chips = slot_count // 2
    kept = slot_count // 2
    me = lax.axis_index("slot").astype(jnp.int32).reshape(1)

    def swap(x, k):
        return lax.ppermute(x, "slot", [(i, i ^ k) for i in range(slot_count)])

    mate_patch, mate_routes = swap(patch_kv[0], 1), swap(routes[0], 1)
    near = [prefix_kv[0]] + [swap(prefix_kv[0], 2 * offset) for offset in range(1, chips)]
    buffers = pack(PARTS, chips, me, routes[0], mate_routes, patch_kv[0], mate_patch)
    held = lax.optimization_barrier((near[1:], buffers[0]))[0]
    far = [swap(block, 1) for block in [near[0], *held]]
    first = lax.optimization_barrier((buffers[:chips], near[:-1]))[0]
    prefix = [block for pair in zip(near, far) for block in pair]
    suffix = suffix_kv[0, 0]
    summed, stats, text_rows = attend_text(me, prefix_len, queries[0, 0], prefix, suffix)

    second = lax.optimization_barrier((buffers[chips:], stats))[0]
    arrived = [
        [sent[0]] + [swap(sent[offset], 2 * offset) for offset in range(1, chips)]
        for sent in (first, second)
    ]
    head = score_head.reshape(HEADS, HD)
    last = (prefix_len, prefix_kv.shape[1], head, text_rows)
    main = (queries[0, 0], summed, stats)
    context, share = attend_image(chips, kept, PARTS[0], arrived[0], *main, last=last)
    devices = prompt_count * slot_count
    shares = last_rows(chips, kept, PARTS[1], arrived[1], queries[0, 0], *last, share, devices)
    every = lax.all_to_all(shares, ("prompt", "slot"), 0, 0, tiled=True)
    (context,) = attend_image(chips, kept, PARTS[1], arrived[1], *main, context)
    advantage = pl.pallas_call(
        functools.partial(normalize_kernel, prompt_count, slot_count),
        out_shape=jax.ShapeDtypeStruct((1, 1), jnp.float32),
        in_specs=[pl.BlockSpec(memory_space=pltpu.VMEM)],
        out_specs=pl.BlockSpec(memory_space=pltpu.VMEM),
        cost_estimate=lasting(1),
        name="normalize",
    )(every)
    return (context[None, None], advantage)


def solution(mesh):
    placed = (
        P("prompt", "slot", None, None),
        P("prompt", "slot"),
        P("prompt", None, "slot"),
        P("prompt"),
        P("prompt", "slot", None, None),
        P("prompt", "slot", None, None),
        P(),
    )
    return jax.shard_map(
        per_device,
        mesh=mesh,
        in_specs=placed,
        out_specs=(P("prompt", "slot", None, None), P("prompt", "slot")),
        check_vma=False,
    )
```

time: 93.5 us -> 87.4 us (0.935)
  waiting for transfers between devices: 13.1 us -> 7.05 us
  local copies, waits for them, and re-layouts: 7.97 us -> 3.83 us
  starting transfers between devices: 16.9 us -> 20 us
  Pallas kernels: 53.4 us -> 54.6 us
    ppermute x9 -> x15, starting transfers between devices: 8.29 us -> 14.8 us  [swap(): return lax.ppermute(x, 'slot', [(i, i ^ k) for i in range(slot_count)])]
    all_to_all x1 -> x0, waiting for transfers between devices: 5.32 us -> none  [per_device(): lax.all_to_all(sent[0], 'slot', 0, 0, tiled=True, axis_index_groups=groups)]
    all_to_all x1 -> x0, starting transfers between devices: 3.7 us -> none  [per_device(): lax.all_to_all(sent[0], 'slot', 0, 0, tiled=True, axis_index_groups=groups)]
    unnamed x23 -> x28, local copies, waits for them, and re-layouts: 7 us -> 3.83 us
    all_to_all x1, waiting for transfers between devices: 1.31 us -> 0.01 us  [per_device(): every = lax.all_to_all(shares, ('prompt', 'slot'), 0, 0, tiled=True)]
    pallas_call x4, Pallas kernels: 46.2 us -> 47.3 us  [the longest x1 22.8 us: attend_text(): pl.pallas_call(functools.partial(text_kernel, len(prefix)), out_shape=[ja...]
    concatenate x1 -> x0, local copies, waits for them, and re-layouts: 0.97 us -> none  [per_device(): near = jnp.concatenate(near, axis=0)]
    ppermute x9 -> x15, waiting for transfers between devices: 6.49 us -> 7.05 us  [swap(): return lax.ppermute(x, 'slot', [(i, i ^ k) for i in range(slot_count)])]
  transfers between devices with their start and end apart: 11 -> 16, of which waited for: 5 -> 5; matrix products, arithmetic and copies ran while one was open for 3% -> 0% of each run, Pallas kernels for 52% -> 57%
where the time goes in v3:
time: 87.4 us; the launch traced here: 86.9 us
  Pallas kernels  54.6 us (62%)
  starting transfers between devices  20 us (23%)
  waiting for transfers between devices  7.05 us (8%)
  local copies, waits for them, and re-layouts  3.83 us (4%)
  between operations  1.42 us (2%)
    pallas_call x1, Pallas kernels, attend_text(): pl.pallas_call(functools.partial(text_kernel, len(prefix)), out_shape=[ja...  22.8 us
    pallas_call x2, Pallas kernels, attend_image(): pl.pallas_call(functools.partial(image_kernel, 2 * chips, kept, len(tiles...  20.8 us
    ppermute x15, starting transfers between devices, swap(): return lax.ppermute(x, 'slot', [(i, i ^ k) for i in range(slot_count)])  14.8 us
    ppermute x15, waiting for transfers between devices, swap(): return lax.ppermute(x, 'slot', [(i, i ^ k) for i in range(slot_count)])  7.05 us
    pallas_call x1, Pallas kernels, pack(): pl.pallas_call(functools.partial(pack_kernel, chips, parts), out_shape=[j...  5.9 us
    all_to_all x1, starting transfers between devices, per_device(): every = lax.all_to_all(shares, ('prompt', 'slot'), 0, 0, tiled=True)  5.21 us
    unnamed x28, local copies, waits for them, and re-layouts  3.83 us
    pallas_call x1, Pallas kernels, last_rows(): pl.pallas_call(functools.partial(last_kernel, 2 * chips, kept, len(tiles)...  3.75 us
  transfers between devices with their start and end apart: 16, of which 5 were waited for; matrix products, arithmetic and copies ran while one was open for 0% of the time, Pallas kernels for 57%

profile of v3, /device:TPU:0, one launch (start us, length us, event | category | flops | bytes accessed | tf_op | source)
XLA Modules:
  0.0 86.9 jit_solution(12203923933367168061)
XLA Ops:
  0.6 0.5 collective-permute-start.5
  1.1 2.6 %collective-permute-start.2 = (bf16[512,256]{1,0:T(8,128)(2,1)}, bf16[512,256]{1,0:T(8,128)(2,1)S(1)}, u32[]{:S(2)}, u32[]{:S(2)}) collective-permute-start(bf16[512,256]{1,0:T(8,128)(2,1)} %bitcast.25), channel_id=1, source_target_pairs={{0,4},{1,5},{2,6},{3,7},{4,0},{5,1},{6,2},{7,3},{8,12},{9,13},{10,... | collective-permute-start | bytes 786440 | tf_op jit(solution)/shard_map/ppermute | solution.py:436
  3.7 1.5 %collective-permute-start.1 = (bf16[512,256]{1,0:T(8,128)(2,1)}, bf16[512,256]{1,0:T(8,128)(2,1)S(1)}, u32[]{:S(2)}, u32[]{:S(2)}) collective-permute-start(bf16[512,256]{1,0:T(8,128)(2,1)} %bitcast.26), channel_id=1, source_target_pairs={{0,2},{1,3},{2,0},{3,1},{4,6},{5,7},{6,4},{7,5},{8,10},{9,11},{10,... | collective-permute-start | bytes 786440 | tf_op jit(solution)/shard_map/ppermute | solution.py:436
  5.3 2.8 %collective-permute-done.4.mate_routes = s32[8]{0:T(128)S(1)} collective-permute-done((s32[8]{0:T(128)}, s32[8]{0:T(128)S(1)}, u32[]{:S(2)}, u32[]{:S(2)}) %collective-permute-start.4) | collective-permute-done | bytes 64 | tf_op jit(solution)/shard_map/ppermute | solution.py:436
  8.6 5.9 %pack_tiles.1 = (bf16[2,128,1280]{2,1,0:T(8,128)(2,1)}, bf16[2,128,1280]{2,1,0:T(8,128)(2,1)}, bf16[2,128,1280]{2,1,0:T(8,128)(2,1)}, bf16[2,128,1280]{2,1,0:T(8...) custom-call(s32[1]{0:T(128)} %bitcast.1.me, ...), custom_call_target="tpu_custom_call" | custom-call | bytes 17500000 | tf_op jit(solution)/shard_map/pack_tiles/pallas_call | solution.py:81
  14.6 3.0 %collective-permute-start.12 = (bf16[2,128,1280]{2,1,0:T(8,128)(2,1)}, bf16[2,128,1280]{2,1,0:T(8,128)(2,1)S(1)}, u32[]{:S(2)}, u32[]{:S(2)}) collective-permute-start(bf16[2,128,1280]{2,1,0:T(8,128)(2,1)} %get-tuple-element.44), channel_id=1, source_target_pairs={{0,2},{1,3},{2,0},{3,1},{4,6},{5,7},{6,4},{7,5},{8,10},{9,11},{10,... | collective-permute-start | bytes 1966088 | tf_op jit(solution)/shard_map/ppermute | solution.py:436
  18.6 0.5 collective-permute-done.rest_1_
  19.1 1.4 %collective-permute-start.13 = (bf16[2,128,1280]{2,1,0:T(8,128)(2,1)}, bf16[2,128,1280]{2,1,0:T(8,128)(2,1)}, u32[]{:S(2)}, u32[]{:S(2)}) collective-permute-start(bf16[2,128,1280]{2,1,0:T(8,128)(2,1)} %get-tuple-element.45), channel_id=1, source_target_pairs={{0,4},{1,5},{2,6},{3,7},{4,0},{5,1},{6,2},{7,3},{8,12},{9,13},{10,... | collective-permute-start | bytes 1966088 | tf_op jit(solution)/shard_map/ppermute | solution.py:436
  20.5 0.7 copy-done.9
  21.2 1.4 %collective-permute-start.14 = (bf16[2,128,1280]{2,1,0:T(8,128)(2,1)}, bf16[2,128,1280]{2,1,0:T(8,128)(2,1)}, u32[]{:S(2)}, u32[]{:S(2)}) collective-permute-start(bf16[2,128,1280]{2,1,0:T(8,128)(2,1)} %get-tuple-element.46), channel_id=1, source_target_pairs={{0,6},{1,7},{2,4},{3,5},{4,2},{5,3},{6,0},{7,1},{8,14},{9,15},{10,... | collective-permute-start | bytes 1966088 | tf_op jit(solution)/shard_map/ppermute | solution.py:436
  23.3 0.7 copy-done.10
  23.9 0.7 copy-done.11
  24.6 22.8 %attend_text.1 = (f32[256,8192]{1,0:T(8,128)}, f32[256,1024]{1,0:T(8,128)}, bf16[8,768,256]{2,1,0:T(8,128)(2,1)}) custom-call(s32[1]{0:T(128)} %bitcast.1.me, s32[1]{0:T(128)S(6)} %copy.12.length.rest_4_, bf16[256,8192]{1,0:T(8,128)(2,1)} %bitcast.12, bf16[512,256]{1,0:T(8,128)(2,1)} %bitcast.28, bf16[512,256]{1,0:T(8,128)(2,1)} %copy-done.8, ...), custom_call_target="tpu_custom_call" | custom-call | bytes 73500000 | tf_op jit(solution)/shard_map/attend_text/pallas_call | solution.py:163
  47.4 0.8 collective-permute-start.9
  48.2 1.3 %collective-permute-start.10 = (bf16[2,128,768]{2,1,0:T(8,128)(2,1)}, bf16[2,128,768]{2,1,0:T(8,128)(2,1)S(1)}, u32[]{:S(2)}, u32[]{:S(2)}) collective-permute-start(bf16[2,128,768]{2,1,0:T(8,128)(2,1)} %get-tuple-element.38), channel_id=1, source_target_pairs={{0,4},{1,5},{2,6},{3,7},{4,0},{5,1},{6,2},{7,3},{8,12},{9,13},{10,... | collective-permute-start | bytes 1179656 | tf_op jit(solution)/shard_map/ppermute | solution.py:436
  49.6 1.4 %collective-permute-start.11 = (bf16[2,128,768]{2,1,0:T(8,128)(2,1)}, bf16[2,128,768]{2,1,0:T(8,128)(2,1)S(1)}, u32[]{:S(2)}, u32[]{:S(2)}) collective-permute-start(bf16[2,128,768]{2,1,0:T(8,128)(2,1)} %get-tuple-element.39), channel_id=1, source_target_pairs={{0,6},{1,7},{2,4},{3,5},{4,2},{5,3},{6,0},{7,1},{8,14},{9,15},{10,... | collective-permute-start | bytes 1179656 | tf_op jit(solution)/shard_map/ppermute | solution.py:436
  50.9 13.1 %attend_image.2 = (bf16[256,8192]{1,0:T(8,128)(2,1)}, f32[8,128]{1,0:T(8,128)}) custom-call(bf16[256,8192]{1,0:T(8,128)(2,1)} %bitcast.13, f32[256,8192]{1,0:T(8,128)} %get-tuple-element.30.acc_ref, f32[256,1024]{1,0:T(8,128)} %get-tuple-element.31.stat_ref, bf16[2,128,1280]{2,1,0:T(8,128)(2,1)} %get-tuple-element.43.rest_0_, ...), custom_call_target="tpu_custom_call" | custom-call | bytes 35000000 | tf_op jit(solution)/shard_map/attend_image/pallas_call | solution.py:329
  64.1 3.4 %collective-permute-done.11.rest_3_ = bf16[2,128,768]{2,1,0:T(8,128)(2,1)S(1)} collective-permute-done((bf16[2,128,768]{2,1,0:T(8,128)(2,1)}, bf16[2,128,768]{2,1,0:T(8,128)(2,1)S(1)}, u32[]{:S(2)}, u32[]{:S(2)}) %collective-permute-start.11) | collective-permute-done | bytes 393248 | tf_op jit(solution)/shard_map/ppermute | solution.py:436
  67.6 0.8 copy-done.2
  68.3 3.8 %last_rows.1 = f32[32,128]{1,0:T(8,128)} custom-call(s32[1]{0:T(128)S(6)} %copy.12.length.rest_4_, bf16[256,8192]{1,0:T(8,128)(2,1)} %bitcast.15, f32[64,128]{1,0:T(8,128)} %bitcast.31, bf16[8,768,256]{2,1,0:T(8,128)(2,1)} %get-tuple-element.47.rest_7_.kv_ref, bf16[2,128,768]{2,1,0:T(8,128)(2,1)} %get-tuple-element.36.rest_0_, bf16[2,128,768]{2,1,0:T(8,128)(2,1)} %copy-done, ...), custom_call_target="tpu_custom_call" | custom-call | bytes 10500000 | tf_op jit(solution)/shard_map/last_rows/pallas_call | solution.py:400
  72.1 5.2 %all-to-all-start = ((f32[32,1,128]{2,1,0:T(1,128)}), f32[32,1,128]{2,1,0:T(1,128)S(1)}, u32[]{:S(2)}, u32[]{:S(2)}) async-start(f32[32,1,128]{2,1,0:T(1,128)} %bitcast.32), calls=%async_computation | async-start | bytes 32768 | tf_op jit(solution)/shard_map/all_to_all | solution.py:459
  77.3 7.6 %attend_image.3 = bf16[256,8192]{1,0:T(8,128)(2,1)} custom-call(bf16[256,8192]{1,0:T(8,128)(2,1)} %bitcast.16, f32[256,8192]{1,0:T(8,128)} %get-tuple-element.30.acc_ref, f32[256,1024]{1,0:T(8,128)} %get-tuple-element.31.stat_ref, bf16[2,128,768]{2,1,0:T(8,128)(2,1)} %get-tuple-element.36.rest_0_, ...), custom_call_target="tpu_custom_call", output_to_operand_aliasing={{}: (7, {})} | custom-call | bytes 21000000 | tf_op jit(solution)/shard_map/attend_image/pallas_call | solution.py:329
  84.9 0.6 copy-done.12
  85.5 1.4 %normalize.1 = f32[1,1]{1,0:T(1,128)} custom-call(f32[32,128]{1,0:T(8,128)} %bitcast.33), custom_call_target="tpu_custom_call" | custom-call | bytes 3500000 | tf_op jit(solution)/shard_map/normalize/pallas_call | solution.py:461
  (42 shorter events, 1.7 us)
Async XLA Ops:
  0.6 7.6 %collective-permute-start.5 = (bf16[8,128,2048]{2,1,0:T(8,128)(2,1)}, bf16[8,128,2048]{2,1,0:T(8,128)(2,1)}, u32[]{:S(2)}, u32[]{:S(2)}) collective-permute-start(bf16[8,128,2048]{2,1,0:T(8,128)(2,1)} %bitcast.17), channel_id=1, source_target_pairs={{0,1},{1,0},{2,3},{3,2},{4,5},{5,4},{6,7},{7,6},{8,9},{9,8},{10,11... | collective-permute-start | bytes 12582920 | tf_op jit(solution)/shard_map/ppermute | solution.py:436
  1.1 13.4 %collective-permute-start.2 = (bf16[512,256]{1,0:T(8,128)(2,1)}, bf16[512,256]{1,0:T(8,128)(2,1)S(1)}, u32[]{:S(2)}, u32[]{:S(2)}) collective-permute-start(bf16[512,256]{1,0:T(8,128)(2,1)} %bitcast.25), channel_id=1, source_target_pairs={{0,4},{1,5},{2,6},{3,7},{4,0},{5,1},{6,2},{7,3},{8,12},{9,13},{10,... | collective-permute-start | bytes 786440 | tf_op jit(solution)/shard_map/ppermute | solution.py:436
  3.7 10.8 %collective-permute-start.1 = (bf16[512,256]{1,0:T(8,128)(2,1)}, bf16[512,256]{1,0:T(8,128)(2,1)S(1)}, u32[]{:S(2)}, u32[]{:S(2)}) collective-permute-start(bf16[512,256]{1,0:T(8,128)(2,1)} %bitcast.26), channel_id=1, source_target_pairs={{0,2},{1,3},{2,0},{3,1},{4,6},{5,7},{6,4},{7,5},{8,10},{9,11},{10,... | collective-permute-start | bytes 786440 | tf_op jit(solution)/shard_map/ppermute | solution.py:436
  5.2 12.4 %collective-permute-start.3 = (bf16[512,256]{1,0:T(8,128)(2,1)}, bf16[512,256]{1,0:T(8,128)(2,1)S(1)}, u32[]{:S(2)}, u32[]{:S(2)}) collective-permute-start(bf16[512,256]{1,0:T(8,128)(2,1)} %bitcast.27), channel_id=1, source_target_pairs={{0,6},{1,7},{2,4},{3,5},{4,2},{5,3},{6,0},{7,1},{8,14},{9,15},{10,... | collective-permute-start | bytes 786440 | tf_op jit(solution)/shard_map/ppermute | solution.py:436
  5.3 2.8 %collective-permute-start.4 = (s32[8]{0:T(128)}, s32[8]{0:T(128)S(1)}, u32[]{:S(2)}, u32[]{:S(2)}) collective-permute-start(s32[8]{0:T(128)} %bitcast.34), channel_id=1, source_target_pairs={{0,1},{1,0},{2,3},{3,2},{4,5},{5,4},{6,7},{7,6},{8,9},{9,8},{10,11... | collective-permute-start | bytes 104 | tf_op jit(solution)/shard_map/ppermute | solution.py:436
  8.6 8.9 %copy-start.4 = (bf16[1,512,256]{2,1,0:T(8,128)(2,1)S(1)}, bf16[1,512,256]{2,1,0:T(8,128)(2,1)}, u32[]{:S(2)}) copy-start(bf16[1,512,256]{2,1,0:T(8,128)(2,1)} %param.9) | copy-start | bytes 786436
  14.5 10.1 %copy-start.5 = (bf16[512,256]{1,0:T(8,128)(2,1)}, bf16[512,256]{1,0:T(8,128)(2,1)S(1)}, u32[]{:S(2)}) copy-start(bf16[512,256]{1,0:T(8,128)(2,1)S(1)} %collective-permute-done.2.rest_4_) | copy-start | bytes 786436
  14.6 10.1 %copy-start.6 = (bf16[512,256]{1,0:T(8,128)(2,1)}, bf16[512,256]{1,0:T(8,128)(2,1)S(1)}, u32[]{:S(2)}) copy-start(bf16[512,256]{1,0:T(8,128)(2,1)S(1)} %collective-permute-done.1.rest_2_) | copy-start | bytes 786436
  14.6 35.0 %collective-permute-start.12 = (bf16[2,128,1280]{2,1,0:T(8,128)(2,1)}, bf16[2,128,1280]{2,1,0:T(8,128)(2,1)S(1)}, u32[]{:S(2)}, u32[]{:S(2)}) collective-permute-start(bf16[2,128,1280]{2,1,0:T(8,128)(2,1)} %get-tuple-element.44), channel_id=1, source_target_pairs={{0,2},{1,3},{2,0},{3,1},{4,6},{5,7},{6,4},{7,5},{8,10},{9,11},{10,... | collective-permute-start | bytes 1966088 | tf_op jit(solution)/shard_map/ppermute | solution.py:436
  17.6 1.5 %collective-permute-start = (bf16[512,256]{1,0:T(8,128)(2,1)S(1)}, bf16[512,256]{1,0:T(8,128)(2,1)S(1)}, u32[]{:S(2)}, u32[]{:S(2)}) collective-permute-start(bf16[512,256]{1,0:T(8,128)(2,1)S(1)} %bitcast.29), channel_id=1, source_target_pairs={{0,1},{1,0},{2,3},{3,2},{4,5},{5,4},{6,7},{7,6},{8,9},{9,8},{10,11... | collective-permute-start | bytes 786440 | tf_op jit(solution)/shard_map/ppermute | solution.py:436
  17.7 7.0 %copy-start.7 = (bf16[512,256]{1,0:T(8,128)(2,1)}, bf16[512,256]{1,0:T(8,128)(2,1)S(1)}, u32[]{:S(2)}) copy-start(bf16[512,256]{1,0:T(8,128)(2,1)S(1)} %collective-permute-done.3.rest_6_) | copy-start | bytes 786436
  17.7 2.8 %collective-permute-start.6 = (bf16[512,256]{1,0:T(8,128)(2,1)S(1)}, bf16[512,256]{1,0:T(8,128)(2,1)S(1)}, u32[]{:S(2)}, u32[]{:S(2)}) collective-permute-start(bf16[512,256]{1,0:T(8,128)(2,1)S(1)} %collective-permute-done.1.rest_2_), channel_id=1, source_target_pairs={{0,1},{1,0},{2,3},{3,2},{4,5},{5,4},{6,7},{7,6},{8,9},{9,8},{10,11... | collective-permute-start | bytes 786440 | tf_op jit(solution)/shard_map/ppermute | solution.py:436
  18.1 5.1 %collective-permute-start.7 = (bf16[512,256]{1,0:T(8,128)(2,1)S(1)}, bf16[512,256]{1,0:T(8,128)(2,1)S(1)}, u32[]{:S(2)}, u32[]{:S(2)}) collective-permute-start(bf16[512,256]{1,0:T(8,128)(2,1)S(1)} %collective-permute-done.2.rest_4_), channel_id=1, source_target_pairs={{0,1},{1,0},{2,3},{3,2},{4,5},{5,4},{6,7},{7,6},{8,9},{9,8},{10,11... | collective-permute-start | bytes 786440 | tf_op jit(solution)/shard_map/ppermute | solution.py:436
  18.2 5.1 %collective-permute-start.8 = (bf16[512,256]{1,0:T(8,128)(2,1)S(1)}, bf16[512,256]{1,0:T(8,128)(2,1)S(1)}, u32[]{:S(2)}, u32[]{:S(2)}) collective-permute-start(bf16[512,256]{1,0:T(8,128)(2,1)S(1)} %collective-permute-done.3.rest_6_), channel_id=1, source_target_pairs={{0,1},{1,0},{2,3},{3,2},{4,5},{5,4},{6,7},{7,6},{8,9},{9,8},{10,11... | collective-permute-start | bytes 786440 | tf_op jit(solution)/shard_map/ppermute | solution.py:436
  19.1 1.4 %copy-start.8 = (bf16[512,256]{1,0:T(8,128)(2,1)}, bf16[512,256]{1,0:T(8,128)(2,1)S(1)}, u32[]{:S(2)}) copy-start(bf16[512,256]{1,0:T(8,128)(2,1)S(1)} %collective-permute-done.rest_1_) | copy-start | bytes 786436
  19.1 31.8 %collective-permute-start.13 = (bf16[2,128,1280]{2,1,0:T(8,128)(2,1)}, bf16[2,128,1280]{2,1,0:T(8,128)(2,1)}, u32[]{:S(2)}, u32[]{:S(2)}) collective-permute-start(bf16[2,128,1280]{2,1,0:T(8,128)(2,1)} %get-tuple-element.45), channel_id=1, source_target_pairs={{0,4},{1,5},{2,6},{3,7},{4,0},{5,1},{6,2},{7,3},{8,12},{9,13},{10,... | collective-permute-start | bytes 1966088 | tf_op jit(solution)/shard_map/ppermute | solution.py:436
  21.2 29.8 %collective-permute-start.14 = (bf16[2,128,1280]{2,1,0:T(8,128)(2,1)}, bf16[2,128,1280]{2,1,0:T(8,128)(2,1)}, u32[]{:S(2)}, u32[]{:S(2)}) collective-permute-start(bf16[2,128,1280]{2,1,0:T(8,128)(2,1)} %get-tuple-element.46), channel_id=1, source_target_pairs={{0,6},{1,7},{2,4},{3,5},{4,2},{5,3},{6,0},{7,1},{8,14},{9,15},{10,... | collective-permute-start | bytes 1966088 | tf_op jit(solution)/shard_map/ppermute | solution.py:436
  47.4 16.6 %collective-permute-start.9 = (bf16[2,128,768]{2,1,0:T(8,128)(2,1)}, bf16[2,128,768]{2,1,0:T(8,128)(2,1)S(1)}, u32[]{:S(2)}, u32[]{:S(2)}) collective-permute-start(bf16[2,128,768]{2,1,0:T(8,128)(2,1)} %get-tuple-element.37), channel_id=1, source_target_pairs={{0,2},{1,3},{2,0},{3,1},{4,6},{5,7},{6,4},{7,5},{8,10},{9,11},{10,... | collective-permute-start | bytes 1179656 | tf_op jit(solution)/shard_map/ppermute | solution.py:436
  48.2 15.9 %collective-permute-start.10 = (bf16[2,128,768]{2,1,0:T(8,128)(2,1)}, bf16[2,128,768]{2,1,0:T(8,128)(2,1)S(1)}, u32[]{:S(2)}, u32[]{:S(2)}) collective-permute-start(bf16[2,128,768]{2,1,0:T(8,128)(2,1)} %get-tuple-element.38), channel_id=1, source_target_pairs={{0,4},{1,5},{2,6},{3,7},{4,0},{5,1},{6,2},{7,3},{8,12},{9,13},{10,... | collective-permute-start | bytes 1179656 | tf_op jit(solution)/shard_map/ppermute | solution.py:436
  49.5 1.4 %copy-start.3 = (bf16[2,128,1280]{2,1,0:T(8,128)(2,1)}, bf16[2,128,1280]{2,1,0:T(8,128)(2,1)S(1)}, u32[]{:S(2)}) copy-start(bf16[2,128,1280]{2,1,0:T(8,128)(2,1)S(1)} %collective-permute-done.12.rest_1_) | copy-start | bytes 1966084
  49.6 18.0 %collective-permute-start.11 = (bf16[2,128,768]{2,1,0:T(8,128)(2,1)}, bf16[2,128,768]{2,1,0:T(8,128)(2,1)S(1)}, u32[]{:S(2)}, u32[]{:S(2)}) collective-permute-start(bf16[2,128,768]{2,1,0:T(8,128)(2,1)} %get-tuple-element.39), channel_id=1, source_target_pairs={{0,6},{1,7},{2,4},{3,5},{4,2},{5,3},{6,0},{7,1},{8,14},{9,15},{10,... | collective-permute-start | bytes 1179656 | tf_op jit(solution)/shard_map/ppermute | solution.py:436
  64.1 3.5 %copy-start = (bf16[2,128,768]{2,1,0:T(8,128)(2,1)}, bf16[2,128,768]{2,1,0:T(8,128)(2,1)S(1)}, u32[]{:S(2)}) copy-start(bf16[2,128,768]{2,1,0:T(8,128)(2,1)S(1)} %collective-permute-done.9.rest_1_) | copy-start | bytes 1179652
  64.1 3.4 %copy-start.1 = (bf16[2,128,768]{2,1,0:T(8,128)(2,1)}, bf16[2,128,768]{2,1,0:T(8,128)(2,1)S(1)}, u32[]{:S(2)}) copy-start(bf16[2,128,768]{2,1,0:T(8,128)(2,1)S(1)} %collective-permute-done.10.rest_2_) | copy-start | bytes 1179652
  72.1 12.9 %all-to-all-start = ((f32[32,1,128]{2,1,0:T(1,128)}), f32[32,1,128]{2,1,0:T(1,128)S(1)}, u32[]{:S(2)}, u32[]{:S(2)}) async-start(f32[32,1,128]{2,1,0:T(1,128)} %bitcast.32), calls=%async_computation | async-start | bytes 32768 | tf_op jit(solution)/shard_map/all_to_all | solution.py:459
  (6 other events, 4.0 us)

commit v4 on v3

--- a/solution.py
+++ b/solution.py
@@ -14,7 +14,7 @@
 GROUPS = HEADS // KVH
 SCALE = math.log2(math.e) / math.sqrt(HD)
 LOW = -1e30
-ROOM = 100.0
+ROOM = 2.0**100
 PARTS = ((0, 5, False), (5, 3, False))
 LAST = 16
 EMPTY = 1024.0
@@ -25,7 +25,7 @@
     return pl.CostEstimate(flops=0, bytes_accessed=int(microseconds * 3.5e6), transcendentals=0)
 
 
-PARAMS = pltpu.CompilerParams(vmem_limit_bytes=62 * 2**20)
+PARAMS = pltpu.CompilerParams(vmem_limit_bytes=64 * 2**20)
 
 
 def slot_of(judge, routes):
@@ -102,40 +102,38 @@
     finish(held, GROUPS - 1)
 
 
-def fill_text(me, length, head, blocks, sk_ref, sv_ref, kbuf, vbuf):
+def fill_text(me, length, head, blocks, sk_ref, sv_ref, held, kbuf, vbuf):
     prefix_rows, columns = blocks[0].shape
-    chip, core = me[0] // 2, me[0] % 2
     live = lax.broadcasted_iota(jnp.int32, (prefix_rows, HD), 0) < length[0]
+
+    @pl.when(pl.program_id(0) == 0)
+    def _():
+        chip, core = me[0] // 2, me[0] % 2
+        for n, block in enumerate(blocks):
+            held[2 * (chip ^ (n // 2)) + (core ^ (n % 2))] = block[...]
+        vbuf[:prefix_rows, HD:] = live.astype(vbuf.dtype)
+        vbuf[prefix_rows:, HD:] = jnp.ones((sk_ref.shape[0], HD), vbuf.dtype)
+
     for buf, column, ref in ((kbuf, head, sk_ref), (vbuf, KVH + head, sv_ref)):
         owner, within = column // (columns // HD), column % (columns // HD)
-        wanted = 2 * ((owner // 2) ^ chip) + ((owner % 2) ^ core)
-        span = pl.ds(pl.multiple_of(within * HD, HD), HD)
-        for n, block in enumerate(blocks):
-
-            @pl.when(wanted == n)
-            def _(buf=buf, block=block, span=span):
-                rows = block[:, span]
-                other = rows[0:1, :] if buf is kbuf else jnp.zeros_like(rows)
-                buf[:prefix_rows, :HD] = jnp.where(live, rows, other)
-
+        rows = held[owner, :, pl.ds(pl.multiple_of(within * HD, HD), HD)]
+        other = rows[0:1, :] if buf is kbuf else jnp.zeros_like(rows)
+        buf[:prefix_rows, :HD] = jnp.where(live, rows, other)
         buf[prefix_rows:, :HD] = ref[...]
 
-    @pl.when(pl.program_id(0) == 0)
-    def _():
-        vbuf[:prefix_rows, HD:] = live.astype(vbuf.dtype)
-        vbuf[prefix_rows:, HD:] = jnp.ones((sk_ref.shape[0], HD), vbuf.dtype)
-
 
 def text_kernel(slots, me, length, q_ref, *rest):
-    blocks, (sk_ref, sv_ref, o_ref, stat_ref, kv_ref, kbuf, vbuf) = rest[:slots], rest[slots:]
+    blocks, (sk_ref, sv_ref, o_ref, stat_ref, kv_ref, held, kbuf, vbuf) = rest[:slots], rest[slots:]
     suffix_rows = sk_ref.shape[0]
     prefix_rows = kbuf.shape[0] - suffix_rows
-    fill_text(me, length, pl.program_id(0), blocks, sk_ref, sv_ref, kbuf, vbuf)
+    fill_text(me, length, pl.program_id(0), blocks, sk_ref, sv_ref, held, kbuf, vbuf)
     kv_ref[0, :, :HD] = kbuf[...]
     kv_ref[0, :, HD:] = vbuf[:, :HD]
     causal = lax.broadcasted_iota(jnp.int32, (suffix_rows, suffix_rows), 1) <= lax.broadcasted_iota(
         jnp.int32, (suffix_rows, suffix_rows), 0
     )
+
+    lane = lax.broadcasted_iota(jnp.int32, (suffix_rows, HD), 1)
 
     def scores(h):
         s = lax.dot_general(
@@ -150,8 +148,8 @@
         weights = jnp.exp2((s - peak) * SCALE).astype(jnp.bfloat16)
         mixed = jnp.dot(weights, vbuf[...], preferred_element_type=jnp.float32)
         o_ref[:, h * HD : (h + 1) * HD] = mixed[:, :HD]
-        stat_ref[:, h : h + 1] = peak
-        stat_ref[:, GROUPS + h : GROUPS + h + 1] = mixed[:, HD : HD + 1]
+        held = jnp.where(lane == GROUPS + h, mixed[:, HD:], stat_ref[...])
+        stat_ref[...] = jnp.where(lane == h, peak, held)
 
     pipelined(scores, finish)
 
@@ -182,6 +180,7 @@
                 pl.BlockSpec((1, total, 2 * HD), lambda g, *_: (g, 0, 0)),
             ],
             scratch_shapes=[
+                pltpu.VMEM((len(prefix),) + prefix[0].shape, queries.dtype),
                 pltpu.VMEM((total, HD), queries.dtype),
                 pltpu.VMEM((total, 2 * HD), queries.dtype),
             ],
@@ -245,7 +244,7 @@
     def close(summed, totals, column):
         o_ref[:, column] = (summed / totals).astype(o_ref.dtype)
 
-    largest = [jnp.full((8, HD), LOW, jnp.float32)]
+    largest = [jnp.zeros((8, HD), jnp.float32)]
 
     def finish(s, h):
         column = slice(h * HD, (h + 1) * HD)
@@ -253,11 +252,11 @@
         powers = []
         for k in range(total // HD):
             power = (s[:, k * HD : (k + 1) * HD] - held) * SCALE
-            largest[0] = jnp.maximum(largest[0], jnp.max(power.reshape(rows // 8, 8, HD), axis=0))
             powers.append(jnp.exp2(power).astype(jnp.bfloat16))
         weights = jnp.concatenate(powers, axis=1)
         mixed = jnp.dot(weights, vbuf[:total], preferred_element_type=jnp.float32)
         totals = mixed[:, HD:] + stat_ref[:, GROUPS + h : GROUPS + h + 1]
+        largest[0] = jnp.maximum(largest[0], jnp.max(totals.reshape(rows // 8, 8, HD), axis=0))
         close(mixed[:, :HD] + acc_ref[:, column], totals, column)
 
     pipelined(lambda h: scores(slice(h * HD, (h + 1) * HD)), finish)
@@ -440,12 +439,14 @@
     buffers = pack(PARTS, chips, me, routes[0], mate_routes, patch_kv[0], mate_patch)
     held = lax.optimization_barrier((near[1:], buffers[0]))[0]
     far = [swap(block, 1) for block in [near[0], *held]]
-    first = lax.optimization_barrier((buffers[:chips], near[:-1]))[0]
+    first, second = list(buffers[:chips]), list(buffers[chips:])
+    for n in range(1, chips):
+        first[n] = lax.optimization_barrier((first[n], near[:-1] if n < chips - 1 else near))[0]
     prefix = [block for pair in zip(near, far) for block in pair]
     suffix = suffix_kv[0, 0]
     summed, stats, text_rows = attend_text(me, prefix_len, queries[0, 0], prefix, suffix)
 
-    second = lax.optimization_barrier((buffers[chips:], stats))[0]
+    second[-1] = lax.optimization_barrier((second[-1], stats))[0]
     arrived = [
         [sent[0]] + [swap(sent[offset], 2 * offset) for offset in range(1, chips)]
         for sent in (first, second)

time: 87.4 us -> 84.9 us (0.971)
  waiting for transfers between devices: 7.05 us -> 10.9 us
  local copies, waits for them, and re-layouts: 3.83 us -> 0 us
  starting transfers between devices: 20 us -> 18.1 us
    ppermute x15, waiting for transfers between devices: 7.05 us -> 10.9 us  [swap(): return lax.ppermute(x, 'slot', [(i, i ^ k) for i in range(slot_count)])]
    unnamed x28 -> x0, local copies, waits for them, and re-layouts: 3.83 us -> none
    ppermute x15, starting transfers between devices: 14.8 us -> 12.8 us  [swap(): return lax.ppermute(x, 'slot', [(i, i ^ k) for i in range(slot_count)])]
  transfers between devices with their start and end apart: 16 -> 16, of which waited for: 5 -> 6; matrix products, arithmetic and copies ran while one was open for 0% -> 0% of each run, Pallas kernels for 57% -> 58%
where the time goes in v4:
time: 84.9 us; the launch traced here: 84.4 us
  Pallas kernels  54.1 us (64%)
  starting transfers between devices  18.1 us (21%)
  waiting for transfers between devices  10.9 us (13%)
  between operations  1.35 us (2%)
    pallas_call x1, Pallas kernels, attend_text(): pl.pallas_call(functools.partial(text_kernel, len(prefix)), out_shape=[ja...  22 us
    pallas_call x2, Pallas kernels, attend_image(): pl.pallas_call(functools.partial(image_kernel, 2 * chips, kept, len(tiles...  21 us
    ppermute x15, starting transfers between devices, swap(): return lax.ppermute(x, 'slot', [(i, i ^ k) for i in range(slot_count)])  12.8 us
    ppermute x15, waiting for transfers between devices, swap(): return lax.ppermute(x, 'slot', [(i, i ^ k) for i in range(slot_count)])  10.9 us
    pallas_call x1, Pallas kernels, pack(): pl.pallas_call(functools.partial(pack_kernel, chips, parts), out_shape=[j...  6.05 us
    all_to_all x1, starting transfers between devices, per_device(): every = lax.all_to_all(shares, ('prompt', 'slot'), 0, 0, tiled=True)  5.26 us
    pallas_call x1, Pallas kernels, last_rows(): pl.pallas_call(functools.partial(last_kernel, 2 * chips, kept, len(tiles)...  3.75 us
  transfers between devices with their start and end apart: 16, of which 6 were waited for; matrix products, arithmetic and copies ran while one was open for 0% of the time, Pallas kernels for 58%

profile of v4, /device:TPU:0, one launch (start us, length us, event | category | flops | bytes accessed | tf_op | source)
XLA Modules:
  0.0 84.4 jit_solution(18217821413781842445)
XLA Ops:
  0.6 0.5 collective-permute-start.5
  1.1 3.5 %collective-permute-start.3 = (bf16[512,256]{1,0:T(8,128)(2,1)}, bf16[512,256]{1,0:T(8,128)(2,1)}, u32[]{:S(2)}, u32[]{:S(2)}) collective-permute-start(bf16[512,256]{1,0:T(8,128)(2,1)} %bitcast.25), channel_id=1, source_target_pairs={{0,6},{1,7},{2,4},{3,5},{4,2},{5,3},{6,0},{7,1},{8,14},{9,15},{10,... | collective-permute-start | bytes 786440 | tf_op jit(solution)/shard_map/ppermute | solution.py:435
  4.7 0.5 collective-permute-start.2
  5.3 3.0 %collective-permute-done.4.mate_routes = s32[8]{0:T(128)} collective-permute-done((s32[8]{0:T(128)}, s32[8]{0:T(128)}, u32[]{:S(2)}, u32[]{:S(2)}) %collective-permute-start.4) | collective-permute-done | bytes 64 | tf_op jit(solution)/shard_map/ppermute | solution.py:435
  8.3 6.0 %pack_tiles.1 = (bf16[2,128,1280]{2,1,0:T(8,128)(2,1)}, bf16[2,128,1280]{2,1,0:T(8,128)(2,1)}, bf16[2,128,1280]{2,1,0:T(8,128)(2,1)}, bf16[2,128,1280]{2,1,0:T(8...) custom-call(s32[1]{0:T(128)} %bitcast.1.me, ...), custom_call_target="tpu_custom_call" | custom-call | bytes 17500000 | tf_op jit(solution)/shard_map/pack_tiles/pallas_call | solution.py:81
  14.3 3.2 %collective-permute-done.2.rest_4_ = bf16[512,256]{1,0:T(8,128)(2,1)} collective-permute-done((bf16[512,256]{1,0:T(8,128)(2,1)}, bf16[512,256]{1,0:T(8,128)(2,1)}, u32[]{:S(2)}, u32[]{:S(2)}) %collective-permute-start.2) | collective-permute-done | bytes 262176 | tf_op jit(solution)/shard_map/ppermute | solution.py:435
  17.5 0.3 collective-permute-done.1.rest_2_
  17.8 1.5 %collective-permute-start.14 = (bf16[2,128,1280]{2,1,0:T(8,128)(2,1)}, bf16[2,128,1280]{2,1,0:T(8,128)(2,1)}, u32[]{:S(2)}, u32[]{:S(2)}) collective-permute-start(bf16[2,128,1280]{2,1,0:T(8,128)(2,1)} %get-tuple-element.38), channel_id=1, source_target_pairs={{0,6},{1,7},{2,4},{3,5},{4,2},{5,3},{6,0},{7,1},{8,14},{9,15},{10,... | collective-permute-start | bytes 1966088 | tf_op jit(solution)/shard_map/ppermute | solution.py:435
  19.3 0.5 collective-permute-start.6
  19.8 0.5 collective-permute-start.8
  20.3 0.9 %collective-permute-done.rest_1_ = bf16[512,256]{1,0:T(8,128)(2,1)} collective-permute-done((bf16[512,256]{1,0:T(8,128)(2,1)}, bf16[512,256]{1,0:T(8,128)(2,1)}, u32[]{:S(2)}, u32[]{:S(2)}) %collective-permute-start) | collective-permute-done | bytes 262176 | tf_op jit(solution)/shard_map/ppermute | solution.py:435
  21.1 1.5 %collective-permute-start.13 = (bf16[2,128,1280]{2,1,0:T(8,128)(2,1)}, bf16[2,128,1280]{2,1,0:T(8,128)(2,1)}, u32[]{:S(2)}, u32[]{:S(2)}) collective-permute-start(bf16[2,128,1280]{2,1,0:T(8,128)(2,1)} %get-tuple-element.36), channel_id=1, source_target_pairs={{0,4},{1,5},{2,6},{3,7},{4,0},{5,1},{6,2},{7,3},{8,12},{9,13},{10,... | collective-permute-start | bytes 1966088 | tf_op jit(solution)/shard_map/ppermute | solution.py:435
  22.6 0.5 collective-permute-start.12
  23.8 1.6 %collective-permute-start.9 = (bf16[2,128,768]{2,1,0:T(8,128)(2,1)}, bf16[2,128,768]{2,1,0:T(8,128)(2,1)}, u32[]{:S(2)}, u32[]{:S(2)}) collective-permute-start(bf16[2,128,768]{2,1,0:T(8,128)(2,1)} %get-tuple-element.29), channel_id=1, source_target_pairs={{0,2},{1,3},{2,0},{3,1},{4,6},{5,7},{6,4},{7,5},{8,10},{9,11},{10,... | collective-permute-start | bytes 1179656 | tf_op jit(solution)/shard_map/ppermute | solution.py:435
  25.4 0.5 collective-permute-start.10
  25.9 22.0 %attend_text.1 = (f32[256,8192]{1,0:T(8,128)}, f32[256,1024]{1,0:T(8,128)}, bf16[8,768,256]{2,1,0:T(8,128)(2,1)}) custom-call(s32[1]{0:T(128)} %bitcast.1.me, s32[1]{0:T(128)S(6)} %copy.12.length.rest_4_, bf16[256,8192]{1,0:T(8,128)(2,1)} %bitcast.12, bf16[512,256]{1,0:T(8,128)(2,1)} %bitcast.29, bf16[512,256]{1,0:T(8,128)(2,1)} %collective-permute-done.rest_1_, ...), custom_call_target="tpu_custom_call" | custom-call | bytes 73500000 | tf_op jit(solution)/shard_map/attend_text/pallas_call | solution.py:161
  47.9 1.5 %collective-permute-start.11 = (bf16[2,128,768]{2,1,0:T(8,128)(2,1)}, bf16[2,128,768]{2,1,0:T(8,128)(2,1)}, u32[]{:S(2)}, u32[]{:S(2)}) collective-permute-start(bf16[2,128,768]{2,1,0:T(8,128)(2,1)} %get-tuple-element.32), channel_id=1, source_target_pairs={{0,6},{1,7},{2,4},{3,5},{4,2},{5,3},{6,0},{7,1},{8,14},{9,15},{10,... | collective-permute-start | bytes 1179656 | tf_op jit(solution)/shard_map/ppermute | solution.py:435
  49.5 1.1 %collective-permute-done.12.rest_1_ = bf16[2,128,1280]{2,1,0:T(8,128)(2,1)} collective-permute-done((bf16[2,128,1280]{2,1,0:T(8,128)(2,1)}, bf16[2,128,1280]{2,1,0:T(8,128)(2,1)}, u32[]{:S(2)}, u32[]{:S(2)}) %collective-permute-start.12) | collective-permute-done | bytes 655392 | tf_op jit(solution)/shard_map/ppermute | solution.py:435
  50.7 13.2 %attend_image.2 = (bf16[256,8192]{1,0:T(8,128)(2,1)}, f32[8,128]{1,0:T(8,128)}) custom-call(bf16[256,8192]{1,0:T(8,128)(2,1)} %bitcast.13, f32[256,8192]{1,0:T(8,128)} %get-tuple-element.26.acc_ref, f32[256,1024]{1,0:T(8,128)} %get-tuple-element.27.stat_ref, bf16[2,128,1280]{2,1,0:T(8,128)(2,1)} %get-tuple-element.22.rest_0_, ...), custom_call_target="tpu_custom_call" | custom-call | bytes 35000000 | tf_op jit(solution)/shard_map/attend_image/pallas_call | solution.py:328
  63.9 2.4 %collective-permute-done.11.rest_3_ = bf16[2,128,768]{2,1,0:T(8,128)(2,1)} collective-permute-done((bf16[2,128,768]{2,1,0:T(8,128)(2,1)}, bf16[2,128,768]{2,1,0:T(8,128)(2,1)}, u32[]{:S(2)}, u32[]{:S(2)}) %collective-permute-start.11) | collective-permute-done | bytes 393248 | tf_op jit(solution)/shard_map/ppermute | solution.py:435
  66.3 3.7 %last_rows.1 = f32[32,128]{1,0:T(8,128)} custom-call(s32[1]{0:T(128)S(6)} %copy.12.length.rest_4_, bf16[256,8192]{1,0:T(8,128)(2,1)} %bitcast.15, f32[64,128]{1,0:T(8,128)} %bitcast.31, bf16[8,768,256]{2,1,0:T(8,128)(2,1)} %get-tuple-element.39.rest_7_.kv_ref, bf16[2,128,768]{2,1,0:T(8,128)(2,1)} %get-tuple-element.28.rest_0_, ...), custom_call_target="tpu_custom_call" | custom-call | bytes 10500000 | tf_op jit(solution)/shard_map/last_rows/pallas_call | solution.py:399
  70.1 5.3 %all-to-all-start = ((f32[32,1,128]{2,1,0:T(1,128)}), f32[32,1,128]{2,1,0:T(1,128)}, u32[]{:S(2)}, u32[]{:S(2)}) async-start(f32[32,1,128]{2,1,0:T(1,128)} %bitcast.32), calls=%async_computation | async-start | bytes 32768 | tf_op jit(solution)/shard_map/all_to_all | solution.py:460
  75.4 7.7 %attend_image.3 = bf16[256,8192]{1,0:T(8,128)(2,1)} custom-call(bf16[256,8192]{1,0:T(8,128)(2,1)} %bitcast.16, f32[256,8192]{1,0:T(8,128)} %get-tuple-element.26.acc_ref, f32[256,1024]{1,0:T(8,128)} %get-tuple-element.27.stat_ref, bf16[2,128,768]{2,1,0:T(8,128)(2,1)} %get-tuple-element.28.rest_0_, ...), custom_call_target="tpu_custom_call", output_to_operand_aliasing={{}: (7, {})} | custom-call | bytes 21000000 | tf_op jit(solution)/shard_map/attend_image/pallas_call | solution.py:328
  83.1 1.4 %normalize.1 = f32[1,1]{1,0:T(1,128)} custom-call(f32[32,128]{1,0:T(8,128)} %bitcast.10.every_ref), custom_call_target="tpu_custom_call" | custom-call | bytes 3500000 | tf_op jit(solution)/shard_map/normalize/pallas_call | solution.py:462
  (14 shorter events, 0.2 us)
Async XLA Ops:
  0.6 7.6 %collective-permute-start.5 = (bf16[8,128,2048]{2,1,0:T(8,128)(2,1)}, bf16[8,128,2048]{2,1,0:T(8,128)(2,1)}, u32[]{:S(2)}, u32[]{:S(2)}) collective-permute-start(bf16[8,128,2048]{2,1,0:T(8,128)(2,1)} %bitcast.17), channel_id=1, source_target_pairs={{0,1},{1,0},{2,3},{3,2},{4,5},{5,4},{6,7},{7,6},{8,9},{9,8},{10,11... | collective-permute-start | bytes 12582920 | tf_op jit(solution)/shard_map/ppermute | solution.py:435
  1.1 13.2 %collective-permute-start.3 = (bf16[512,256]{1,0:T(8,128)(2,1)}, bf16[512,256]{1,0:T(8,128)(2,1)}, u32[]{:S(2)}, u32[]{:S(2)}) collective-permute-start(bf16[512,256]{1,0:T(8,128)(2,1)} %bitcast.25), channel_id=1, source_target_pairs={{0,6},{1,7},{2,4},{3,5},{4,2},{5,3},{6,0},{7,1},{8,14},{9,15},{10,... | collective-permute-start | bytes 786440 | tf_op jit(solution)/shard_map/ppermute | solution.py:435
  4.7 12.8 %collective-permute-start.2 = (bf16[512,256]{1,0:T(8,128)(2,1)}, bf16[512,256]{1,0:T(8,128)(2,1)}, u32[]{:S(2)}, u32[]{:S(2)}) collective-permute-start(bf16[512,256]{1,0:T(8,128)(2,1)} %bitcast.26), channel_id=1, source_target_pairs={{0,4},{1,5},{2,6},{3,7},{4,0},{5,1},{6,2},{7,3},{8,12},{9,13},{10,... | collective-permute-start | bytes 786440 | tf_op jit(solution)/shard_map/ppermute | solution.py:435
  5.2 12.6 %collective-permute-start.1 = (bf16[512,256]{1,0:T(8,128)(2,1)}, bf16[512,256]{1,0:T(8,128)(2,1)}, u32[]{:S(2)}, u32[]{:S(2)}) collective-permute-start(bf16[512,256]{1,0:T(8,128)(2,1)} %bitcast.27), channel_id=1, source_target_pairs={{0,2},{1,3},{2,0},{3,1},{4,6},{5,7},{6,4},{7,5},{8,10},{9,11},{10,... | collective-permute-start | bytes 786440 | tf_op jit(solution)/shard_map/ppermute | solution.py:435
  5.3 3.0 %collective-permute-start.4 = (s32[8]{0:T(128)}, s32[8]{0:T(128)}, u32[]{:S(2)}, u32[]{:S(2)}) collective-permute-start(s32[8]{0:T(128)} %bitcast.33), channel_id=1, source_target_pairs={{0,1},{1,0},{2,3},{3,2},{4,5},{5,4},{6,7},{7,6},{8,9},{9,8},{10,11... | collective-permute-start | bytes 104 | tf_op jit(solution)/shard_map/ppermute | solution.py:435
  17.8 30.1 %collective-permute-start.14 = (bf16[2,128,1280]{2,1,0:T(8,128)(2,1)}, bf16[2,128,1280]{2,1,0:T(8,128)(2,1)}, u32[]{:S(2)}, u32[]{:S(2)}) collective-permute-start(bf16[2,128,1280]{2,1,0:T(8,128)(2,1)} %get-tuple-element.38), channel_id=1, source_target_pairs={{0,6},{1,7},{2,4},{3,5},{4,2},{5,3},{6,0},{7,1},{8,14},{9,15},{10,... | collective-permute-start | bytes 1966088 | tf_op jit(solution)/shard_map/ppermute | solution.py:435
  19.3 1.9 %collective-permute-start = (bf16[512,256]{1,0:T(8,128)(2,1)}, bf16[512,256]{1,0:T(8,128)(2,1)}, u32[]{:S(2)}, u32[]{:S(2)}) collective-permute-start(bf16[512,256]{1,0:T(8,128)(2,1)} %bitcast.28), channel_id=1, source_target_pairs={{0,1},{1,0},{2,3},{3,2},{4,5},{5,4},{6,7},{7,6},{8,9},{9,8},{10,11... | collective-permute-start | bytes 786440 | tf_op jit(solution)/shard_map/ppermute | solution.py:435
  19.3 3.4 %collective-permute-start.6 = (bf16[512,256]{1,0:T(8,128)(2,1)}, bf16[512,256]{1,0:T(8,128)(2,1)}, u32[]{:S(2)}, u32[]{:S(2)}) collective-permute-start(bf16[512,256]{1,0:T(8,128)(2,1)} %collective-permute-done.1.rest_2_), channel_id=1, source_target_pairs={{0,1},{1,0},{2,3},{3,2},{4,5},{5,4},{6,7},{7,6},{8,9},{9,8},{10,11... | collective-permute-start | bytes 786440 | tf_op jit(solution)/shard_map/ppermute | solution.py:435
  19.8 4.1 %collective-permute-start.7 = (bf16[512,256]{1,0:T(8,128)(2,1)}, bf16[512,256]{1,0:T(8,128)(2,1)}, u32[]{:S(2)}, u32[]{:S(2)}) collective-permute-start(bf16[512,256]{1,0:T(8,128)(2,1)} %collective-permute-done.2.rest_4_), channel_id=1, source_target_pairs={{0,1},{1,0},{2,3},{3,2},{4,5},{5,4},{6,7},{7,6},{8,9},{9,8},{10,11... | collective-permute-start | bytes 786440 | tf_op jit(solution)/shard_map/ppermute | solution.py:435
  19.8 5.6 %collective-permute-start.8 = (bf16[512,256]{1,0:T(8,128)(2,1)}, bf16[512,256]{1,0:T(8,128)(2,1)}, u32[]{:S(2)}, u32[]{:S(2)}) collective-permute-start(bf16[512,256]{1,0:T(8,128)(2,1)} %collective-permute-done.3.rest_6_), channel_id=1, source_target_pairs={{0,1},{1,0},{2,3},{3,2},{4,5},{5,4},{6,7},{7,6},{8,9},{9,8},{10,11... | collective-permute-start | bytes 786440 | tf_op jit(solution)/shard_map/ppermute | solution.py:435
  21.1 28.4 %collective-permute-start.13 = (bf16[2,128,1280]{2,1,0:T(8,128)(2,1)}, bf16[2,128,1280]{2,1,0:T(8,128)(2,1)}, u32[]{:S(2)}, u32[]{:S(2)}) collective-permute-start(bf16[2,128,1280]{2,1,0:T(8,128)(2,1)} %get-tuple-element.36), channel_id=1, source_target_pairs={{0,4},{1,5},{2,6},{3,7},{4,0},{5,1},{6,2},{7,3},{8,12},{9,13},{10,... | collective-permute-start | bytes 1966088 | tf_op jit(solution)/shard_map/ppermute | solution.py:435
  22.6 28.0 %collective-permute-start.12 = (bf16[2,128,1280]{2,1,0:T(8,128)(2,1)}, bf16[2,128,1280]{2,1,0:T(8,128)(2,1)}, u32[]{:S(2)}, u32[]{:S(2)}) collective-permute-start(bf16[2,128,1280]{2,1,0:T(8,128)(2,1)} %get-tuple-element.34), channel_id=1, source_target_pairs={{0,2},{1,3},{2,0},{3,1},{4,6},{5,7},{6,4},{7,5},{8,10},{9,11},{10,... | collective-permute-start | bytes 1966088 | tf_op jit(solution)/shard_map/ppermute | solution.py:435
  23.8 40.1 %collective-permute-start.9 = (bf16[2,128,768]{2,1,0:T(8,128)(2,1)}, bf16[2,128,768]{2,1,0:T(8,128)(2,1)}, u32[]{:S(2)}, u32[]{:S(2)}) collective-permute-start(bf16[2,128,768]{2,1,0:T(8,128)(2,1)} %get-tuple-element.29), channel_id=1, source_target_pairs={{0,2},{1,3},{2,0},{3,1},{4,6},{5,7},{6,4},{7,5},{8,10},{9,11},{10,... | collective-permute-start | bytes 1179656 | tf_op jit(solution)/shard_map/ppermute | solution.py:435
  25.4 38.5 %collective-permute-start.10 = (bf16[2,128,768]{2,1,0:T(8,128)(2,1)}, bf16[2,128,768]{2,1,0:T(8,128)(2,1)}, u32[]{:S(2)}, u32[]{:S(2)}) collective-permute-start(bf16[2,128,768]{2,1,0:T(8,128)(2,1)} %get-tuple-element.30), channel_id=1, source_target_pairs={{0,4},{1,5},{2,6},{3,7},{4,0},{5,1},{6,2},{7,3},{8,12},{9,13},{10,... | collective-permute-start | bytes 1179656 | tf_op jit(solution)/shard_map/ppermute | solution.py:435
  47.9 18.4 %collective-permute-start.11 = (bf16[2,128,768]{2,1,0:T(8,128)(2,1)}, bf16[2,128,768]{2,1,0:T(8,128)(2,1)}, u32[]{:S(2)}, u32[]{:S(2)}) collective-permute-start(bf16[2,128,768]{2,1,0:T(8,128)(2,1)} %get-tuple-element.32), channel_id=1, source_target_pairs={{0,6},{1,7},{2,4},{3,5},{4,2},{5,3},{6,0},{7,1},{8,14},{9,15},{10,... | collective-permute-start | bytes 1179656 | tf_op jit(solution)/shard_map/ppermute | solution.py:435
  70.1 13.0 %all-to-all-start = ((f32[32,1,128]{2,1,0:T(1,128)}), f32[32,1,128]{2,1,0:T(1,128)}, u32[]{:S(2)}, u32[]{:S(2)}) async-start(f32[32,1,128]{2,1,0:T(1,128)} %bitcast.32), calls=%async_computation | async-start | bytes 32768 | tf_op jit(solution)/shard_map/all_to_all | solution.py:460

commit v5 on v4

--- a/solution.py
+++ b/solution.py
@@ -15,7 +15,7 @@
 SCALE = math.log2(math.e) / math.sqrt(HD)
 LOW = -1e30
 ROOM = 2.0**100
-PARTS = ((0, 5, False), (5, 3, False))
+PARTS = ((0, 5), (5, 3))
 LAST = 16
 EMPTY = 1024.0
 NT = (((1,), (1,)), ((), ()))
@@ -40,36 +40,27 @@
     tiles, outs = rest[: 2 * chips], list(rest[2 * chips :])
     chip, core = me[0] // 2, me[0] % 2
     top = (lax.broadcasted_iota(jnp.int32, (16, HD), 0) == 0) & (pl.program_id(0) == 0)
-    for head_from, heads, together in parts:
-        width = heads * HD
+    for head_from, heads in parts:
         for offset in range(chips):
-            out = outs[0].at[chip ^ offset] if together else outs.pop(0)
+            out = outs.pop(0)
             for n, held in enumerate((routes, mate_routes)):
                 tile = tiles[2 * offset + n]
                 found = slot_of(2 * (chip ^ offset) + core, held)[1]
-                for half in range(2):
-                    first = (half * KVH + head_from) * HD
-                    out[n, :, half * width : (half + 1) * width] = tile[0, :, first : first + width]
+                for i in range(2 * heads):
+                    first = (i % 2 * KVH + head_from + i // 2) * HD
+                    out[n, :, i * HD : (i + 1) * HD] = tile[0, :, first : first + HD]
                 mark = top & jnp.logical_not(found)
                 kept = tile[0, :16, head_from * HD : (head_from + 1) * HD]
                 out[n, :16, :HD] = jnp.where(mark, jnp.full_like(kept, EMPTY), kept)
-        if together:
-            outs.pop(0)
 
 
 def pack(parts, chips, me, routes, mate_routes, patch, mate_patch):
     tile_rows, width = patch.shape[1:]
     rows = tile_rows // 4
     shapes, specs, sources = [], [], []
-    for _, heads, together in parts:
-        shape = (2, tile_rows, 2 * heads * HD)
-        block = (2, rows, 2 * heads * HD)
-        if together:
-            shapes.append((chips,) + shape)
-            specs.append(pl.BlockSpec((chips,) + block, lambda r, *_: (0, 0, r, 0)))
-        else:
-            shapes += [shape] * chips
-            specs += [pl.BlockSpec(block, lambda r, *_: (0, r, 0))] * chips
+    for _, heads in parts:
+        shapes += [(2, tile_rows, 2 * heads * HD)] * chips
+        specs += [pl.BlockSpec((2, rows, 2 * heads * HD), lambda r, *_: (0, r, 0))] * chips
     for offset in range(chips):
         for n in range(2):
 
@@ -192,7 +183,7 @@
 
 
 def tile_at(tiles, n):
-    return tiles[0].at[n // 2, n % 2] if len(tiles) == 1 else tiles[n // 2].at[n % 2]
+    return tiles[n // 2].at[n % 2]
 
 
 def place_tiles(slots, kept, tiles, place_ref):
@@ -204,21 +195,20 @@
 
 
 def fill_image(slots, head, tiles, place_ref, kbuf, vbuf):
-    tile_rows, width = tiles[0].shape[-2], tiles[0].shape[-1] // 2
+    tile_rows = tiles[0].shape[-2]
     for n in range(slots):
         row = pl.ds(pl.multiple_of(place_ref[n] * tile_rows, tile_rows), tile_rows)
         tile = tile_at(tiles, n)
-        for buf, first in ((kbuf, 0), (vbuf, width)):
-            column = first + head * HD
-            column = column if isinstance(head, int) else pl.multiple_of(column, HD)
-            buf[row, :HD] = tile[:, pl.ds(column, HD)]
+        for i, buf in enumerate((kbuf, vbuf)):
+            first = (2 * head + i) * HD
+            buf[row, :HD] = tile[:, first : first + HD]
 
 
 def image_kernel(slots, kept, count, last, q_ref, acc_ref, stat_ref, *rest):
     tiles, rest = rest[:count], rest[count:]
     if last:
         length, last_ref, head_ref, text_ref, o_ref, score_ref, kbuf, vbuf, place_ref = rest[:9]
-        last_kbuf, last_vbuf, kv_ref, sem = rest[9:]
+        kv_ref, sem = rest[9:]
         head_from, heads, prefix_rows = last
         copy = pltpu.make_async_copy(text_ref.at[pl.ds(head_from, heads)], kv_ref, sem)
     else:
@@ -229,16 +219,16 @@
 
     @pl.when(g == 0)
     def _():
-        vbuf[:, HD:] = jnp.ones((total + tile_rows, HD), vbuf.dtype)
+        vbuf[:, :, HD:] = jnp.ones(vbuf.shape[:2] + (HD,), vbuf.dtype)
         place_tiles(slots, kept, tiles, place_ref)
         if last:
             copy.start()
 
-    fill_image(slots, g, tiles, place_ref, kbuf, vbuf)
+    fill_image(slots, 0, tiles, place_ref, kbuf.at[g], vbuf.at[g])
 
     def scores(column):
         return lax.dot_general(
-            q_ref[:, column], kbuf[:total], NT, preferred_element_type=jnp.float32
+            q_ref[:, column], kbuf[g, :total], NT, preferred_element_type=jnp.float32
         )
 
     def close(summed, totals, column):
@@ -254,7 +244,7 @@
             power = (s[:, k * HD : (k + 1) * HD] - held) * SCALE
             powers.append(jnp.exp2(power).astype(jnp.bfloat16))
         weights = jnp.concatenate(powers, axis=1)
-        mixed = jnp.dot(weights, vbuf[:total], preferred_element_type=jnp.float32)
+        mixed = jnp.dot(weights, vbuf[g, :total], preferred_element_type=jnp.float32)
         totals = mixed[:, HD:] + stat_ref[:, GROUPS + h : GROUPS + h + 1]
         largest[0] = jnp.maximum(largest[0], jnp.max(totals.reshape(rows // 8, 8, HD), axis=0))
         close(mixed[:, :HD] + acc_ref[:, column], totals, column)
@@ -273,7 +263,7 @@
             sums = jnp.sum(sums, axis=1, keepdims=True)
             peak = jnp.maximum(held, jnp.max(s, axis=1, keepdims=True))
             weights = jnp.exp2((s - peak) * SCALE).astype(jnp.bfloat16)
-            mixed = jnp.dot(weights, vbuf[:total], preferred_element_type=jnp.float32)
+            mixed = jnp.dot(weights, vbuf[g, :total], preferred_element_type=jnp.float32)
             fade = jnp.exp2((held - peak) * SCALE)
             summed = acc_ref[:, column] * fade + mixed[:, :HD]
             close(summed, sums * fade + mixed[:, HD:], column)
@@ -283,24 +273,23 @@
         def _():
             copy.wait()
             score_ref[...] = last_row_gain(
-                slots, head_from, heads, prefix_rows, total, length, last_ref, head_ref, kv_ref, tiles,
-                place_ref, last_kbuf, last_vbuf,
+                head_from, heads, prefix_rows, total, length, last_ref, head_ref, kv_ref, kbuf, vbuf
             )
 
 
 def attend_image(chips, kept, part, tiles, queries, summed, stats, context=None, last=None):
-    head_from, heads, _ = part
+    head_from, heads = part
     tile_rows = tiles[0].shape[-2]
     total, wide, rows = kept * tile_rows, GROUPS * HD, queries.shape[0]
     column = lambda g: (0, head_from + g)
     specs = [pl.BlockSpec((rows, wide), column)] * 2 + [pl.BlockSpec((rows, HD), column)]
-    specs += [pl.BlockSpec(tile.shape, lambda g, d=tile.ndim: (0,) * d) for tile in tiles]
+    specs += [pl.BlockSpec((2, tile_rows, 2 * HD), lambda g: (0, 0, g)) for tile in tiles]
     operands = [queries, summed, stats, *tiles]
     shapes = [jax.ShapeDtypeStruct(queries.shape, queries.dtype)]
     outs = [pl.BlockSpec((rows, wide), column)]
     scratch = [
-        pltpu.VMEM((total + tile_rows, HD), queries.dtype),
-        pltpu.VMEM((total + tile_rows, 2 * HD), queries.dtype),
+        pltpu.VMEM((heads, total + tile_rows, HD), queries.dtype),
+        pltpu.VMEM((heads, total + tile_rows, 2 * HD), queries.dtype),
         pltpu.SMEM((2 * chips,), jnp.int32),
     ]
     aliases, static = {}, None
@@ -317,7 +306,7 @@
         ]
         shapes.append(jax.ShapeDtypeStruct((GROUPS, HD), jnp.float32))
         outs.append(pl.BlockSpec((GROUPS, HD), lambda g: (0, 0)))
-        scratch += last_scratch(heads, total + tile_rows, queries.dtype) + [
+        scratch += [
             pltpu.VMEM((heads,) + text_rows.shape[1:], queries.dtype),
             pltpu.SemaphoreType.DMA,
         ]
@@ -339,12 +328,12 @@
     )(*operands)
 
 
-def last_row_gain(slots, head_from, heads, prefix_rows, total, length, q_ref, head_ref, kv_ref, tiles, place_ref, kbuf, vbuf):
+def last_row_gain(
+    head_from, heads, prefix_rows, total, length, q_ref, head_ref, kv_ref, kbuf, vbuf
+):
     gain = jnp.zeros((GROUPS, HD), jnp.float32)
     column = lax.broadcasted_iota(jnp.int32, (GROUPS, kv_ref.shape[1]), 1)
     live = (column < length[0]) | (column >= prefix_rows)
-    for i in range(heads):
-        fill_image(slots, i, tiles, place_ref, kbuf.at[i], vbuf.at[i])
     for i in range(heads):
         first = (head_from + i) * GROUPS
         q = [q_ref[:, (first + h) * HD : (first + h + 1) * HD] for h in range(GROUPS)]
@@ -359,7 +348,7 @@
         weights = [jnp.exp2((part - peak) * SCALE) for part in s]
         mixed = sum(
             jnp.dot(part.astype(jnp.bfloat16), values, preferred_element_type=jnp.float32)
-            for part, values in zip(weights, (kv_ref[i, :, HD:], vbuf[i, :total]))
+            for part, values in zip(weights, (kv_ref[i, :, HD:], vbuf[i, :total, :HD]))
         )
         totals = sum(jnp.sum(part, axis=1, keepdims=True) for part in weights)
         out = (mixed / totals).astype(jnp.bfloat16).astype(jnp.float32)
@@ -371,9 +360,10 @@
     tiles, (before, score_ref, kbuf, vbuf, place_ref) = rest[:count], rest[count:]
     total = kept * tiles[0].shape[-2]
     place_tiles(slots, kept, tiles, place_ref)
+    for i in range(heads):
+        fill_image(slots, i, tiles, place_ref, kbuf.at[i], vbuf.at[i])
     gain = before[...] + last_row_gain(
-        slots, head_from, heads, prefix_rows, total, length, q_ref, head_ref, kv_ref, tiles, place_ref,
-        kbuf, vbuf,
+        head_from, heads, prefix_rows, total, length, q_ref, head_ref, kv_ref, kbuf, vbuf
     )
     score_ref[...] = jnp.broadcast_to(jnp.sum(gain, axis=0, keepdims=True), score_ref.shape)
 
@@ -383,7 +373,7 @@
 
 
 def last_rows(chips, kept, part, tiles, queries, length, prefix_rows, head, text_rows, share, devices):
-    head_from, heads, _ = part
+    head_from, heads = part
     tile_rows, text = tiles[0].shape[-2], text_rows.shape[1]
     whole = lambda x: pl.BlockSpec(x.shape, lambda g, d=x.ndim: (0,) * d)
     end = queries.shape[0] // LAST - 1
@@ -441,7 +431,7 @@
     far = [swap(block, 1) for block in [near[0], *held]]
     first, second = list(buffers[:chips]), list(buffers[chips:])
     for n in range(1, chips):
-        first[n] = lax.optimization_barrier((first[n], near[:-1] if n < chips - 1 else near))[0]
+        first[n] = lax.optimization_barrier((first[n], near[:-1] if n == chips - 1 else near))[0]
     prefix = [block for pair in zip(near, far) for block in pair]
     suffix = suffix_kv[0, 0]
     summed, stats, text_rows = attend_text(me, prefix_len, queries[0, 0], prefix, suffix)

time: 84.9 us -> 83.8 us (0.987)
  waiting for transfers between devices: 10.9 us -> 7.69 us
  starting transfers between devices: 18.1 us -> 21.3 us
  Pallas kernels: 54.1 us -> 53.1 us
    ppermute x15, waiting for transfers between devices: 10.9 us -> 7.69 us  [swap(): return lax.ppermute(x, 'slot', [(i, i ^ k) for i in range(slot_count)])]
    ppermute x15, starting transfers between devices: 12.8 us -> 14.7 us  [swap(): return lax.ppermute(x, 'slot', [(i, i ^ k) for i in range(slot_count)])]
    all_to_all x1, starting transfers between devices: 5.26 us -> 6.62 us  [per_device(): every = lax.all_to_all(shares, ('prompt', 'slot'), 0, 0, tiled=True)]
    pallas_call x2, Pallas kernels: 21 us -> 20 us  [attend_image(): pl.pallas_call(functools.partial(image_kernel, 2 * chips, kept, len(tiles...]
  transfers between devices with their start and end apart: 16 -> 16, of which waited for: 6 -> 4; matrix products, arithmetic and copies ran while one was open for 0% -> 0% of each run, Pallas kernels for 58% -> 58%
where the time goes in v5:
time: 83.8 us; the launch traced here: 83.4 us
  Pallas kernels  53.1 us (63%)
  starting transfers between devices  21.3 us (25%)
  waiting for transfers between devices  7.69 us (9%)
  between operations  1.36 us (2%)
    pallas_call x1, Pallas kernels, attend_text(): pl.pallas_call(functools.partial(text_kernel, len(prefix)), out_shape=[ja...  22 us
    pallas_call x2, Pallas kernels, attend_image(): pl.pallas_call(functools.partial(image_kernel, 2 * chips, kept, len(tiles...  20 us
    ppermute x15, starting transfers between devices, swap(): return lax.ppermute(x, 'slot', [(i, i ^ k) for i in range(slot_count)])  14.7 us
    ppermute x15, waiting for transfers between devices, swap(): return lax.ppermute(x, 'slot', [(i, i ^ k) for i in range(slot_count)])  7.69 us
    all_to_all x1, starting transfers between devices, per_device(): every = lax.all_to_all(shares, ('prompt', 'slot'), 0, 0, tiled=True)  6.62 us
    pallas_call x1, Pallas kernels, pack(): pl.pallas_call(functools.partial(pack_kernel, chips, parts), out_shape=[j...  5.99 us
    pallas_call x1, Pallas kernels, last_rows(): pl.pallas_call(functools.partial(last_kernel, 2 * chips, kept, len(tiles)...  3.75 us
  transfers between devices with their start and end apart: 16, of which 4 were waited for; matrix products, arithmetic and copies ran while one was open for 0% of the time, Pallas kernels for 58%

profile of v5, /device:TPU:0, one launch (start us, length us, event | category | flops | bytes accessed | tf_op | source)
XLA Modules:
  0.0 83.4 jit_solution(907785731626645373)
XLA Ops:
  0.6 0.5 collective-permute-start.5
  1.1 2.6 %collective-permute-start.2 = (bf16[512,256]{1,0:T(8,128)(2,1)}, bf16[512,256]{1,0:T(8,128)(2,1)}, u32[]{:S(2)}, u32[]{:S(2)}) collective-permute-start(bf16[512,256]{1,0:T(8,128)(2,1)} %bitcast.25), channel_id=1, source_target_pairs={{0,4},{1,5},{2,6},{3,7},{4,0},{5,1},{6,2},{7,3},{8,12},{9,13},{10,... | collective-permute-start | bytes 786440 | tf_op jit(solution)/shard_map/ppermute | solution.py:425
  3.7 1.5 %collective-permute-start.1 = (bf16[512,256]{1,0:T(8,128)(2,1)}, bf16[512,256]{1,0:T(8,128)(2,1)}, u32[]{:S(2)}, u32[]{:S(2)}) collective-permute-start(bf16[512,256]{1,0:T(8,128)(2,1)} %bitcast.26), channel_id=1, source_target_pairs={{0,2},{1,3},{2,0},{3,1},{4,6},{5,7},{6,4},{7,5},{8,10},{9,11},{10,... | collective-permute-start | bytes 786440 | tf_op jit(solution)/shard_map/ppermute | solution.py:425
  5.2 0.1 collective-permute-start.3
  5.3 3.0 %collective-permute-done.4.mate_routes = s32[8]{0:T(128)} collective-permute-done((s32[8]{0:T(128)}, s32[8]{0:T(128)}, u32[]{:S(2)}, u32[]{:S(2)}) %collective-permute-start.4) | collective-permute-done | bytes 64 | tf_op jit(solution)/shard_map/ppermute | solution.py:425
  8.3 6.0 %pack_tiles.1 = (bf16[2,128,1280]{2,1,0:T(8,128)(2,1)}, bf16[2,128,1280]{2,1,0:T(8,128)(2,1)}, bf16[2,128,1280]{2,1,0:T(8,128)(2,1)}, bf16[2,128,1280]{2,1,0:T(8...) custom-call(s32[1]{0:T(128)} %bitcast.1.me, ...), custom_call_target="tpu_custom_call" | custom-call | bytes 17500000 | tf_op jit(solution)/shard_map/pack_tiles/pallas_call | solution.py:72
  14.3 3.9 %collective-permute-start.14 = (bf16[2,128,1280]{2,1,0:T(8,128)(2,1)}, bf16[2,128,1280]{2,1,0:T(8,128)(2,1)}, u32[]{:S(2)}, u32[]{:S(2)}) collective-permute-start(bf16[2,128,1280]{2,1,0:T(8,128)(2,1)} %get-tuple-element.38), channel_id=1, source_target_pairs={{0,6},{1,7},{2,4},{3,5},{4,2},{5,3},{6,0},{7,1},{8,14},{9,15},{10,... | collective-permute-start | bytes 1966088 | tf_op jit(solution)/shard_map/ppermute | solution.py:425
  18.2 0.5 collective-permute-start.6
  18.7 0.0 collective-permute-start.7
  18.7 0.5 collective-permute-start.8
  19.2 0.9 %collective-permute-done.rest_1_ = bf16[512,256]{1,0:T(8,128)(2,1)} collective-permute-done((bf16[512,256]{1,0:T(8,128)(2,1)}, bf16[512,256]{1,0:T(8,128)(2,1)}, u32[]{:S(2)}, u32[]{:S(2)}) %collective-permute-start) | collective-permute-done | bytes 262176 | tf_op jit(solution)/shard_map/ppermute | solution.py:425
  20.0 0.8 collective-permute-start.13
  20.8 0.7 collective-permute-start.12
  22.2 1.4 %collective-permute-start.9 = (bf16[2,128,768]{2,1,0:T(8,128)(2,1)}, bf16[2,128,768]{2,1,0:T(8,128)(2,1)}, u32[]{:S(2)}, u32[]{:S(2)}) collective-permute-start(bf16[2,128,768]{2,1,0:T(8,128)(2,1)} %get-tuple-element.29), channel_id=1, source_target_pairs={{0,2},{1,3},{2,0},{3,1},{4,6},{5,7},{6,4},{7,5},{8,10},{9,11},{10,... | collective-permute-start | bytes 1179656 | tf_op jit(solution)/shard_map/ppermute | solution.py:425
  23.6 1.2 %collective-permute-start.10 = (bf16[2,128,768]{2,1,0:T(8,128)(2,1)}, bf16[2,128,768]{2,1,0:T(8,128)(2,1)}, u32[]{:S(2)}, u32[]{:S(2)}) collective-permute-start(bf16[2,128,768]{2,1,0:T(8,128)(2,1)} %get-tuple-element.30), channel_id=1, source_target_pairs={{0,4},{1,5},{2,6},{3,7},{4,0},{5,1},{6,2},{7,3},{8,12},{9,13},{10,... | collective-permute-start | bytes 1179656 | tf_op jit(solution)/shard_map/ppermute | solution.py:425
  24.8 22.0 %attend_text.1 = (f32[256,8192]{1,0:T(8,128)}, f32[256,1024]{1,0:T(8,128)}, bf16[8,768,256]{2,1,0:T(8,128)(2,1)}) custom-call(s32[1]{0:T(128)} %bitcast.1.me, s32[1]{0:T(128)S(6)} %copy.12.length.rest_4_, bf16[256,8192]{1,0:T(8,128)(2,1)} %bitcast.12, bf16[512,256]{1,0:T(8,128)(2,1)} %bitcast.29, bf16[512,256]{1,0:T(8,128)(2,1)} %collective-permute-done.rest_1_, ...), custom_call_target="tpu_custom_call" | custom-call | bytes 73500000 | tf_op jit(solution)/shard_map/attend_text/pallas_call | solution.py:152
  46.8 1.0 %collective-permute-start.11 = (bf16[2,128,768]{2,1,0:T(8,128)(2,1)}, bf16[2,128,768]{2,1,0:T(8,128)(2,1)}, u32[]{:S(2)}, u32[]{:S(2)}) collective-permute-start(bf16[2,128,768]{2,1,0:T(8,128)(2,1)} %get-tuple-element.32), channel_id=1, source_target_pairs={{0,6},{1,7},{2,4},{3,5},{4,2},{5,3},{6,0},{7,1},{8,14},{9,15},{10,... | collective-permute-start | bytes 1179656 | tf_op jit(solution)/shard_map/ppermute | solution.py:425
  47.8 1.0 %collective-permute-done.12.rest_1_ = bf16[2,128,1280]{2,1,0:T(8,128)(2,1)} collective-permute-done((bf16[2,128,1280]{2,1,0:T(8,128)(2,1)}, bf16[2,128,1280]{2,1,0:T(8,128)(2,1)}, u32[]{:S(2)}, u32[]{:S(2)}) %collective-permute-start.12) | collective-permute-done | bytes 655392 | tf_op jit(solution)/shard_map/ppermute | solution.py:425
  48.8 12.8 %attend_image.2 = (bf16[256,8192]{1,0:T(8,128)(2,1)}, f32[8,128]{1,0:T(8,128)}) custom-call(bf16[256,8192]{1,0:T(8,128)(2,1)} %bitcast.13, f32[256,8192]{1,0:T(8,128)} %get-tuple-element.26.acc_ref, f32[256,1024]{1,0:T(8,128)} %get-tuple-element.27.stat_ref, bf16[2,128,1280]{2,1,0:T(8,128)(2,1)} %get-tuple-element.22.rest_0_, ...), custom_call_target="tpu_custom_call" | custom-call | bytes 35000000 | tf_op jit(solution)/shard_map/attend_image/pallas_call | solution.py:317
  61.6 2.9 %collective-permute-done.11.rest_3_ = bf16[2,128,768]{2,1,0:T(8,128)(2,1)} collective-permute-done((bf16[2,128,768]{2,1,0:T(8,128)(2,1)}, bf16[2,128,768]{2,1,0:T(8,128)(2,1)}, u32[]{:S(2)}, u32[]{:S(2)}) %collective-permute-start.11) | collective-permute-done | bytes 393248 | tf_op jit(solution)/shard_map/ppermute | solution.py:425
  64.5 3.7 %last_rows.1 = f32[32,128]{1,0:T(8,128)} custom-call(s32[1]{0:T(128)S(6)} %copy.12.length.rest_4_, bf16[256,8192]{1,0:T(8,128)(2,1)} %bitcast.15, f32[64,128]{1,0:T(8,128)} %bitcast.31, bf16[8,768,256]{2,1,0:T(8,128)(2,1)} %get-tuple-element.39.rest_7_.kv_ref, bf16[2,128,768]{2,1,0:T(8,128)(2,1)} %get-tuple-element.28.rest_0_, ...), custom_call_target="tpu_custom_call" | custom-call | bytes 10500000 | tf_op jit(solution)/shard_map/last_rows/pallas_call | solution.py:389
  68.2 6.6 %all-to-all-start = ((f32[32,1,128]{2,1,0:T(1,128)}), f32[32,1,128]{2,1,0:T(1,128)}, u32[]{:S(2)}, u32[]{:S(2)}) async-start(f32[32,1,128]{2,1,0:T(1,128)} %bitcast.32), calls=%async_computation | async-start | bytes 32768 | tf_op jit(solution)/shard_map/all_to_all | solution.py:450
  74.8 7.2 %attend_image.3 = bf16[256,8192]{1,0:T(8,128)(2,1)} custom-call(bf16[256,8192]{1,0:T(8,128)(2,1)} %bitcast.16, f32[256,8192]{1,0:T(8,128)} %get-tuple-element.26.acc_ref, f32[256,1024]{1,0:T(8,128)} %get-tuple-element.27.stat_ref, bf16[2,128,768]{2,1,0:T(8,128)(2,1)} %get-tuple-element.28.rest_0_, ...), custom_call_target="tpu_custom_call", output_to_operand_aliasing={{}: (7, {})} | custom-call | bytes 21000000 | tf_op jit(solution)/shard_map/attend_image/pallas_call | solution.py:317
  82.1 1.4 %normalize.1 = f32[1,1]{1,0:T(1,128)} custom-call(f32[32,128]{1,0:T(8,128)} %bitcast.10.every_ref), custom_call_target="tpu_custom_call" | custom-call | bytes 3500000 | tf_op jit(solution)/shard_map/normalize/pallas_call | solution.py:452
  (14 shorter events, 0.0 us)
Async XLA Ops:
  0.6 7.6 %collective-permute-start.5 = (bf16[8,128,2048]{2,1,0:T(8,128)(2,1)}, bf16[8,128,2048]{2,1,0:T(8,128)(2,1)}, u32[]{:S(2)}, u32[]{:S(2)}) collective-permute-start(bf16[8,128,2048]{2,1,0:T(8,128)(2,1)} %bitcast.17), channel_id=1, source_target_pairs={{0,1},{1,0},{2,3},{3,2},{4,5},{5,4},{6,7},{7,6},{8,9},{9,8},{10,11... | collective-permute-start | bytes 12582920 | tf_op jit(solution)/shard_map/ppermute | solution.py:425
  1.1 13.1 %collective-permute-start.2 = (bf16[512,256]{1,0:T(8,128)(2,1)}, bf16[512,256]{1,0:T(8,128)(2,1)}, u32[]{:S(2)}, u32[]{:S(2)}) collective-permute-start(bf16[512,256]{1,0:T(8,128)(2,1)} %bitcast.25), channel_id=1, source_target_pairs={{0,4},{1,5},{2,6},{3,7},{4,0},{5,1},{6,2},{7,3},{8,12},{9,13},{10,... | collective-permute-start | bytes 786440 | tf_op jit(solution)/shard_map/ppermute | solution.py:425
  3.7 10.5 %collective-permute-start.1 = (bf16[512,256]{1,0:T(8,128)(2,1)}, bf16[512,256]{1,0:T(8,128)(2,1)}, u32[]{:S(2)}, u32[]{:S(2)}) collective-permute-start(bf16[512,256]{1,0:T(8,128)(2,1)} %bitcast.26), channel_id=1, source_target_pairs={{0,2},{1,3},{2,0},{3,1},{4,6},{5,7},{6,4},{7,5},{8,10},{9,11},{10,... | collective-permute-start | bytes 786440 | tf_op jit(solution)/shard_map/ppermute | solution.py:425
  5.2 12.9 %collective-permute-start.3 = (bf16[512,256]{1,0:T(8,128)(2,1)}, bf16[512,256]{1,0:T(8,128)(2,1)}, u32[]{:S(2)}, u32[]{:S(2)}) collective-permute-start(bf16[512,256]{1,0:T(8,128)(2,1)} %bitcast.27), channel_id=1, source_target_pairs={{0,6},{1,7},{2,4},{3,5},{4,2},{5,3},{6,0},{7,1},{8,14},{9,15},{10,... | collective-permute-start | bytes 786440 | tf_op jit(solution)/shard_map/ppermute | solution.py:425
  5.3 3.0 %collective-permute-start.4 = (s32[8]{0:T(128)}, s32[8]{0:T(128)}, u32[]{:S(2)}, u32[]{:S(2)}) collective-permute-start(s32[8]{0:T(128)} %bitcast.33), channel_id=1, source_target_pairs={{0,1},{1,0},{2,3},{3,2},{4,5},{5,4},{6,7},{7,6},{8,9},{9,8},{10,11... | collective-permute-start | bytes 104 | tf_op jit(solution)/shard_map/ppermute | solution.py:425
  14.3 32.5 %collective-permute-start.14 = (bf16[2,128,1280]{2,1,0:T(8,128)(2,1)}, bf16[2,128,1280]{2,1,0:T(8,128)(2,1)}, u32[]{:S(2)}, u32[]{:S(2)}) collective-permute-start(bf16[2,128,1280]{2,1,0:T(8,128)(2,1)} %get-tuple-element.38), channel_id=1, source_target_pairs={{0,6},{1,7},{2,4},{3,5},{4,2},{5,3},{6,0},{7,1},{8,14},{9,15},{10,... | collective-permute-start | bytes 1966088 | tf_op jit(solution)/shard_map/ppermute | solution.py:425
  18.2 1.9 %collective-permute-start = (bf16[512,256]{1,0:T(8,128)(2,1)}, bf16[512,256]{1,0:T(8,128)(2,1)}, u32[]{:S(2)}, u32[]{:S(2)}) collective-permute-start(bf16[512,256]{1,0:T(8,128)(2,1)} %bitcast.28), channel_id=1, source_target_pairs={{0,1},{1,0},{2,3},{3,2},{4,5},{5,4},{6,7},{7,6},{8,9},{9,8},{10,11... | collective-permute-start | bytes 786440 | tf_op jit(solution)/shard_map/ppermute | solution.py:425
  18.2 2.7 %collective-permute-start.6 = (bf16[512,256]{1,0:T(8,128)(2,1)}, bf16[512,256]{1,0:T(8,128)(2,1)}, u32[]{:S(2)}, u32[]{:S(2)}) collective-permute-start(bf16[512,256]{1,0:T(8,128)(2,1)} %collective-permute-done.1.rest_2_), channel_id=1, source_target_pairs={{0,1},{1,0},{2,3},{3,2},{4,5},{5,4},{6,7},{7,6},{8,9},{9,8},{10,11... | collective-permute-start | bytes 786440 | tf_op jit(solution)/shard_map/ppermute | solution.py:425
  18.7 3.5 %collective-permute-start.7 = (bf16[512,256]{1,0:T(8,128)(2,1)}, bf16[512,256]{1,0:T(8,128)(2,1)}, u32[]{:S(2)}, u32[]{:S(2)}) collective-permute-start(bf16[512,256]{1,0:T(8,128)(2,1)} %collective-permute-done.2.rest_4_), channel_id=1, source_target_pairs={{0,1},{1,0},{2,3},{3,2},{4,5},{5,4},{6,7},{7,6},{8,9},{9,8},{10,11... | collective-permute-start | bytes 786440 | tf_op jit(solution)/shard_map/ppermute | solution.py:425
  18.7 4.9 %collective-permute-start.8 = (bf16[512,256]{1,0:T(8,128)(2,1)}, bf16[512,256]{1,0:T(8,128)(2,1)}, u32[]{:S(2)}, u32[]{:S(2)}) collective-permute-start(bf16[512,256]{1,0:T(8,128)(2,1)} %collective-permute-done.3.rest_6_), channel_id=1, source_target_pairs={{0,1},{1,0},{2,3},{3,2},{4,5},{5,4},{6,7},{7,6},{8,9},{9,8},{10,11... | collective-permute-start | bytes 786440 | tf_op jit(solution)/shard_map/ppermute | solution.py:425
  20.0 27.8 %collective-permute-start.13 = (bf16[2,128,1280]{2,1,0:T(8,128)(2,1)}, bf16[2,128,1280]{2,1,0:T(8,128)(2,1)}, u32[]{:S(2)}, u32[]{:S(2)}) collective-permute-start(bf16[2,128,1280]{2,1,0:T(8,128)(2,1)} %get-tuple-element.36), channel_id=1, source_target_pairs={{0,4},{1,5},{2,6},{3,7},{4,0},{5,1},{6,2},{7,3},{8,12},{9,13},{10,... | collective-permute-start | bytes 1966088 | tf_op jit(solution)/shard_map/ppermute | solution.py:425
  20.8 27.9 %collective-permute-start.12 = (bf16[2,128,1280]{2,1,0:T(8,128)(2,1)}, bf16[2,128,1280]{2,1,0:T(8,128)(2,1)}, u32[]{:S(2)}, u32[]{:S(2)}) collective-permute-start(bf16[2,128,1280]{2,1,0:T(8,128)(2,1)} %get-tuple-element.34), channel_id=1, source_target_pairs={{0,2},{1,3},{2,0},{3,1},{4,6},{5,7},{6,4},{7,5},{8,10},{9,11},{10,... | collective-permute-start | bytes 1966088 | tf_op jit(solution)/shard_map/ppermute | solution.py:425
  22.2 39.4 %collective-permute-start.9 = (bf16[2,128,768]{2,1,0:T(8,128)(2,1)}, bf16[2,128,768]{2,1,0:T(8,128)(2,1)}, u32[]{:S(2)}, u32[]{:S(2)}) collective-permute-start(bf16[2,128,768]{2,1,0:T(8,128)(2,1)} %get-tuple-element.29), channel_id=1, source_target_pairs={{0,2},{1,3},{2,0},{3,1},{4,6},{5,7},{6,4},{7,5},{8,10},{9,11},{10,... | collective-permute-start | bytes 1179656 | tf_op jit(solution)/shard_map/ppermute | solution.py:425
  23.6 38.0 %collective-permute-start.10 = (bf16[2,128,768]{2,1,0:T(8,128)(2,1)}, bf16[2,128,768]{2,1,0:T(8,128)(2,1)}, u32[]{:S(2)}, u32[]{:S(2)}) collective-permute-start(bf16[2,128,768]{2,1,0:T(8,128)(2,1)} %get-tuple-element.30), channel_id=1, source_target_pairs={{0,4},{1,5},{2,6},{3,7},{4,0},{5,1},{6,2},{7,3},{8,12},{9,13},{10,... | collective-permute-start | bytes 1179656 | tf_op jit(solution)/shard_map/ppermute | solution.py:425
  46.8 17.6 %collective-permute-start.11 = (bf16[2,128,768]{2,1,0:T(8,128)(2,1)}, bf16[2,128,768]{2,1,0:T(8,128)(2,1)}, u32[]{:S(2)}, u32[]{:S(2)}) collective-permute-start(bf16[2,128,768]{2,1,0:T(8,128)(2,1)} %get-tuple-element.32), channel_id=1, source_target_pairs={{0,6},{1,7},{2,4},{3,5},{4,2},{5,3},{6,0},{7,1},{8,14},{9,15},{10,... | collective-permute-start | bytes 1179656 | tf_op jit(solution)/shard_map/ppermute | solution.py:425
  68.2 13.9 %all-to-all-start = ((f32[32,1,128]{2,1,0:T(1,128)}), f32[32,1,128]{2,1,0:T(1,128)}, u32[]{:S(2)}, u32[]{:S(2)}) async-start(f32[32,1,128]{2,1,0:T(1,128)} %bitcast.32), calls=%async_computation | async-start | bytes 32768 | tf_op jit(solution)/shard_map/all_to_all | solution.py:450

commit v6 on v5

--- a/solution.py
+++ b/solution.py
@@ -28,35 +28,25 @@
 PARAMS = pltpu.CompilerParams(vmem_limit_bytes=64 * 2**20)
 
 
-def slot_of(judge, routes):
-    tile, found = jnp.int32(0), jnp.bool_(False)
-    for s in range(routes.shape[0]):
-        here = routes[s] == judge
-        tile, found = jnp.where(here, s, tile), found | here
-    return tile, found
-
-
-def pack_kernel(chips, parts, me, routes, mate_routes, *rest):
+def pack_kernel(chips, parts, held, mate_held, *rest):
     tiles, outs = rest[: 2 * chips], list(rest[2 * chips :])
-    chip, core = me[0] // 2, me[0] % 2
     top = (lax.broadcasted_iota(jnp.int32, (16, HD), 0) == 0) & (pl.program_id(0) == 0)
     for head_from, heads in parts:
         for offset in range(chips):
             out = outs.pop(0)
-            for n, held in enumerate((routes, mate_routes)):
+            for n, table in enumerate((held, mate_held)):
                 tile = tiles[2 * offset + n]
-                found = slot_of(2 * (chip ^ offset) + core, held)[1]
                 for i in range(2 * heads):
                     first = (i % 2 * KVH + head_from + i // 2) * HD
                     out[n, :, i * HD : (i + 1) * HD] = tile[0, :, first : first + HD]
-                mark = top & jnp.logical_not(found)
+                mark = top & (table[offset] < 0)
                 kept = tile[0, :16, head_from * HD : (head_from + 1) * HD]
                 out[n, :16, :HD] = jnp.where(mark, jnp.full_like(kept, EMPTY), kept)
 
 
-def pack(parts, chips, me, routes, mate_routes, patch, mate_patch):
+def pack(parts, chips, held, mate_held, patch, mate_patch):
     tile_rows, width = patch.shape[1:]
-    rows = tile_rows // 4
+    rows = tile_rows // 2
     shapes, specs, sources = [], [], []
     for _, heads in parts:
         shapes += [(2, tile_rows, 2 * heads * HD)] * chips
@@ -64,16 +54,15 @@
     for offset in range(chips):
         for n in range(2):
 
-            def source(r, me, *held, offset=offset, n=n):
-                judge = 2 * ((me[0] // 2) ^ offset) + me[0] % 2
-                return slot_of(judge, held[n])[0], r, 0
+            def source(r, *tables, offset=offset, n=n):
+                return jnp.maximum(tables[n][offset], 0), r, 0
 
             sources.append(pl.BlockSpec((1, rows, width), source))
     return pl.pallas_call(
         functools.partial(pack_kernel, chips, parts),
         out_shape=[jax.ShapeDtypeStruct(shape, patch.dtype) for shape in shapes],
         grid_spec=pltpu.PrefetchScalarGridSpec(
-            num_scalar_prefetch=3,
+            num_scalar_prefetch=2,
             grid=(tile_rows // rows,),
             in_specs=sources,
             out_specs=specs,
@@ -81,7 +70,7 @@
         compiler_params=PARAMS,
         cost_estimate=lasting(5),
         name="pack_tiles",
-    )(me, routes, mate_routes, *([patch, mate_patch] * chips))
+    )(held, mate_held, *([patch, mate_patch] * chips))
 
 
 def pipelined(scores, finish):
@@ -424,11 +413,17 @@
     def swap(x, k):
         return lax.ppermute(x, "slot", [(i, i ^ k) for i in range(slot_count)])
 
-    mate_patch, mate_routes = swap(patch_kv[0], 1), swap(routes[0], 1)
+    slot = jnp.arange(routes.shape[1], dtype=jnp.int32)
+    judges = 2 * (jnp.arange(chips, dtype=jnp.int32) ^ (me // 2)) + me % 2
+    held, for_mate = [
+        jnp.max(jnp.where(routes == judge[:, None], slot, -1), axis=1)
+        for judge in (judges, judges ^ 1)
+    ]
+    mate_patch, mate_held = swap(patch_kv[0], 1), swap(for_mate, 1)
     near = [prefix_kv[0]] + [swap(prefix_kv[0], 2 * offset) for offset in range(1, chips)]
-    buffers = pack(PARTS, chips, me, routes[0], mate_routes, patch_kv[0], mate_patch)
-    held = lax.optimization_barrier((near[1:], buffers[0]))[0]
-    far = [swap(block, 1) for block in [near[0], *held]]
+    buffers = pack(PARTS, chips, held, mate_held, patch_kv[0], mate_patch)
+    come = lax.optimization_barrier((near[1:], buffers[0]))[0]
+    far = [swap(block, 1) for block in [near[0], *come]]
     first, second = list(buffers[:chips]), list(buffers[chips:])
     for n in range(1, chips):
         first[n] = lax.optimization_barrier((first[n], near[:-1] if n == chips - 1 else near))[0]

time: 83.8 us -> 82.7 us (0.987)
  waiting for transfers between devices: 7.69 us -> 5.7 us
  other arithmetic: 0 us -> 1.39 us
    ppermute x15, waiting for transfers between devices: 7.69 us -> 5.7 us  [swap(): return lax.ppermute(x, 'slot', [(i, i ^ k) for i in range(slot_count)])]
    reduce_max x0 -> x1, other arithmetic: none -> 1.38 us  [per_device(): jnp.max(jnp.where(routes == judge[:, None], slot, -1), axis=1)]
  transfers between devices with their start and end apart: 16 -> 16, of which waited for: 4 -> 6; matrix products, arithmetic and copies ran while one was open for 0% -> 2% of each run, Pallas kernels for 58% -> 57%
where the time goes in v6:
time: 82.7 us; the launch traced here: 82.5 us
  Pallas kernels  52.4 us (63%)
  starting transfers between devices  21.6 us (26%)
  waiting for transfers between devices  5.7 us (7%)
  other arithmetic  1.39 us (2%)
  between operations  1.36 us (2%)
    pallas_call x1, Pallas kernels, attend_text(): pl.pallas_call(functools.partial(text_kernel, len(prefix)), out_shape=[ja...  22.1 us
    pallas_call x2, Pallas kernels, attend_image(): pl.pallas_call(functools.partial(image_kernel, 2 * chips, kept, len(tiles...  20 us
    ppermute x15, starting transfers between devices, swap(): return lax.ppermute(x, 'slot', [(i, i ^ k) for i in range(slot_count)])  15.1 us
    all_to_all x1, starting transfers between devices, per_device(): every = lax.all_to_all(shares, ('prompt', 'slot'), 0, 0, tiled=True)  6.48 us
    ppermute x15, waiting for transfers between devices, swap(): return lax.ppermute(x, 'slot', [(i, i ^ k) for i in range(slot_count)])  5.7 us
    pallas_call x1, Pallas kernels, pack(): pl.pallas_call(functools.partial(pack_kernel, chips, parts), out_shape=[j...  5.29 us
    pallas_call x1, Pallas kernels, last_rows(): pl.pallas_call(functools.partial(last_kernel, 2 * chips, kept, len(tiles)...  3.75 us
  transfers between devices with their start and end apart: 16, of which 6 were waited for; matrix products, arithmetic and copies ran while one was open for 2% of the time, Pallas kernels for 57%

profile of v6, /device:TPU:0, one launch (start us, length us, event | category | flops | bytes accessed | tf_op | source)
XLA Modules:
  0.0 82.5 jit_solution(7789310979457823608)
XLA Ops:
  0.6 0.5 collective-permute-start.5
  1.1 2.6 %collective-permute-start.2 = (bf16[512,256]{1,0:T(8,128)(2,1)}, bf16[512,256]{1,0:T(8,128)(2,1)}, u32[]{:S(2)}, u32[]{:S(2)}) collective-permute-start(bf16[512,256]{1,0:T(8,128)(2,1)} %bitcast.27), channel_id=1, source_target_pairs={{0,4},{1,5},{2,6},{3,7},{4,0},{5,1},{6,2},{7,3},{8,12},{9,13},{10,... | collective-permute-start | bytes 786440 | tf_op jit(solution)/shard_map/ppermute | solution.py:414
  3.7 1.5 %collective-permute-start.1 = (bf16[512,256]{1,0:T(8,128)(2,1)}, bf16[512,256]{1,0:T(8,128)(2,1)}, u32[]{:S(2)}, u32[]{:S(2)}) collective-permute-start(bf16[512,256]{1,0:T(8,128)(2,1)} %bitcast.28), channel_id=1, source_target_pairs={{0,2},{1,3},{2,0},{3,1},{4,6},{5,7},{6,4},{7,5},{8,10},{9,11},{10,... | collective-permute-start | bytes 786440 | tf_op jit(solution)/shard_map/ppermute | solution.py:414
  5.3 1.4 %select_reduce_fusion = (s32[4]{0:T(128)S(1)}, s32[4]{0:T(128)}) fusion(s32[8]{0:T(128)} %bitcast.35, s32[4]{0:T(128)S(1)} %get-tuple-element.44, s32[4]{0:T(128)S(1)} %get-tuple-element.45), kind=kLoop, calls=%fused_computation | loop fusion | flops 184 | bytes 96 | tf_op jit(solution)/shard_map/reduce_max | solution.py:419
  6.7 1.3 %collective-permute-done.4.mate_held = s32[4]{0:T(128)} collective-permute-done((s32[4]{0:T(128)S(1)}, s32[4]{0:T(128)}, u32[]{:S(2)}, u32[]{:S(2)}) %collective-permute-start.4) | collective-permute-done | bytes 48 | tf_op jit(solution)/shard_map/ppermute | solution.py:414
  7.9 0.3 collective-permute-done.5.rest_1_.rest_3_.rest_5_.rest_7_
  8.3 5.3 %pack_tiles.1 = (bf16[2,128,1280]{2,1,0:T(8,128)(2,1)}, bf16[2,128,1280]{2,1,0:T(8,128)(2,1)}, bf16[2,128,1280]{2,1,0:T(8,128)(2,1)}, bf16[2,128,1280]{2,1,0:T(8...) custom-call(s32[4]{0:T(128)} %get-tuple-element.43.held, ...), custom_call_target="tpu_custom_call" | custom-call | bytes 17500000 | tf_op jit(solution)/shard_map/pack_tiles/pallas_call | solution.py:61
  13.6 3.4 %collective-permute-start.14 = (bf16[2,128,1280]{2,1,0:T(8,128)(2,1)}, bf16[2,128,1280]{2,1,0:T(8,128)(2,1)}, u32[]{:S(2)}, u32[]{:S(2)}) collective-permute-start(bf16[2,128,1280]{2,1,0:T(8,128)(2,1)} %get-tuple-element.38), channel_id=1, source_target_pairs={{0,6},{1,7},{2,4},{3,5},{4,2},{5,3},{6,0},{7,1},{8,14},{9,15},{10,... | collective-permute-start | bytes 1966088 | tf_op jit(solution)/shard_map/ppermute | solution.py:414
  17.0 0.2 collective-permute-start
  17.2 0.6 collective-permute-done.3.rest_6_
  17.8 0.5 collective-permute-start.7
  18.3 0.6 collective-permute-done.rest_1_
  18.9 1.2 %collective-permute-start.13 = (bf16[2,128,1280]{2,1,0:T(8,128)(2,1)}, bf16[2,128,1280]{2,1,0:T(8,128)(2,1)}, u32[]{:S(2)}, u32[]{:S(2)}) collective-permute-start(bf16[2,128,1280]{2,1,0:T(8,128)(2,1)} %get-tuple-element.36), channel_id=1, source_target_pairs={{0,4},{1,5},{2,6},{3,7},{4,0},{5,1},{6,2},{7,3},{8,12},{9,13},{10,... | collective-permute-start | bytes 1966088 | tf_op jit(solution)/shard_map/ppermute | solution.py:414
  20.0 1.5 %collective-permute-start.12 = (bf16[2,128,1280]{2,1,0:T(8,128)(2,1)}, bf16[2,128,1280]{2,1,0:T(8,128)(2,1)}, u32[]{:S(2)}, u32[]{:S(2)}) collective-permute-start(bf16[2,128,1280]{2,1,0:T(8,128)(2,1)} %get-tuple-element.34), channel_id=1, source_target_pairs={{0,2},{1,3},{2,0},{3,1},{4,6},{5,7},{6,4},{7,5},{8,10},{9,11},{10,... | collective-permute-start | bytes 1966088 | tf_op jit(solution)/shard_map/ppermute | solution.py:414
  22.2 0.6 collective-permute-start.9
  22.8 1.4 %collective-permute-start.10 = (bf16[2,128,768]{2,1,0:T(8,128)(2,1)}, bf16[2,128,768]{2,1,0:T(8,128)(2,1)}, u32[]{:S(2)}, u32[]{:S(2)}) collective-permute-start(bf16[2,128,768]{2,1,0:T(8,128)(2,1)} %get-tuple-element.30), channel_id=1, source_target_pairs={{0,4},{1,5},{2,6},{3,7},{4,0},{5,1},{6,2},{7,3},{8,12},{9,13},{10,... | collective-permute-start | bytes 1179656 | tf_op jit(solution)/shard_map/ppermute | solution.py:414
  24.1 22.1 %attend_text.1 = (f32[256,8192]{1,0:T(8,128)}, f32[256,1024]{1,0:T(8,128)}, bf16[8,768,256]{2,1,0:T(8,128)(2,1)}) custom-call(s32[1]{0:T(128)} %bitcast.1.me, s32[1]{0:T(128)S(6)} %copy.13.length.rest_4_, bf16[256,8192]{1,0:T(8,128)(2,1)} %bitcast.14, bf16[512,256]{1,0:T(8,128)(2,1)} %bitcast.31, bf16[512,256]{1,0:T(8,128)(2,1)} %collective-permute-done.rest_1_, ...), custom_call_target="tpu_custom_call" | custom-call | bytes 73500000 | tf_op jit(solution)/shard_map/attend_text/pallas_call | solution.py:141
  46.2 1.7 %collective-permute-start.11 = (bf16[2,128,768]{2,1,0:T(8,128)(2,1)}, bf16[2,128,768]{2,1,0:T(8,128)(2,1)}, u32[]{:S(2)}, u32[]{:S(2)}) collective-permute-start(bf16[2,128,768]{2,1,0:T(8,128)(2,1)} %get-tuple-element.32), channel_id=1, source_target_pairs={{0,6},{1,7},{2,4},{3,5},{4,2},{5,3},{6,0},{7,1},{8,14},{9,15},{10,... | collective-permute-start | bytes 1179656 | tf_op jit(solution)/shard_map/ppermute | solution.py:414
  47.9 12.8 %attend_image.2 = (bf16[256,8192]{1,0:T(8,128)(2,1)}, f32[8,128]{1,0:T(8,128)}) custom-call(bf16[256,8192]{1,0:T(8,128)(2,1)} %bitcast.15, f32[256,8192]{1,0:T(8,128)} %get-tuple-element.26.acc_ref, f32[256,1024]{1,0:T(8,128)} %get-tuple-element.27.stat_ref, bf16[2,128,1280]{2,1,0:T(8,128)(2,1)} %get-tuple-element.22.rest_0_, ...), custom_call_target="tpu_custom_call" | custom-call | bytes 35000000 | tf_op jit(solution)/shard_map/attend_image/pallas_call | solution.py:306
  60.7 2.9 %collective-permute-done.11.rest_3_ = bf16[2,128,768]{2,1,0:T(8,128)(2,1)} collective-permute-done((bf16[2,128,768]{2,1,0:T(8,128)(2,1)}, bf16[2,128,768]{2,1,0:T(8,128)(2,1)}, u32[]{:S(2)}, u32[]{:S(2)}) %collective-permute-start.11) | collective-permute-done | bytes 393248 | tf_op jit(solution)/shard_map/ppermute | solution.py:414
  63.6 3.7 %last_rows.1 = f32[32,128]{1,0:T(8,128)} custom-call(s32[1]{0:T(128)S(6)} %copy.13.length.rest_4_, bf16[256,8192]{1,0:T(8,128)(2,1)} %bitcast.17, f32[64,128]{1,0:T(8,128)} %bitcast.33, bf16[8,768,256]{2,1,0:T(8,128)(2,1)} %get-tuple-element.39.rest_7_.kv_ref, bf16[2,128,768]{2,1,0:T(8,128)(2,1)} %get-tuple-element.28.rest_0_, ...), custom_call_target="tpu_custom_call" | custom-call | bytes 10500000 | tf_op jit(solution)/shard_map/last_rows/pallas_call | solution.py:378
  67.4 6.5 %all-to-all-start = ((f32[32,1,128]{2,1,0:T(1,128)}), f32[32,1,128]{2,1,0:T(1,128)}, u32[]{:S(2)}, u32[]{:S(2)}) async-start(f32[32,1,128]{2,1,0:T(1,128)} %bitcast.34), calls=%async_computation | async-start | bytes 32768 | tf_op jit(solution)/shard_map/all_to_all | solution.py:445
  73.9 7.2 %attend_image.3 = bf16[256,8192]{1,0:T(8,128)(2,1)} custom-call(bf16[256,8192]{1,0:T(8,128)(2,1)} %bitcast.18, f32[256,8192]{1,0:T(8,128)} %get-tuple-element.26.acc_ref, f32[256,1024]{1,0:T(8,128)} %get-tuple-element.27.stat_ref, bf16[2,128,768]{2,1,0:T(8,128)(2,1)} %get-tuple-element.28.rest_0_, ...), custom_call_target="tpu_custom_call", output_to_operand_aliasing={{}: (7, {})} | custom-call | bytes 21000000 | tf_op jit(solution)/shard_map/attend_image/pallas_call | solution.py:306
  81.1 1.4 %normalize.1 = f32[1,1]{1,0:T(1,128)} custom-call(f32[32,128]{1,0:T(8,128)} %bitcast.12.every_ref), custom_call_target="tpu_custom_call" | custom-call | bytes 3500000 | tf_op jit(solution)/shard_map/normalize/pallas_call | solution.py:447
  (16 shorter events, 0.1 us)
Async XLA Ops:
  0.6 7.6 %collective-permute-start.5 = (bf16[8,128,2048]{2,1,0:T(8,128)(2,1)}, bf16[8,128,2048]{2,1,0:T(8,128)(2,1)}, u32[]{:S(2)}, u32[]{:S(2)}) collective-permute-start(bf16[8,128,2048]{2,1,0:T(8,128)(2,1)} %bitcast.19), channel_id=1, source_target_pairs={{0,1},{1,0},{2,3},{3,2},{4,5},{5,4},{6,7},{7,6},{8,9},{9,8},{10,11... | collective-permute-start | bytes 12582920 | tf_op jit(solution)/shard_map/ppermute | solution.py:414
  1.1 12.4 %collective-permute-start.2 = (bf16[512,256]{1,0:T(8,128)(2,1)}, bf16[512,256]{1,0:T(8,128)(2,1)}, u32[]{:S(2)}, u32[]{:S(2)}) collective-permute-start(bf16[512,256]{1,0:T(8,128)(2,1)} %bitcast.27), channel_id=1, source_target_pairs={{0,4},{1,5},{2,6},{3,7},{4,0},{5,1},{6,2},{7,3},{8,12},{9,13},{10,... | collective-permute-start | bytes 786440 | tf_op jit(solution)/shard_map/ppermute | solution.py:414
  3.7 9.8 %collective-permute-start.1 = (bf16[512,256]{1,0:T(8,128)(2,1)}, bf16[512,256]{1,0:T(8,128)(2,1)}, u32[]{:S(2)}, u32[]{:S(2)}) collective-permute-start(bf16[512,256]{1,0:T(8,128)(2,1)} %bitcast.28), channel_id=1, source_target_pairs={{0,2},{1,3},{2,0},{3,1},{4,6},{5,7},{6,4},{7,5},{8,10},{9,11},{10,... | collective-permute-start | bytes 786440 | tf_op jit(solution)/shard_map/ppermute | solution.py:414
  5.2 12.5 %collective-permute-start.3 = (bf16[512,256]{1,0:T(8,128)(2,1)}, bf16[512,256]{1,0:T(8,128)(2,1)}, u32[]{:S(2)}, u32[]{:S(2)}) collective-permute-start(bf16[512,256]{1,0:T(8,128)(2,1)} %bitcast.29), channel_id=1, source_target_pairs={{0,6},{1,7},{2,4},{3,5},{4,2},{5,3},{6,0},{7,1},{8,14},{9,15},{10,... | collective-permute-start | bytes 786440 | tf_op jit(solution)/shard_map/ppermute | solution.py:414
  6.7 1.3 %collective-permute-start.4 = (s32[4]{0:T(128)S(1)}, s32[4]{0:T(128)}, u32[]{:S(2)}, u32[]{:S(2)}) collective-permute-start(s32[4]{0:T(128)S(1)} %get-tuple-element.42), channel_id=1, source_target_pairs={{0,1},{1,0},{2,3},{3,2},{4,5},{5,4},{6,7},{7,6},{8,9},{9,8},{10,11... | collective-permute-start | bytes 56 | tf_op jit(solution)/shard_map/ppermute | solution.py:414
  13.6 32.6 %collective-permute-start.14 = (bf16[2,128,1280]{2,1,0:T(8,128)(2,1)}, bf16[2,128,1280]{2,1,0:T(8,128)(2,1)}, u32[]{:S(2)}, u32[]{:S(2)}) collective-permute-start(bf16[2,128,1280]{2,1,0:T(8,128)(2,1)} %get-tuple-element.38), channel_id=1, source_target_pairs={{0,6},{1,7},{2,4},{3,5},{4,2},{5,3},{6,0},{7,1},{8,14},{9,15},{10,... | collective-permute-start | bytes 1966088 | tf_op jit(solution)/shard_map/ppermute | solution.py:414
  17.0 1.9 %collective-permute-start = (bf16[512,256]{1,0:T(8,128)(2,1)}, bf16[512,256]{1,0:T(8,128)(2,1)}, u32[]{:S(2)}, u32[]{:S(2)}) collective-permute-start(bf16[512,256]{1,0:T(8,128)(2,1)} %bitcast.30), channel_id=1, source_target_pairs={{0,1},{1,0},{2,3},{3,2},{4,5},{5,4},{6,7},{7,6},{8,9},{9,8},{10,11... | collective-permute-start | bytes 786440 | tf_op jit(solution)/shard_map/ppermute | solution.py:414
  17.8 2.3 %collective-permute-start.6 = (bf16[512,256]{1,0:T(8,128)(2,1)}, bf16[512,256]{1,0:T(8,128)(2,1)}, u32[]{:S(2)}, u32[]{:S(2)}) collective-permute-start(bf16[512,256]{1,0:T(8,128)(2,1)} %collective-permute-done.1.rest_2_), channel_id=1, source_target_pairs={{0,1},{1,0},{2,3},{3,2},{4,5},{5,4},{6,7},{7,6},{8,9},{9,8},{10,11... | collective-permute-start | bytes 786440 | tf_op jit(solution)/shard_map/ppermute | solution.py:414
  17.8 4.4 %collective-permute-start.7 = (bf16[512,256]{1,0:T(8,128)(2,1)}, bf16[512,256]{1,0:T(8,128)(2,1)}, u32[]{:S(2)}, u32[]{:S(2)}) collective-permute-start(bf16[512,256]{1,0:T(8,128)(2,1)} %collective-permute-done.2.rest_4_), channel_id=1, source_target_pairs={{0,1},{1,0},{2,3},{3,2},{4,5},{5,4},{6,7},{7,6},{8,9},{9,8},{10,11... | collective-permute-start | bytes 786440 | tf_op jit(solution)/shard_map/ppermute | solution.py:414
  18.3 4.5 %collective-permute-start.8 = (bf16[512,256]{1,0:T(8,128)(2,1)}, bf16[512,256]{1,0:T(8,128)(2,1)}, u32[]{:S(2)}, u32[]{:S(2)}) collective-permute-start(bf16[512,256]{1,0:T(8,128)(2,1)} %collective-permute-done.3.rest_6_), channel_id=1, source_target_pairs={{0,1},{1,0},{2,3},{3,2},{4,5},{5,4},{6,7},{7,6},{8,9},{9,8},{10,11... | collective-permute-start | bytes 786440 | tf_op jit(solution)/shard_map/ppermute | solution.py:414
  18.9 29.0 %collective-permute-start.13 = (bf16[2,128,1280]{2,1,0:T(8,128)(2,1)}, bf16[2,128,1280]{2,1,0:T(8,128)(2,1)}, u32[]{:S(2)}, u32[]{:S(2)}) collective-permute-start(bf16[2,128,1280]{2,1,0:T(8,128)(2,1)} %get-tuple-element.36), channel_id=1, source_target_pairs={{0,4},{1,5},{2,6},{3,7},{4,0},{5,1},{6,2},{7,3},{8,12},{9,13},{10,... | collective-permute-start | bytes 1966088 | tf_op jit(solution)/shard_map/ppermute | solution.py:414
  20.0 27.9 %collective-permute-start.12 = (bf16[2,128,1280]{2,1,0:T(8,128)(2,1)}, bf16[2,128,1280]{2,1,0:T(8,128)(2,1)}, u32[]{:S(2)}, u32[]{:S(2)}) collective-permute-start(bf16[2,128,1280]{2,1,0:T(8,128)(2,1)} %get-tuple-element.34), channel_id=1, source_target_pairs={{0,2},{1,3},{2,0},{3,1},{4,6},{5,7},{6,4},{7,5},{8,10},{9,11},{10,... | collective-permute-start | bytes 1966088 | tf_op jit(solution)/shard_map/ppermute | solution.py:414
  22.2 38.5 %collective-permute-start.9 = (bf16[2,128,768]{2,1,0:T(8,128)(2,1)}, bf16[2,128,768]{2,1,0:T(8,128)(2,1)}, u32[]{:S(2)}, u32[]{:S(2)}) collective-permute-start(bf16[2,128,768]{2,1,0:T(8,128)(2,1)} %get-tuple-element.29), channel_id=1, source_target_pairs={{0,2},{1,3},{2,0},{3,1},{4,6},{5,7},{6,4},{7,5},{8,10},{9,11},{10,... | collective-permute-start | bytes 1179656 | tf_op jit(solution)/shard_map/ppermute | solution.py:414
  22.8 37.9 %collective-permute-start.10 = (bf16[2,128,768]{2,1,0:T(8,128)(2,1)}, bf16[2,128,768]{2,1,0:T(8,128)(2,1)}, u32[]{:S(2)}, u32[]{:S(2)}) collective-permute-start(bf16[2,128,768]{2,1,0:T(8,128)(2,1)} %get-tuple-element.30), channel_id=1, source_target_pairs={{0,4},{1,5},{2,6},{3,7},{4,0},{5,1},{6,2},{7,3},{8,12},{9,13},{10,... | collective-permute-start | bytes 1179656 | tf_op jit(solution)/shard_map/ppermute | solution.py:414
  46.2 17.4 %collective-permute-start.11 = (bf16[2,128,768]{2,1,0:T(8,128)(2,1)}, bf16[2,128,768]{2,1,0:T(8,128)(2,1)}, u32[]{:S(2)}, u32[]{:S(2)}) collective-permute-start(bf16[2,128,768]{2,1,0:T(8,128)(2,1)} %get-tuple-element.32), channel_id=1, source_target_pairs={{0,6},{1,7},{2,4},{3,5},{4,2},{5,3},{6,0},{7,1},{8,14},{9,15},{10,... | collective-permute-start | bytes 1179656 | tf_op jit(solution)/shard_map/ppermute | solution.py:414
  67.4 13.7 %all-to-all-start = ((f32[32,1,128]{2,1,0:T(1,128)}), f32[32,1,128]{2,1,0:T(1,128)}, u32[]{:S(2)}, u32[]{:S(2)}) async-start(f32[32,1,128]{2,1,0:T(1,128)} %bitcast.34), calls=%async_computation | async-start | bytes 32768 | tf_op jit(solution)/shard_map/all_to_all | solution.py:445

commit v7 on v6

--- a/solution.py
+++ b/solution.py
@@ -74,12 +74,11 @@
 
 
 def pipelined(scores, finish):
-    held = scores(0)
-    for h in range(1, GROUPS):
-        following = scores(h)
-        finish(held, h - 1)
-        held = following
-    finish(held, GROUPS - 1)
+    held = [scores(0), scores(1)]
+    for h in range(GROUPS):
+        if h + 2 < GROUPS:
+            held.append(scores(h + 2))
+        finish(held.pop(0), h)
 
 
 def fill_text(me, length, head, blocks, sk_ref, sv_ref, held, kbuf, vbuf):

time: 82.7 us -> 82.6 us (level)
  transfers between devices with their start and end apart: 16 -> 16, of which waited for: 6 -> 5; matrix products, arithmetic and copies ran while one was open for 2% -> 2% of each run, Pallas kernels for 57% -> 59%
where the time goes in v7:
time: 82.6 us; the launch traced here: 81.9 us
  Pallas kernels  53.1 us (64%)
  starting transfers between devices  20.8 us (25%)
  waiting for transfers between devices  5.19 us (6%)
  other arithmetic  1.39 us (2%)
  between operations  1.36 us (2%)
    pallas_call x1, Pallas kernels, attend_text(): pl.pallas_call(functools.partial(text_kernel, len(prefix)), out_shape=[ja...  22.6 us
    pallas_call x2, Pallas kernels, attend_image(): pl.pallas_call(functools.partial(image_kernel, 2 * chips, kept, len(tiles...  20.1 us
    ppermute x15, starting transfers between devices, swap(): return lax.ppermute(x, 'slot', [(i, i ^ k) for i in range(slot_count)])  15.1 us
    all_to_all x1, starting transfers between devices, per_device(): every = lax.all_to_all(shares, ('prompt', 'slot'), 0, 0, tiled=True)  5.75 us
    pallas_call x1, Pallas kernels, pack(): pl.pallas_call(functools.partial(pack_kernel, chips, parts), out_shape=[j...  5.4 us
    ppermute x15, waiting for transfers between devices, swap(): return lax.ppermute(x, 'slot', [(i, i ^ k) for i in range(slot_count)])  5.19 us
    pallas_call x1, Pallas kernels, last_rows(): pl.pallas_call(functools.partial(last_kernel, 2 * chips, kept, len(tiles)...  3.75 us
  transfers between devices with their start and end apart: 16, of which 5 were waited for; matrix products, arithmetic and copies ran while one was open for 2% of the time, Pallas kernels for 59%

profile of v7, /device:TPU:0, one launch (start us, length us, event | category | flops | bytes accessed | tf_op | source)
XLA Modules:
  0.0 81.9 jit_solution(13616944046575083914)
XLA Ops:
  0.6 0.5 collective-permute-start.5
  1.1 2.6 %collective-permute-start.2 = (bf16[512,256]{1,0:T(8,128)(2,1)}, bf16[512,256]{1,0:T(8,128)(2,1)}, u32[]{:S(2)}, u32[]{:S(2)}) collective-permute-start(bf16[512,256]{1,0:T(8,128)(2,1)} %bitcast.27), channel_id=1, source_target_pairs={{0,4},{1,5},{2,6},{3,7},{4,0},{5,1},{6,2},{7,3},{8,12},{9,13},{10,... | collective-permute-start | bytes 786440 | tf_op jit(solution)/shard_map/ppermute | solution.py:413
  3.7 1.5 %collective-permute-start.1 = (bf16[512,256]{1,0:T(8,128)(2,1)}, bf16[512,256]{1,0:T(8,128)(2,1)}, u32[]{:S(2)}, u32[]{:S(2)}) collective-permute-start(bf16[512,256]{1,0:T(8,128)(2,1)} %bitcast.28), channel_id=1, source_target_pairs={{0,2},{1,3},{2,0},{3,1},{4,6},{5,7},{6,4},{7,5},{8,10},{9,11},{10,... | collective-permute-start | bytes 786440 | tf_op jit(solution)/shard_map/ppermute | solution.py:413
  5.3 1.4 %select_reduce_fusion = (s32[4]{0:T(128)S(1)}, s32[4]{0:T(128)}) fusion(s32[8]{0:T(128)} %bitcast.35, s32[4]{0:T(128)S(1)} %get-tuple-element.44, s32[4]{0:T(128)S(1)} %get-tuple-element.45), kind=kLoop, calls=%fused_computation | loop fusion | flops 184 | bytes 96 | tf_op jit(solution)/shard_map/reduce_max | solution.py:418
  6.7 1.3 %collective-permute-done.4.mate_held = s32[4]{0:T(128)} collective-permute-done((s32[4]{0:T(128)S(1)}, s32[4]{0:T(128)}, u32[]{:S(2)}, u32[]{:S(2)}) %collective-permute-start.4) | collective-permute-done | bytes 48 | tf_op jit(solution)/shard_map/ppermute | solution.py:413
  7.9 0.3 collective-permute-done.5.rest_1_.rest_3_.rest_5_.rest_7_
  8.3 5.4 %pack_tiles.1 = (bf16[2,128,1280]{2,1,0:T(8,128)(2,1)}, bf16[2,128,1280]{2,1,0:T(8,128)(2,1)}, bf16[2,128,1280]{2,1,0:T(8,128)(2,1)}, bf16[2,128,1280]{2,1,0:T(8...) custom-call(s32[4]{0:T(128)} %get-tuple-element.43.held, ...), custom_call_target="tpu_custom_call" | custom-call | bytes 17500000 | tf_op jit(solution)/shard_map/pack_tiles/pallas_call | solution.py:61
  13.7 3.3 %collective-permute-start.14 = (bf16[2,128,1280]{2,1,0:T(8,128)(2,1)}, bf16[2,128,1280]{2,1,0:T(8,128)(2,1)}, u32[]{:S(2)}, u32[]{:S(2)}) collective-permute-start(bf16[2,128,1280]{2,1,0:T(8,128)(2,1)} %get-tuple-element.38), channel_id=1, source_target_pairs={{0,6},{1,7},{2,4},{3,5},{4,2},{5,3},{6,0},{7,1},{8,14},{9,15},{10,... | collective-permute-start | bytes 1966088 | tf_op jit(solution)/shard_map/ppermute | solution.py:413
  17.0 0.4 collective-permute-start
  17.4 0.4 collective-permute-done.3.rest_6_
  17.8 0.5 collective-permute-start.7
  18.3 0.6 collective-permute-done.rest_1_
  18.9 1.2 %collective-permute-start.13 = (bf16[2,128,1280]{2,1,0:T(8,128)(2,1)}, bf16[2,128,1280]{2,1,0:T(8,128)(2,1)}, u32[]{:S(2)}, u32[]{:S(2)}) collective-permute-start(bf16[2,128,1280]{2,1,0:T(8,128)(2,1)} %get-tuple-element.36), channel_id=1, source_target_pairs={{0,4},{1,5},{2,6},{3,7},{4,0},{5,1},{6,2},{7,3},{8,12},{9,13},{10,... | collective-permute-start | bytes 1966088 | tf_op jit(solution)/shard_map/ppermute | solution.py:413
  20.1 1.5 %collective-permute-start.12 = (bf16[2,128,1280]{2,1,0:T(8,128)(2,1)}, bf16[2,128,1280]{2,1,0:T(8,128)(2,1)}, u32[]{:S(2)}, u32[]{:S(2)}) collective-permute-start(bf16[2,128,1280]{2,1,0:T(8,128)(2,1)} %get-tuple-element.34), channel_id=1, source_target_pairs={{0,2},{1,3},{2,0},{3,1},{4,6},{5,7},{6,4},{7,5},{8,10},{9,11},{10,... | collective-permute-start | bytes 1966088 | tf_op jit(solution)/shard_map/ppermute | solution.py:413
  22.2 0.6 collective-permute-start.9
  22.8 1.3 %collective-permute-start.10 = (bf16[2,128,768]{2,1,0:T(8,128)(2,1)}, bf16[2,128,768]{2,1,0:T(8,128)(2,1)}, u32[]{:S(2)}, u32[]{:S(2)}) collective-permute-start(bf16[2,128,768]{2,1,0:T(8,128)(2,1)} %get-tuple-element.30), channel_id=1, source_target_pairs={{0,4},{1,5},{2,6},{3,7},{4,0},{5,1},{6,2},{7,3},{8,12},{9,13},{10,... | collective-permute-start | bytes 1179656 | tf_op jit(solution)/shard_map/ppermute | solution.py:413
  24.1 22.6 %attend_text.1 = (f32[256,8192]{1,0:T(8,128)}, f32[256,1024]{1,0:T(8,128)}, bf16[8,768,256]{2,1,0:T(8,128)(2,1)}) custom-call(s32[1]{0:T(128)} %bitcast.1.me, s32[1]{0:T(128)S(6)} %copy.13.length.rest_4_, bf16[256,8192]{1,0:T(8,128)(2,1)} %bitcast.14, bf16[512,256]{1,0:T(8,128)(2,1)} %bitcast.31, bf16[512,256]{1,0:T(8,128)(2,1)} %collective-permute-done.rest_1_, ...), custom_call_target="tpu_custom_call" | custom-call | bytes 73500000 | tf_op jit(solution)/shard_map/attend_text/pallas_call | solution.py:140
  46.7 1.7 %collective-permute-start.11 = (bf16[2,128,768]{2,1,0:T(8,128)(2,1)}, bf16[2,128,768]{2,1,0:T(8,128)(2,1)}, u32[]{:S(2)}, u32[]{:S(2)}) collective-permute-start(bf16[2,128,768]{2,1,0:T(8,128)(2,1)} %get-tuple-element.32), channel_id=1, source_target_pairs={{0,6},{1,7},{2,4},{3,5},{4,2},{5,3},{6,0},{7,1},{8,14},{9,15},{10,... | collective-permute-start | bytes 1179656 | tf_op jit(solution)/shard_map/ppermute | solution.py:413
  48.4 12.8 %attend_image.2 = (bf16[256,8192]{1,0:T(8,128)(2,1)}, f32[8,128]{1,0:T(8,128)}) custom-call(bf16[256,8192]{1,0:T(8,128)(2,1)} %bitcast.15, f32[256,8192]{1,0:T(8,128)} %get-tuple-element.26.acc_ref, f32[256,1024]{1,0:T(8,128)} %get-tuple-element.27.stat_ref, bf16[2,128,1280]{2,1,0:T(8,128)(2,1)} %get-tuple-element.22.rest_0_, ...), custom_call_target="tpu_custom_call" | custom-call | bytes 35000000 | tf_op jit(solution)/shard_map/attend_image/pallas_call | solution.py:305
  61.2 2.6 %collective-permute-done.11.rest_3_ = bf16[2,128,768]{2,1,0:T(8,128)(2,1)} collective-permute-done((bf16[2,128,768]{2,1,0:T(8,128)(2,1)}, bf16[2,128,768]{2,1,0:T(8,128)(2,1)}, u32[]{:S(2)}, u32[]{:S(2)}) %collective-permute-start.11) | collective-permute-done | bytes 393248 | tf_op jit(solution)/shard_map/ppermute | solution.py:413
  63.8 3.7 %last_rows.1 = f32[32,128]{1,0:T(8,128)} custom-call(s32[1]{0:T(128)S(6)} %copy.13.length.rest_4_, bf16[256,8192]{1,0:T(8,128)(2,1)} %bitcast.17, f32[64,128]{1,0:T(8,128)} %bitcast.33, bf16[8,768,256]{2,1,0:T(8,128)(2,1)} %get-tuple-element.39.rest_7_.kv_ref, bf16[2,128,768]{2,1,0:T(8,128)(2,1)} %get-tuple-element.28.rest_0_, ...), custom_call_target="tpu_custom_call" | custom-call | bytes 10500000 | tf_op jit(solution)/shard_map/last_rows/pallas_call | solution.py:377
  67.6 5.7 %all-to-all-start = ((f32[32,1,128]{2,1,0:T(1,128)}), f32[32,1,128]{2,1,0:T(1,128)}, u32[]{:S(2)}, u32[]{:S(2)}) async-start(f32[32,1,128]{2,1,0:T(1,128)} %bitcast.34), calls=%async_computation | async-start | bytes 32768 | tf_op jit(solution)/shard_map/all_to_all | solution.py:444
  73.3 7.2 %attend_image.3 = bf16[256,8192]{1,0:T(8,128)(2,1)} custom-call(bf16[256,8192]{1,0:T(8,128)(2,1)} %bitcast.18, f32[256,8192]{1,0:T(8,128)} %get-tuple-element.26.acc_ref, f32[256,1024]{1,0:T(8,128)} %get-tuple-element.27.stat_ref, bf16[2,128,768]{2,1,0:T(8,128)(2,1)} %get-tuple-element.28.rest_0_, ...), custom_call_target="tpu_custom_call", output_to_operand_aliasing={{}: (7, {})} | custom-call | bytes 21000000 | tf_op jit(solution)/shard_map/attend_image/pallas_call | solution.py:305
  80.5 1.4 %normalize.1 = f32[1,1]{1,0:T(1,128)} custom-call(f32[32,128]{1,0:T(8,128)} %bitcast.12.every_ref), custom_call_target="tpu_custom_call" | custom-call | bytes 3500000 | tf_op jit(solution)/shard_map/normalize/pallas_call | solution.py:446
  (16 shorter events, 0.1 us)
Async XLA Ops:
  0.6 7.6 %collective-permute-start.5 = (bf16[8,128,2048]{2,1,0:T(8,128)(2,1)}, bf16[8,128,2048]{2,1,0:T(8,128)(2,1)}, u32[]{:S(2)}, u32[]{:S(2)}) collective-permute-start(bf16[8,128,2048]{2,1,0:T(8,128)(2,1)} %bitcast.19), channel_id=1, source_target_pairs={{0,1},{1,0},{2,3},{3,2},{4,5},{5,4},{6,7},{7,6},{8,9},{9,8},{10,11... | collective-permute-start | bytes 12582920 | tf_op jit(solution)/shard_map/ppermute | solution.py:413
  1.1 12.5 %collective-permute-start.2 = (bf16[512,256]{1,0:T(8,128)(2,1)}, bf16[512,256]{1,0:T(8,128)(2,1)}, u32[]{:S(2)}, u32[]{:S(2)}) collective-permute-start(bf16[512,256]{1,0:T(8,128)(2,1)} %bitcast.27), channel_id=1, source_target_pairs={{0,4},{1,5},{2,6},{3,7},{4,0},{5,1},{6,2},{7,3},{8,12},{9,13},{10,... | collective-permute-start | bytes 786440 | tf_op jit(solution)/shard_map/ppermute | solution.py:413
  3.7 9.9 %collective-permute-start.1 = (bf16[512,256]{1,0:T(8,128)(2,1)}, bf16[512,256]{1,0:T(8,128)(2,1)}, u32[]{:S(2)}, u32[]{:S(2)}) collective-permute-start(bf16[512,256]{1,0:T(8,128)(2,1)} %bitcast.28), channel_id=1, source_target_pairs={{0,2},{1,3},{2,0},{3,1},{4,6},{5,7},{6,4},{7,5},{8,10},{9,11},{10,... | collective-permute-start | bytes 786440 | tf_op jit(solution)/shard_map/ppermute | solution.py:413
  5.2 12.5 %collective-permute-start.3 = (bf16[512,256]{1,0:T(8,128)(2,1)}, bf16[512,256]{1,0:T(8,128)(2,1)}, u32[]{:S(2)}, u32[]{:S(2)}) collective-permute-start(bf16[512,256]{1,0:T(8,128)(2,1)} %bitcast.29), channel_id=1, source_target_pairs={{0,6},{1,7},{2,4},{3,5},{4,2},{5,3},{6,0},{7,1},{8,14},{9,15},{10,... | collective-permute-start | bytes 786440 | tf_op jit(solution)/shard_map/ppermute | solution.py:413
  6.7 1.3 %collective-permute-start.4 = (s32[4]{0:T(128)S(1)}, s32[4]{0:T(128)}, u32[]{:S(2)}, u32[]{:S(2)}) collective-permute-start(s32[4]{0:T(128)S(1)} %get-tuple-element.42), channel_id=1, source_target_pairs={{0,1},{1,0},{2,3},{3,2},{4,5},{5,4},{6,7},{7,6},{8,9},{9,8},{10,11... | collective-permute-start | bytes 56 | tf_op jit(solution)/shard_map/ppermute | solution.py:413
  13.7 33.0 %collective-permute-start.14 = (bf16[2,128,1280]{2,1,0:T(8,128)(2,1)}, bf16[2,128,1280]{2,1,0:T(8,128)(2,1)}, u32[]{:S(2)}, u32[]{:S(2)}) collective-permute-start(bf16[2,128,1280]{2,1,0:T(8,128)(2,1)} %get-tuple-element.38), channel_id=1, source_target_pairs={{0,6},{1,7},{2,4},{3,5},{4,2},{5,3},{6,0},{7,1},{8,14},{9,15},{10,... | collective-permute-start | bytes 1966088 | tf_op jit(solution)/shard_map/ppermute | solution.py:413
  17.0 1.9 %collective-permute-start = (bf16[512,256]{1,0:T(8,128)(2,1)}, bf16[512,256]{1,0:T(8,128)(2,1)}, u32[]{:S(2)}, u32[]{:S(2)}) collective-permute-start(bf16[512,256]{1,0:T(8,128)(2,1)} %bitcast.30), channel_id=1, source_target_pairs={{0,1},{1,0},{2,3},{3,2},{4,5},{5,4},{6,7},{7,6},{8,9},{9,8},{10,11... | collective-permute-start | bytes 786440 | tf_op jit(solution)/shard_map/ppermute | solution.py:413
  17.8 2.3 %collective-permute-start.6 = (bf16[512,256]{1,0:T(8,128)(2,1)}, bf16[512,256]{1,0:T(8,128)(2,1)}, u32[]{:S(2)}, u32[]{:S(2)}) collective-permute-start(bf16[512,256]{1,0:T(8,128)(2,1)} %collective-permute-done.1.rest_2_), channel_id=1, source_target_pairs={{0,1},{1,0},{2,3},{3,2},{4,5},{5,4},{6,7},{7,6},{8,9},{9,8},{10,11... | collective-permute-start | bytes 786440 | tf_op jit(solution)/shard_map/ppermute | solution.py:413
  17.8 4.4 %collective-permute-start.7 = (bf16[512,256]{1,0:T(8,128)(2,1)}, bf16[512,256]{1,0:T(8,128)(2,1)}, u32[]{:S(2)}, u32[]{:S(2)}) collective-permute-start(bf16[512,256]{1,0:T(8,128)(2,1)} %collective-permute-done.2.rest_4_), channel_id=1, source_target_pairs={{0,1},{1,0},{2,3},{3,2},{4,5},{5,4},{6,7},{7,6},{8,9},{9,8},{10,11... | collective-permute-start | bytes 786440 | tf_op jit(solution)/shard_map/ppermute | solution.py:413
  18.3 4.5 %collective-permute-start.8 = (bf16[512,256]{1,0:T(8,128)(2,1)}, bf16[512,256]{1,0:T(8,128)(2,1)}, u32[]{:S(2)}, u32[]{:S(2)}) collective-permute-start(bf16[512,256]{1,0:T(8,128)(2,1)} %collective-permute-done.3.rest_6_), channel_id=1, source_target_pairs={{0,1},{1,0},{2,3},{3,2},{4,5},{5,4},{6,7},{7,6},{8,9},{9,8},{10,11... | collective-permute-start | bytes 786440 | tf_op jit(solution)/shard_map/ppermute | solution.py:413
  18.9 29.5 %collective-permute-start.13 = (bf16[2,128,1280]{2,1,0:T(8,128)(2,1)}, bf16[2,128,1280]{2,1,0:T(8,128)(2,1)}, u32[]{:S(2)}, u32[]{:S(2)}) collective-permute-start(bf16[2,128,1280]{2,1,0:T(8,128)(2,1)} %get-tuple-element.36), channel_id=1, source_target_pairs={{0,4},{1,5},{2,6},{3,7},{4,0},{5,1},{6,2},{7,3},{8,12},{9,13},{10,... | collective-permute-start | bytes 1966088 | tf_op jit(solution)/shard_map/ppermute | solution.py:413
  20.1 28.3 %collective-permute-start.12 = (bf16[2,128,1280]{2,1,0:T(8,128)(2,1)}, bf16[2,128,1280]{2,1,0:T(8,128)(2,1)}, u32[]{:S(2)}, u32[]{:S(2)}) collective-permute-start(bf16[2,128,1280]{2,1,0:T(8,128)(2,1)} %get-tuple-element.34), channel_id=1, source_target_pairs={{0,2},{1,3},{2,0},{3,1},{4,6},{5,7},{6,4},{7,5},{8,10},{9,11},{10,... | collective-permute-start | bytes 1966088 | tf_op jit(solution)/shard_map/ppermute | solution.py:413
  22.2 39.0 %collective-permute-start.9 = (bf16[2,128,768]{2,1,0:T(8,128)(2,1)}, bf16[2,128,768]{2,1,0:T(8,128)(2,1)}, u32[]{:S(2)}, u32[]{:S(2)}) collective-permute-start(bf16[2,128,768]{2,1,0:T(8,128)(2,1)} %get-tuple-element.29), channel_id=1, source_target_pairs={{0,2},{1,3},{2,0},{3,1},{4,6},{5,7},{6,4},{7,5},{8,10},{9,11},{10,... | collective-permute-start | bytes 1179656 | tf_op jit(solution)/shard_map/ppermute | solution.py:413
  22.8 38.4 %collective-permute-start.10 = (bf16[2,128,768]{2,1,0:T(8,128)(2,1)}, bf16[2,128,768]{2,1,0:T(8,128)(2,1)}, u32[]{:S(2)}, u32[]{:S(2)}) collective-permute-start(bf16[2,128,768]{2,1,0:T(8,128)(2,1)} %get-tuple-element.30), channel_id=1, source_target_pairs={{0,4},{1,5},{2,6},{3,7},{4,0},{5,1},{6,2},{7,3},{8,12},{9,13},{10,... | collective-permute-start | bytes 1179656 | tf_op jit(solution)/shard_map/ppermute | solution.py:413
  46.7 17.1 %collective-permute-start.11 = (bf16[2,128,768]{2,1,0:T(8,128)(2,1)}, bf16[2,128,768]{2,1,0:T(8,128)(2,1)}, u32[]{:S(2)}, u32[]{:S(2)}) collective-permute-start(bf16[2,128,768]{2,1,0:T(8,128)(2,1)} %get-tuple-element.32), channel_id=1, source_target_pairs={{0,6},{1,7},{2,4},{3,5},{4,2},{5,3},{6,0},{7,1},{8,14},{9,15},{10,... | collective-permute-start | bytes 1179656 | tf_op jit(solution)/shard_map/ppermute | solution.py:413
  67.6 13.0 %all-to-all-start = ((f32[32,1,128]{2,1,0:T(1,128)}), f32[32,1,128]{2,1,0:T(1,128)}, u32[]{:S(2)}, u32[]{:S(2)}) async-start(f32[32,1,128]{2,1,0:T(1,128)} %bitcast.34), calls=%async_computation | async-start | bytes 32768 | tf_op jit(solution)/shard_map/all_to_all | solution.py:444
